TPU v7x, 32 devices: a whole 2x2x4 slice. The times are simulated.
32 devices in a mesh: seq: 8 (over y, x, core), tp: 4 (over z).
Axes of the slice: x: 2, y: 2, z: 4, core: 2. Of those that a mesh axis runs over, the one named last changes fastest.
Arguments:
- tokens: bfloat16 [32768, 512], P(('seq', 'tp')), may hold values from -6 to 6
- ln_gain: float32 [512], replicated, may hold values from 0.25 to 1.75
- in_proj: bfloat16 [2, 512, 256], P(None, None, 'tp'), may hold values from -0.25 to 0.25
- decay_log: float32 [256], P('tp'), as said below
- angle: float32 [256], P('tp'), may hold values from -3.140625 to 3.140625
- out_proj: bfloat16 [2, 256, 512], P(None, 'tp'), may hold values from -0.375 to 0.375
- skip: bfloat16 [512], replicated, may hold values from -4 to 4
- glu_proj: bfloat16 [2, 512, 1024], P(None, None, 'tp'), may hold values from -0.25 to 0.25
- down_proj: bfloat16 [1024, 512], P('tp'), may hold values from -0.5 to 0.5
- lengths: int32 [6], replicated, may hold values from 1 to 28672, as said below
- cotangent: bfloat16 [32768, 512], P(('seq', 'tp')), may hold values from -6 to 6
Outputs:
- result: bfloat16 [32768, 512], P(('seq', 'tp'))
- grad_tokens: float32 [32768, 512], P(('seq', 'tp'))
- grad_gain: float32 [512], replicated
- grad_in_proj: float32 [2, 512, 256], P(None, None, 'tp')
- grad_decay: float32 [256], P('tp')
- grad_angle: float32 [256], P('tp')
- grad_out_proj: float32 [2, 256, 512], P(None, 'tp')
- grad_skip: float32 [512], replicated
- grad_glu: float32 [2, 512, 1024], P(None, None, 'tp')
- grad_down: float32 [1024, 512], P('tp')
Inputs may be any that keep to these rules, and one draw needn't show every extreme that they name: 6 positive lengths that sum to 32768; the tokens are packed one sequence after another in this order; the second sequence has exactly 28672 tokens, and the first together with all after the second have 4096. exp(decay_log) lies between 0.2 / 32768 and 1 / 25.
All inputs are finite; a program needn't handle non-finite values.
Results may differ from a plain program's by a relative error of at most 0.025.
Values may be sent and summed in bfloat16 or wider, within the bound.
A program may use at most 256 MiB of HBM per device.

v0:
```python
import jax
import jax.numpy as jnp
from jax import lax
from jax.sharding import PartitionSpec as P

epsilon = 1e-05


def prefix(value, axis, join, neutral, backward):
    count, mine = (lax.axis_size(axis), lax.axis_index(axis))
    pieces = jax.tree.map(lambda part: lax.all_gather(part, axis), value)
    if backward:
        pieces = jax.tree.map(lambda part: part[::-1], pieces)
        mine = count - 1 - mine
    total = jax.tree.map(
        lambda part, zero: jnp.full_like(part, 0) + jnp.asarray(zero, part.dtype), value, neutral
    )

    def lap(position, total):
        longer = join(total, jax.tree.map(lambda part: part[position], pieces))
        return jax.tree.map(lambda new, old: jnp.where(position < mine, new, old), longer, total)

    return lax.fori_loop(0, count - 1, lap, total)


def complex_mul(left_re, left_im, right_re, right_im):
    return (left_re * right_re - left_im * right_im, left_re * right_im + left_im * right_re)


def compose(earlier, latter):
    scaled = complex_mul(latter[0], latter[1], earlier[0], earlier[1])
    moved = complex_mul(latter[0], latter[1], earlier[2], earlier[3])
    return (scaled[0], scaled[1], moved[0] + latter[2], moved[1] + latter[3])


def decay_terms(decay_log, angle):
    rate_step = jnp.exp(decay_log)
    radius = jnp.exp(-rate_step)
    return (
        radius * jnp.cos(angle),
        radius * jnp.sin(angle),
        jnp.sqrt(-jnp.expm1(-2.0 * rate_step)),
    )


def flip_rows(items):
    return tuple((jnp.flip(item, 0) for item in items))


def start_mask(lengths, first_row, row_count):
    starts = jnp.cumsum(lengths) - lengths
    positions = first_row + jnp.arange(row_count, dtype=jnp.int32)
    keep_mask = 1.0 - jnp.any(positions[:, None] == starts[None, :], axis=1).astype(jnp.float32)
    return keep_mask[:, None]


def forward_state(normed, w_in, keep_mask, lam_re, lam_im, gamma, pass_state):
    proj_re = jnp.dot(normed, w_in[0], preferred_element_type=jnp.float32)
    proj_im = jnp.dot(normed, w_in[1], preferred_element_type=jnp.float32)
    local_run = lax.associative_scan(
        compose, (lam_re * keep_mask, lam_im * keep_mask, gamma * proj_re, gamma * proj_im), axis=0
    )
    identity = (
        jnp.ones_like(lam_re),
        jnp.zeros_like(lam_re),
        jnp.zeros_like(lam_re),
        jnp.zeros_like(lam_re),
    )
    incoming = pass_state(
        (local_run[0][-1], local_run[1][-1], local_run[2][-1], local_run[3][-1]), identity
    )
    carry_re, carry_im = (incoming[2], incoming[3])
    reached = complex_mul(local_run[0], local_run[1], carry_re, carry_im)
    return (
        proj_re,
        proj_im,
        local_run[2] + reached[0],
        local_run[3] + reached[1],
        carry_re,
        carry_im,
    )


def backward_state(d_state_re, d_state_im, keep_mask, lam_re, lam_im, pass_adjoint):
    keep_next = jnp.concatenate([keep_mask[1:], jnp.ones((1, 1), jnp.float32)], 0)
    back_re = (lam_re * keep_next).at[-1].set(1.0)
    back_im = (-lam_im * keep_next).at[-1].set(0.0)
    back_run = flip_rows(
        lax.associative_scan(compose, flip_rows((back_re, back_im, d_state_re, d_state_im)), axis=0)
    )
    lead_re = lam_re * keep_mask[0]
    lead_im = -lam_im * keep_mask[0]
    lead_scale = complex_mul(lead_re, lead_im, back_run[0][0], back_run[1][0])
    lead_value = complex_mul(lead_re, lead_im, back_run[2][0], back_run[3][0])
    identity = (
        jnp.ones_like(lam_re),
        jnp.zeros_like(lam_re),
        jnp.zeros_like(lam_re),
        jnp.zeros_like(lam_re),
    )
    later_in = pass_adjoint((lead_scale[0], lead_scale[1], lead_value[0], lead_value[1]), identity)
    reached_back = complex_mul(back_run[0], back_run[1], later_in[2], later_in[3])
    return (back_run[2] + reached_back[0], back_run[3] + reached_back[1])


def rate_grads(
    adjoint_re,
    adjoint_im,
    state_re,
    state_im,
    carry_re,
    carry_im,
    proj_re,
    proj_im,
    keep_mask,
    decay_log,
    angle,
):
    prev_re = jnp.concatenate([carry_re[None, :], state_re[:-1]], 0)
    prev_im = jnp.concatenate([carry_im[None, :], state_im[:-1]], 0)
    grad_lam_re = jnp.sum(keep_mask * (adjoint_re * prev_re + adjoint_im * prev_im), 0)
    grad_lam_im = jnp.sum(keep_mask * (adjoint_im * prev_re - adjoint_re * prev_im), 0)
    grad_gamma = jnp.sum(adjoint_re * proj_re + adjoint_im * proj_im, 0)
    _, param_pull = jax.vjp(decay_terms, decay_log, angle)
    return param_pull((grad_lam_re, grad_lam_im, grad_gamma))


def local(
    tokens,
    ln_gain,
    in_proj,
    decay_log,
    angle,
    out_proj,
    skip,
    glu_proj,
    down_proj,
    lengths,
    cotangent,
):
    row_share, model_width = tokens.shape
    tp_count = lax.axis_size("tp")
    tok_rows = row_share * tp_count
    tp_index = lax.axis_index("tp")
    tokens_f = tokens.astype(jnp.float32)
    row_mean = jnp.mean(tokens_f, 1)
    inv_std = lax.rsqrt(jnp.mean(tokens_f * tokens_f, 1) - row_mean * row_mean + epsilon)
    centred = (tokens_f - row_mean[:, None]) * inv_std[:, None]
    normed_part = (centred * ln_gain).astype(jnp.bfloat16)
    normed_part_f = normed_part.astype(jnp.float32)
    skip_f = skip.astype(jnp.float32)
    normed = lax.all_gather(normed_part, "tp", axis=0, tiled=True)
    keep_mask = start_mask(lengths, lax.axis_index("seq") * tok_rows, tok_rows)
    lam_re, lam_im, gamma = decay_terms(decay_log, angle)

    def pass_block_state(items, identity):
        return prefix(items, "seq", compose, identity, False)

    proj_re, proj_im, state_re, state_im, carry_re, carry_im = forward_state(
        normed, in_proj, keep_mask, lam_re, lam_im, gamma, pass_block_state
    )
    state_low_re = state_re.astype(jnp.bfloat16)
    state_low_im = state_im.astype(jnp.bfloat16)
    partial_mix = jnp.dot(state_low_re, out_proj[0], preferred_element_type=jnp.float32) - jnp.dot(
        state_low_im, out_proj[1], preferred_element_type=jnp.float32
    )
    mixed = lax.psum(partial_mix.astype(jnp.bfloat16), "tp").astype(
        jnp.float32
    ) + skip_f * normed.astype(jnp.float32)
    activated, gelu_pull = jax.vjp(jax.nn.gelu, mixed)
    act = activated.astype(jnp.bfloat16)
    value = jnp.dot(act, glu_proj[0], preferred_element_type=jnp.float32)
    gate = jnp.dot(act, glu_proj[1], preferred_element_type=jnp.float32)
    sigma = jax.nn.sigmoid(gate)
    hidden = (value * sigma).astype(jnp.bfloat16)
    down_part = jnp.dot(hidden, down_proj, preferred_element_type=jnp.float32)
    result = (
        tokens_f
        + lax.psum_scatter(
            down_part.astype(jnp.bfloat16), "tp", scatter_dimension=0, tiled=True
        ).astype(jnp.float32)
    ).astype(jnp.bfloat16)
    cot_full = lax.all_gather(cotangent, "tp", axis=0, tiled=True)
    d_hidden = jnp.dot(cot_full, down_proj.T, preferred_element_type=jnp.float32)
    grad_down = jnp.dot(hidden.T, cot_full, preferred_element_type=jnp.float32)
    d_value = (d_hidden * sigma).astype(jnp.bfloat16)
    d_gate = (d_hidden * value * sigma * (1.0 - sigma)).astype(jnp.bfloat16)
    grad_glu = jnp.stack(
        [
            jnp.dot(act.T, d_value, preferred_element_type=jnp.float32),
            jnp.dot(act.T, d_gate, preferred_element_type=jnp.float32),
        ]
    )
    d_act_part = jnp.dot(d_value, glu_proj[0].T, preferred_element_type=jnp.float32) + jnp.dot(
        d_gate, glu_proj[1].T, preferred_element_type=jnp.float32
    )
    d_mixed = gelu_pull(lax.psum(d_act_part.astype(jnp.bfloat16), "tp").astype(jnp.float32))[
        0
    ].astype(jnp.bfloat16)
    d_mixed_part = lax.dynamic_slice_in_dim(d_mixed, tp_index * row_share, row_share, 0)
    d_mixed_part_f = d_mixed_part.astype(jnp.float32)
    grad_skip = jnp.sum(d_mixed_part_f * normed_part_f, 0)
    grad_out = jnp.stack(
        [
            jnp.dot(state_low_re.T, d_mixed, preferred_element_type=jnp.float32),
            -jnp.dot(state_low_im.T, d_mixed, preferred_element_type=jnp.float32),
        ]
    )
    d_state_re = jnp.dot(d_mixed, out_proj[0].T, preferred_element_type=jnp.float32)
    d_state_im = -jnp.dot(d_mixed, out_proj[1].T, preferred_element_type=jnp.float32)

    def pass_block_adjoint(items, identity):
        return prefix(items, "seq", compose, identity, True)

    adjoint_re, adjoint_im = backward_state(
        d_state_re, d_state_im, keep_mask, lam_re, lam_im, pass_block_adjoint
    )
    grad_decay, grad_angle = rate_grads(
        adjoint_re,
        adjoint_im,
        state_re,
        state_im,
        carry_re,
        carry_im,
        proj_re,
        proj_im,
        keep_mask,
        decay_log,
        angle,
    )
    d_proj_re = (gamma * adjoint_re).astype(jnp.bfloat16)
    d_proj_im = (gamma * adjoint_im).astype(jnp.bfloat16)
    grad_in = jnp.stack(
        [
            jnp.dot(normed.T, d_proj_re, preferred_element_type=jnp.float32),
            jnp.dot(normed.T, d_proj_im, preferred_element_type=jnp.float32),
        ]
    )
    d_normed_part = jnp.dot(d_proj_re, in_proj[0].T, preferred_element_type=jnp.float32) + jnp.dot(
        d_proj_im, in_proj[1].T, preferred_element_type=jnp.float32
    )
    d_normed = (
        lax.psum_scatter(
            d_normed_part.astype(jnp.bfloat16), "tp", scatter_dimension=0, tiled=True
        ).astype(jnp.float32)
        + d_mixed_part_f * skip_f
    )
    grad_gain = jnp.sum(d_normed * centred, 0)
    d_cent = d_normed * ln_gain
    cent_mean = jnp.mean(d_cent, 1)
    cross_mean = jnp.mean(d_cent * centred, 1)
    grad_tokens = cotangent.astype(jnp.float32) + inv_std[:, None] * (
        d_cent - cent_mean[:, None] - centred * cross_mean[:, None]
    )
    norm_sums = lax.psum((grad_gain, grad_skip), ("seq", "tp"))
    summed = (
        lax.psum(grad_in.astype(jnp.bfloat16), "seq").astype(jnp.float32),
        lax.psum(grad_decay.astype(jnp.bfloat16), "seq").astype(jnp.float32),
        lax.psum(grad_angle.astype(jnp.bfloat16), "seq").astype(jnp.float32),
        lax.psum(grad_out.astype(jnp.bfloat16), "seq").astype(jnp.float32),
        lax.psum(grad_glu.astype(jnp.bfloat16), "seq").astype(jnp.float32),
        lax.psum(grad_down.astype(jnp.bfloat16), "seq").astype(jnp.float32),
    )
    return (
        result,
        grad_tokens,
        norm_sums[0],
        summed[0],
        summed[1],
        summed[2],
        summed[3],
        norm_sums[1],
        summed[4],
        summed[5],
    )


def solution(mesh):
    in_specs = (
        P(("seq", "tp"), None),
        P(),
        P(None, None, "tp"),
        P("tp"),
        P("tp"),
        P(None, "tp", None),
        P(),
        P(None, None, "tp"),
        P("tp", None),
        P(),
        P(("seq", "tp"), None),
    )
    out_specs = (
        P(("seq", "tp"), None),
        P(("seq", "tp"), None),
        P(),
        P(None, None, "tp"),
        P("tp"),
        P("tp"),
        P(None, "tp", None),
        P(),
        P(None, None, "tp"),
        P("tp", None),
    )
    return jax.shard_map(local, mesh=mesh, in_specs=in_specs, out_specs=out_specs, check_vma=False)
```

profile of v0, /device:TPU:1, one launch (start us, length us, event | category | flops | bytes accessed | tf_op | source)
XLA Modules:
  0.0 3004.6 jit_solution(7797579240788774455)
XLA Ops:
  15.9 18.1 slice.1542
  34.1 18.2 slice.1549
  52.2 18.1 slice.1544
  70.4 18.3 slice.1550
  88.8 18.1 slice.1541
  106.9 18.1 slice.1716
  133.1 18.6 slice.1543
  151.6 18.1 slice.1547
  169.7 18.1 slice.1546
  187.9 18.3 slice.1555
  614.8 18.1 slice.1720
  632.9 18.5 slice.1771
  795.1 21.7 pad.685
  816.8 21.9 pad.684
  838.7 20.2 pad.635
  858.9 19.9 pad.634
  956.3 17.4 pad.682
  973.7 19.6 pad.683
  995.7 21.9 pad.680
  1017.7 21.8 pad.681
  1094.7 148.0 %all-reduce.206.cloned.1.call-done = bf16[4096,512]{1,0:T(8,128)(2,1)} async-done(((bf16[4096,512]{1,0:T(8,128)(2,1)}), bf16[4096,512]{1,0:T(8,128)(2,1)}) %all-reduce.206.cloned.1.call-update) | async-done | bytes 4194320 | tf_op jit(solution)/shard_map/psum | solution.py:167
  1263.7 19.0 slice.1783
  1282.7 19.0 slice.1795
  1304.0 19.0 slice.1788
  1323.0 19.0 slice.1797
  1342.0 19.0 slice.1965
  1361.0 19.2 slice.1781
  1464.7 19.4 slice.1785
  1484.1 19.0 slice.1792
  1503.1 19.0 slice.1790
  1522.1 19.2 slice.1803
  2001.2 19.0 slice.2021
  2020.2 19.0 slice.1970
  2490.1 21.9 pad.730
  2512.0 21.7 pad.731
  2539.4 21.7 pad.777
  2561.1 22.1 pad.776
  2588.9 21.8 pad.779
  2612.8 22.1 pad.778
  2638.5 21.8 pad.781
  2662.3 21.9 pad.780
  2687.8 16.2 rev.29
  2704.0 16.3 rev.30
  2733.9 16.2 rev.35
  2806.5 27.3 all-reduce.210.cloned.1.call-done
  2841.0 71.9 %reduce-scatter.5.cloned.1.call-done = bf16[1024,512]{1,0:T(8,128)(2,1)} async-done(((bf16[4096,512]{1,0:T(8,128)(2,1)}), bf16[1024,512]{1,0:T(8,128)(2,1)}) %reduce-scatter.5.cloned.1.call-update) | async-done | bytes 1048592 | tf_op jit(solution)/shard_map/reduce_scatter | solution.py:243
  2915.9 45.8 %all-reduce.198 = (f32[512]{0:T(512)}, f32[512]{0:T(512)}) all-reduce(f32[512]{0:T(512)S(1)} %get-tuple-element.372, f32[512]{0:T(512)S(1)} %get-tuple-element.377), channel_id=1, replica_groups=mesh['seq'=8,'tp'=4] {'seq','tp'}, use_global_device_ids=true, to_apply=%region_15.16 | all-reduce | flops 1024 | bytes 8192 | tf_op jit(solution)/shard_map/psum | solution.py:255
  2961.7 32.0 %reduce-scatter.3.cloned.1.call-done = bf16[1024,512]{1,0:T(8,128)(2,1)} async-done(((bf16[4096,512]{1,0:T(8,128)(2,1)}), bf16[1024,512]{1,0:T(8,128)(2,1)}) %reduce-scatter.3.cloned.1.call-update) | async-done | bytes 1048592 | tf_op jit(solution)/shard_map/reduce_scatter | solution.py:179
  (1115 shorter events, 1826.2 us)
Async XLA Ops:
  7.2 1081.9 %copy-start = (bf16[256,512]{1,0:T(8,128)(2,1)S(1)}, bf16[256,512]{1,0:T(8,128)(2,1)}, u32[]{:S(2)}) copy-start(bf16[256,512]{1,0:T(8,128)(2,1)} %param.27) | copy-start | bytes 786436
  7.2 119.0 %all-gather.11.cloned.1.call-start = ((), (), s32[]{:S(2)}) async-start(), calls=%async_computation.2 | async-start | bytes 5242880 | tf_op jit(solution)/shard_map/all_gather | solution.py:152
  12.2 1076.9 %all-gather.13.cloned.1.call-start = ((), (), s32[]{:S(2)}) async-start(), calls=%async_computation.5 | async-start | bytes 5242880 | tf_op jit(solution)/shard_map/all_gather | solution.py:183
  12.9 1229.8 %all-reduce.206.cloned.1.call-start = ((), (), s32[]{:S(2)}) async-start(), calls=%async_computation.3 | async-start | bytes 8388608 | tf_op jit(solution)/shard_map/psum | solution.py:167
  13.0 75.7 %copy-start.144 = (f32[64]{0:T(128)}, f32[64]{0:T(128)S(1)}, u32[]{:S(2)}) copy-start(f32[64]{0:T(128)S(1)} %get-tuple-element.696) | copy-start | bytes 772
  13.0 75.7 %copy-start.146 = (f32[64]{0:T(128)}, f32[64]{0:T(128)S(1)}, u32[]{:S(2)}) copy-start(f32[64]{0:T(128)S(1)} %get-tuple-element.697) | copy-start | bytes 772
  14.1 74.7 %copy-start.135 = (f32[64]{0:T(128)}, f32[64]{0:T(128)S(1)}, u32[]{:S(2)}) copy-start(f32[64]{0:T(128)S(1)} %get-tuple-element.434) | copy-start | bytes 772
  14.1 74.7 %copy-start.137 = (f32[64]{0:T(128)}, f32[64]{0:T(128)S(1)}, u32[]{:S(2)}) copy-start(f32[64]{0:T(128)S(1)} %get-tuple-element.695) | copy-start | bytes 772
  15.9 110.3 %copy-start.73 = (bf16[2,512,64]{1,2,0:T(8,128)(2,1)S(1)}, bf16[2,512,64]{1,2,0:T(8,128)(2,1)}, u32[]{:S(2)}) copy-start(bf16[2,512,64]{1,2,0:T(8,128)(2,1)} %param.21) | copy-start | bytes 393220
  345.7 123.0 %copy-start.44 = (f32[512,64]{0,1:T(8,128)}, f32[512,64]{0,1:T(8,128)S(1)}, u32[]{:S(2)}) copy-start(f32[512,64]{0,1:T(8,128)S(1)} %get-tuple-element.495) | copy-start | bytes 393220
  632.9 40.7 %copy-start.58 = (f32[32,64]{0,1:T(8,128)S(1)}, f32[32,64]{0,1:T(8,128)}, u32[]{:S(2)}) copy-start(f32[32,64]{0,1:T(8,128)} %get-tuple-element.628) | copy-start | bytes 24580
  790.3 68.5 %copy-start.36 = (f32[2048,64]{0,1:T(8,128)S(1)}, f32[2048,64]{0,1:T(8,128)}, u32[]{:S(2)}) copy-start(f32[2048,64]{0,1:T(8,128)} %pad_maximum_fusion.2) | copy-start | bytes 1572868
  790.4 88.4 %copy-start.90 = (f32[256,64]{0,1:T(8,128)S(1)}, f32[256,64]{0,1:T(8,128)}, u32[]{:S(2)}) copy-start(f32[256,64]{0,1:T(8,128)} %pad_maximum_fusion.30) | copy-start | bytes 196612
  790.4 95.2 %copy-start.89 = (f32[256,64]{0,1:T(8,128)S(1)}, f32[256,64]{0,1:T(8,128)}, u32[]{:S(2)}) copy-start(f32[256,64]{0,1:T(8,128)} %pad_maximum_fusion.29) | copy-start | bytes 196612
  791.4 96.5 %copy-start.40 = (f32[511,64]{0,1:T(8,128)S(1)}, f32[511,64]{0,1:T(8,128)}, u32[]{:S(2)}) copy-start(f32[511,64]{0,1:T(8,128)} %slice.1704) | copy-start | bytes 392452
  858.9 48.6 %copy-start.27 = (f32[1023,64]{0,1:T(8,128)S(1)}, f32[1023,64]{0,1:T(8,128)}, u32[]{:S(2)}) copy-start(f32[1023,64]{0,1:T(8,128)} %slice.1551) | copy-start | bytes 785668
  858.9 48.6 %copy-start.29 = (f32[1023,64]{0,1:T(8,128)S(1)}, f32[1023,64]{0,1:T(8,128)}, u32[]{:S(2)}) copy-start(f32[1023,64]{0,1:T(8,128)} %slice.1710) | copy-start | bytes 785668
  888.0 50.0 %copy-start.116 = (f32[1,64]{0,1:T(8,128)S(1)}, f32[1,64]{0,1:T(8,128)}, u32[]{:S(2)}) copy-start(f32[1,64]{0,1:T(8,128)} %slice.2102) | copy-start | bytes 772
  908.2 45.6 %copy-start.20 = (f32[2047,64]{0,1:T(8,128)S(1)}, f32[2047,64]{0,1:T(8,128)}, u32[]{:S(2)}) copy-start(f32[2047,64]{0,1:T(8,128)} %slice.1541) | copy-start | bytes 1572100
  908.2 45.6 %copy-start.21 = (f32[2047,64]{0,1:T(8,128)S(1)}, f32[2047,64]{0,1:T(8,128)}, u32[]{:S(2)}) copy-start(f32[2047,64]{0,1:T(8,128)} %slice.1716) | copy-start | bytes 1572100
  956.1 122.0 %copy-start.126 = (f32[64]{0:T(128)S(1)}, f32[64]{0:T(128)}, u32[]{:S(2)}) copy-start(f32[64]{0:T(128)} %custom-call) | copy-start | bytes 772
  956.1 122.0 %copy-start.128 = (f32[64]{0:T(128)S(1)}, f32[64]{0:T(128)}, u32[]{:S(2)}) copy-start(f32[64]{0:T(128)} %custom-call.1) | copy-start | bytes 772
  973.6 104.7 %copy-start.22 = (f32[4096,64]{0,1:T(8,128)}, f32[4096,64]{0,1:T(8,128)S(1)}, u32[]{:S(2)}) copy-start(f32[4096,64]{0,1:T(8,128)S(1)} %pad.682) | copy-start | bytes 3145732
  993.3 85.1 %copy-start.23 = (f32[4096,64]{0,1:T(8,128)}, f32[4096,64]{0,1:T(8,128)S(1)}, u32[]{:S(2)}) copy-start(f32[4096,64]{0,1:T(8,128)S(1)} %pad.683) | copy-start | bytes 3145732
  1087.8 359.4 %all-reduce.208.cloned.1.call-start = ((), (), s32[]{:S(2)}) async-start(), calls=%async_computation.6 | async-start | bytes 8388608 | tf_op jit(solution)/shard_map/psum | solution.py:197
  1261.1 1572.7 %all-reduce.210.cloned.1.call-start = ((), (), s32[]{:S(2)}) async-start(), calls=%async_computation.8 | async-start | bytes 2097152 | tf_op jit(solution)/shard_map/psum | solution.py:257
  1715.6 123.1 %copy-start.45 = (f32[512,64]{0,1:T(8,128)}, f32[512,64]{0,1:T(8,128)S(1)}, u32[]{:S(2)}) copy-start(f32[512,64]{0,1:T(8,128)S(1)} %get-tuple-element.513) | copy-start | bytes 393220
  1927.1 132.6 %copy-start.94 = (f32[1,64]{0,1:T(8,128)S(1)}, f32[1,64]{0,1:T(8,128)}, u32[]{:S(2)}) copy-start(f32[1,64]{0,1:T(8,128)} %get-tuple-element.677) | copy-start | bytes 772
  1927.1 132.6 %copy-start.118 = (f32[1,64]{0,1:T(8,128)S(1)}, f32[1,64]{0,1:T(8,128)}, u32[]{:S(2)}) copy-start(f32[1,64]{0,1:T(8,128)} %get-tuple-element.533) | copy-start | bytes 772
  1927.1 135.7 %copy-start.93 = (f32[1,64]{0,1:T(8,128)S(1)}, f32[1,64]{0,1:T(8,128)}, u32[]{:S(2)}) copy-start(f32[1,64]{0,1:T(8,128)} %get-tuple-element.678) | copy-start | bytes 772
  2065.6 128.2 %copy-start.41 = (f32[511,64]{0,1:T(8,128)S(1)}, f32[511,64]{0,1:T(8,128)}, u32[]{:S(2)}) copy-start(f32[511,64]{0,1:T(8,128)} %slice.1810) | copy-start | bytes 392452
  2228.1 110.8 %copy-start.49 = (f32[64,64]{0,1:T(8,128)S(1)}, f32[64,64]{0,1:T(8,128)}, u32[]{:S(2)}) copy-start(f32[64,64]{0,1:T(8,128)} %get-tuple-element.599) | copy-start | bytes 49156
  2228.1 117.2 %copy-start.48 = (f32[64,64]{0,1:T(8,128)S(1)}, f32[64,64]{0,1:T(8,128)}, u32[]{:S(2)}) copy-start(f32[64,64]{0,1:T(8,128)} %get-tuple-element.600) | copy-start | bytes 49156
  2229.7 122.4 %copy-start.47 = (f32[128,64]{0,1:T(8,128)S(1)}, f32[128,64]{0,1:T(8,128)}, u32[]{:S(2)}) copy-start(f32[128,64]{0,1:T(8,128)} %get-tuple-element.656) | copy-start | bytes 98308
  2240.9 113.3 %copy-start.46 = (f32[128,64]{0,1:T(8,128)S(1)}, f32[128,64]{0,1:T(8,128)}, u32[]{:S(2)}) copy-start(f32[128,64]{0,1:T(8,128)} %get-tuple-element.655) | copy-start | bytes 98308
  2588.9 71.3 %copy-start.97 = (f32[1,64]{0,1:T(8,128)S(1)}, f32[1,64]{0,1:T(8,128)}, u32[]{:S(2)}) copy-start(f32[1,64]{0,1:T(8,128)} %slice.2327) | copy-start | bytes 772
  2662.3 58.0 %copy-start.136 = (f32[64]{0:T(128)S(1)}, f32[64]{0:T(128)}, u32[]{:S(2)}) copy-start(f32[64]{0:T(128)} %copy-done.135) | copy-start | bytes 772
  2662.3 58.0 %copy-start.138 = (f32[64]{0:T(128)S(1)}, f32[64]{0:T(128)}, u32[]{:S(2)}) copy-start(f32[64]{0:T(128)} %copy-done.137) | copy-start | bytes 772
  2662.3 71.3 %copy-start.130 = (f32[64]{0:T(128)S(1)}, f32[64]{0:T(128)}, u32[]{:S(2)}) copy-start(f32[64]{0:T(128)} %custom-call.2) | copy-start | bytes 772
  2662.3 71.3 %copy-start.132 = (f32[64]{0:T(128)S(1)}, f32[64]{0:T(128)}, u32[]{:S(2)}) copy-start(f32[64]{0:T(128)} %custom-call.3) | copy-start | bytes 772
  2778.5 134.3 %reduce-scatter.5.cloned.1.call-start = ((), (), s32[]{:S(2)}) async-start(), calls=%async_computation.7 | async-start | bytes 5242880 | tf_op jit(solution)/shard_map/reduce_scatter | solution.py:243
  2785.8 207.8 %reduce-scatter.3.cloned.1.call-start = ((), (), s32[]{:S(2)}) async-start(), calls=%async_computation.4 | async-start | bytes 5242880 | tf_op jit(solution)/shard_map/reduce_scatter | solution.py:179
  2790.8 122.1 %copy-start.6 = (bf16[1024,512]{1,0:T(8,128)(2,1)S(1)}, bf16[1024,512]{1,0:T(8,128)(2,1)}, u32[]{:S(2)}) copy-start(bf16[1024,512]{1,0:T(8,128)(2,1)} %param.19) | copy-start | bytes 3145732
  2790.8 122.1 %copy-start.120 = (f32[1024]{0:T(1024)S(1)}, f32[1024]{0:T(1024)}, u32[]{:S(2)}) copy-start(f32[1024]{0:T(1024)} %copy-done.119) | copy-start | bytes 12292
  2790.8 122.1 %copy-start.122 = (f32[1024]{0:T(1024)S(1)}, f32[1024]{0:T(1024)}, u32[]{:S(2)}) copy-start(f32[1024]{0:T(1024)} %copy-done.121) | copy-start | bytes 12292
  2790.8 122.1 %copy-start.123 = (f32[512]{0:T(512)S(1)}, f32[512]{0:T(512)}, u32[]{:S(2)}) copy-start(f32[512]{0:T(512)} %convert_element_type.119) | copy-start | bytes 6148
  2790.8 122.1 %copy-start.134 = (f32[512]{0:T(512)S(1)}, f32[512]{0:T(512)}, u32[]{:S(2)}) copy-start(f32[512]{0:T(512)} %param.20) | copy-start | bytes 6148
  2790.9 202.8 %copy-start.24 = (bf16[1024,512]{1,0:T(8,128)(2,1)S(1)}, bf16[1024,512]{1,0:T(8,128)(2,1)}, u32[]{:S(2)}) copy-start(bf16[1024,512]{1,0:T(8,128)(2,1)} %param.29) | copy-start | bytes 3145732
  (109 other events, 1345.6 us)
Sparse Core Ops, SparseCore 0:
  12.3 82.8 all-gather.10
  96.7 79.2 all-gather.12
  1087.9 154.7 all-reduce.205
  1261.3 153.9 all-reduce.207
  2778.7 55.0 all-reduce.209
  2835.9 76.8 reduce-scatter.4
  2915.3 78.3 reduce-scatter.2
where the time goes:
time: 3060 us; the launch traced here: 3000 us
  local copies, waits for them, and re-layouts  2230 us (73%)
  other arithmetic  310 us (10%)
  waiting for transfers between devices  280 us (9%)
  blocking collectives  107 us (3%)
  matrix products  59.1 us (2%)
    slice x156, local copies, waits for them, and re-layouts, backward_state(): lax.associative_scan(compose, flip_rows((back_re, back_im, d_state_re, d_...  699 us
    slice x148, local copies, waits for them, and re-layouts, forward_state(): lax.associative_scan(compose, (lam_re * keep_mask, lam_im * keep_mask, ga...  616 us
    pad x88, local copies, waits for them, and re-layouts, backward_state(): lax.associative_scan(compose, flip_rows((back_re, back_im, d_state_re, d_...  464 us
    pad x88, local copies, waits for them, and re-layouts, forward_state(): lax.associative_scan(compose, (lam_re * keep_mask, lam_im * keep_mask, ga...  328 us
    psum x1, waiting for transfers between devices, local(): lax.psum(partial_mix.astype(jnp.bfloat16), 'tp').astype(jnp.float32)  148 us
    add x48, other arithmetic, backward_state(): lax.associative_scan(compose, flip_rows((back_re, back_im, d_state_re, d_...  73.2 us
    reduce_scatter x1, waiting for transfers between devices, local(): lax.psum_scatter(d_normed_part.astype(jnp.bfloat16), 'tp', scatter_dimens...  71.9 us
    rev x4, local copies, waits for them, and re-layouts, flip_rows(): return tuple((jnp.flip(item, 0) for item in items))  64.9 us
  transfers between devices with their start and end apart: 7, of which 4 were waited for; matrix products, arithmetic and copies ran while one was open for 42% of the time, Pallas kernels for 0%

commit v1 on v0

v1 whole, which is shorter than its diff:
```python
import functools
import jax
import jax.numpy as jnp
from jax import lax
from jax.experimental import pallas as pl
from jax.experimental.pallas import tpu as pltpu
from jax.sharding import PartitionSpec as P

epsilon = 1e-05
MESH = pl.DeviceIdType.MESH
F32 = jnp.float32
BF16 = jnp.bfloat16
GROUPS = 2


def dot(left, right):
    return jnp.dot(left, right, preferred_element_type=F32)


def dot_nt(left, right):
    return lax.dot_general(left, right, (((1,), (1,)), ((), ())), preferred_element_type=F32)


def complex_mul(left_re, left_im, right_re, right_im):
    return (left_re * right_re - left_im * right_im, left_re * right_im + left_im * right_re)


def load(ref, rows):
    return jnp.concatenate([ref[tile, rows, :] for tile in range(ref.shape[0])], 1)


def save(ref, rows, value):
    for tile in range(ref.shape[0]):
        ref[tile, rows, :] = value[:, tile * 128 : tile * 128 + 128]


def power(base, exponent):
    result = None
    square = base
    while exponent:
        if exponent & 1:
            result = square if result is None else complex_mul(*result, *square)
        exponent >>= 1
        if exponent:
            square = complex_mul(*square, *square)
    return result


def layer_kernel(
    S,
    T,
    lengths,
    tokens,
    cot,
    gain,
    skip,
    rates,
    w_in,
    w_out,
    glu,
    down,
    result,
    grad_tokens,
    small,
    grad_in,
    grad_out,
    grad_glu,
    grad_down,
    centred,
    inv_std,
    normed,
    normed_t,
    cot_t,
    proj,
    keep,
    keep_next,
    state,
    state_t,
    act,
    act_t,
    d_gelu,
    d_act,
    summed,
    d_mixed,
    adjoint,
    d_proj,
    hidden,
    d_value,
    d_gate,
    seg_carry,
    sums,
    state_tp,
    state_seq,
    adj_tp,
    adj_seq,
    send_sem,
    recv_sem,
):
    R, D = tokens.shape
    N = w_in.shape[1] // 2
    segments = 8 * GROUPS
    L = R // segments
    s = lax.axis_index("seq")
    t = lax.axis_index("tp")
    first = (s * T + t) * R

    peers_tp = [lax.rem(t + k, T) for k in range(1, T)]
    peers_seq = [lax.rem(s + k, S) for k in range(1, S)]
    barrier = pltpu.get_barrier_semaphore()
    for peer in peers_tp:
        pl.semaphore_signal(barrier, inc=1, device_id=(s, peer), device_id_type=MESH)
    for peer in peers_seq:
        pl.semaphore_signal(barrier, inc=1, device_id=(peer, t), device_id_type=MESH)

    starts = []
    total = jnp.int32(0)
    for index in range(lengths.shape[0]):
        starts.append(total)
        total = total + lengths[index]

    def keeps(position):
        hit = position == starts[0]
        for start in starts[1:]:
            hit = hit | (position == start)
        return jnp.where(hit, 0.0, 1.0)

    def clear(low, high):
        hit = (starts[0] >= low) & (starts[0] < high)
        for start in starts[1:]:
            hit = hit | ((start >= low) & (start < high))
        return jnp.where(hit, 0.0, 1.0)

    lam_re = rates[0:1, :N]
    lam_im = rates[0:1, N:]
    gamma = rates[1:2, :N]
    gamma_signed = jnp.concatenate([gamma, -gamma], 1)
    gain_row = gain[...]
    skip_row = skip[...].astype(F32)

    NORM_ROWS = 128

    @pl.loop(0, R // NORM_ROWS)
    def _(tile):
        at = pl.multiple_of(tile * NORM_ROWS, NORM_ROWS)
        rows = pl.ds(at, NORM_ROWS)
        x = tokens[rows, :].astype(F32)
        mean = jnp.mean(x, 1, keepdims=True)
        inv = lax.rsqrt(jnp.mean(x * x, 1, keepdims=True) - mean * mean + epsilon)
        c = (x - mean) * inv
        centred[rows, :] = c
        inv_std[rows, :] = jnp.broadcast_to(inv, (NORM_ROWS, 128))
        n = (c * gain_row).astype(BF16)
        normed[rows, :] = n
        normed_t[:, rows] = n.T
        cot_t[:, rows] = cot[rows, :].T
        position = first + at + lax.broadcasted_iota(jnp.int32, (NORM_ROWS, 128), 0)
        keep[rows, :] = keeps(position)
        keep_next[rows, :] = keeps(position + 1)
        save(proj, rows, dot(n, w_in[...]) * gamma_signed)

    low8_re = jnp.broadcast_to(lam_re, (8, N))
    low8_im = jnp.broadcast_to(lam_im, (8, N))

    def rows_of(group, step):
        return pl.ds(group * 8 * L + step, 8, stride=L)

    def spread(row):
        return jnp.concatenate([row] * (N // 128), 1)

    def scan_step(values, mask, add, sign):
        new_re, new_im = complex_mul(low8_re, sign * low8_im, *(value * mask for value in values))
        return (new_re + add[:, :N], new_im + add[:, N:])

    zero8 = jnp.zeros((8, N), F32)
    none = tuple((zero8, zero8) for _ in range(GROUPS))

    def forward_step(step, carry):
        return tuple(
            scan_step(
                carry[group],
                spread(keep[rows_of(group, step), :]),
                load(proj, rows_of(group, step)),
                -1.0,
            )
            for group in range(GROUPS)
        )

    def segment_rows(finals):
        return [
            (finals[group][0][lane : lane + 1], finals[group][1][lane : lane + 1])
            for group in range(GROUPS)
            for lane in range(8)
        ]

    def fold(start, factor, items, masks, taken):
        before = []
        carry = start
        for (item_re, item_im), mask, take in zip(items, masks, taken):
            before.append(carry)
            moved = complex_mul(*factor, *carry)
            longer = (moved[0] * mask + item_re, moved[1] * mask + item_im)
            if take is None:
                carry = longer
            else:
                carry = tuple(jnp.where(take, new, old) for new, old in zip(longer, carry))
        return carry, before

    zero1 = (jnp.zeros((1, N), F32), jnp.zeros((1, N), F32))
    lam = (lam_re, lam_im)
    conj = (lam_re, -lam_im)

    def unpack(row):
        return (row[:, :N], row[:, N:])

    def exchange(own, factor, tp_buf, seq_buf, base, forward):
        shift = 0 if forward else 1
        factor_tp = power(factor, R)
        factor_seq = power(factor_tp, T)
        order = (lambda items: items) if forward else (lambda items: items[::-1])
        tp_buf[t] = jnp.broadcast_to(jnp.concatenate(own, 1), tp_buf.shape[1:])
        copies = [
            pltpu.make_async_remote_copy(
                src_ref=tp_buf.at[t],
                dst_ref=tp_buf.at[t],
                send_sem=send_sem.at[base + k],
                recv_sem=recv_sem.at[base + k],
                device_id=(s, peer),
                device_id_type=MESH,
            )
            for k, peer in enumerate(peers_tp)
        ]
        for copy in copies:
            copy.start()
        for copy in copies:
            copy.wait()
        items = order([unpack(tp_buf[z, 0:1, :]) for z in range(T)])

        def masks_tp(row):
            return order(
                [clear(row + z * R + shift, row + (z + 1) * R + shift) for z in range(T)]
            )

        masks = masks_tp(s * T * R)
        block, _ = fold(zero1, factor_tp, items, masks, [None] * T)
        seq_buf[s] = jnp.broadcast_to(jnp.concatenate(block, 1), seq_buf.shape[1:])
        copies = [
            pltpu.make_async_remote_copy(
                src_ref=seq_buf.at[s],
                dst_ref=seq_buf.at[s],
                send_sem=send_sem.at[base + T - 1 + k],
                recv_sem=recv_sem.at[base + T - 1 + k],
                device_id=(peer, t),
                device_id_type=MESH,
            )
            for k, peer in enumerate(peers_seq)
        ]
        for copy in copies:
            copy.start()
        return copies, items, masks, factor_tp, factor_seq

    def arrived(pending, seq_buf, forward):
        copies, items, masks, factor_tp, factor_seq = pending
        shift = 0 if forward else 1
        for copy in copies:
            copy.wait()
        order = (lambda items: items) if forward else (lambda items: items[::-1])

        def before(other, mine):
            return other < mine if forward else other > mine

        blocks = order(list(range(S)))
        carry, _ = fold(
            zero1,
            factor_seq,
            [unpack(seq_buf[block, 0:1, :]) for block in blocks],
            [clear(block * T * R + shift, (block + 1) * T * R + shift) for block in blocks],
            [before(block, s) for block in blocks],
        )
        carry, _ = fold(carry, factor_tp, items, masks, [before(z, t) for z in order(list(range(T)))])
        return carry

    finals = segment_rows(lax.fori_loop(0, L, forward_step, none))
    seg_masks = [clear(first + index * L, first + (index + 1) * L) for index in range(segments)]
    factor_seg = power(conj, L)
    own, _ = fold(zero1, factor_seg, finals, seg_masks, [None] * segments)
    pl.semaphore_wait(barrier, T - 1 + S - 1)
    pending = exchange(own, conj, state_tp, state_seq, 0, True)
    carry = arrived(pending, state_seq, True)
    _, entering = fold(carry, factor_seg, finals, seg_masks, [None] * segments)
    for index, (row_re, row_im) in enumerate(entering):
        seg_carry[index : index + 1, :] = jnp.concatenate([row_re, row_im], 1)

    def write_state(step, carry):
        new = forward_step(step, carry)
        for group in range(GROUPS):
            save(state, rows_of(group, step), jnp.concatenate(new[group], 1))
        return new

    def entering_groups():
        return tuple(
            unpack(seg_carry[group * 8 : group * 8 + 8, :]) for group in range(GROUPS)
        )

    lax.fori_loop(0, L, write_state, entering_groups())

    MIX_ROWS = 128

    @pl.loop(0, R // MIX_ROWS)
    def _(tile):
        rows = pl.ds(pl.multiple_of(tile * MIX_ROWS, MIX_ROWS), MIX_ROWS)
        low = load(state, rows).astype(BF16)
        state_t[:, rows] = low.T
        x = dot(low, w_out[...]) + skip_row * normed[rows, :].astype(F32)
        scale = 0.7978845608028654
        th = jnp.tanh(scale * (x + 0.044715 * x * x * x))
        half = 0.5 * (1.0 + th)
        a = (x * half).astype(BF16)
        act[rows, :] = a
        act_t[:, rows] = a.T
        d_gelu[rows, :] = half + 0.5 * x * (1.0 - th * th) * scale * (1.0 + 0.134145 * x * x)

    UNIT_ROWS = 256
    for offset in range(T):
        c = lax.rem(t + offset, T)

        @pl.loop(0, R // UNIT_ROWS)
        def _(tile):
            rows = pl.ds(pl.multiple_of(tile * UNIT_ROWS, UNIT_ROWS), UNIT_ROWS)
            a = act[rows, :]
            value = dot(a, glu[c, 0])
            gate = dot(a, glu[c, 1])
            sigma = 0.5 * jnp.tanh(0.5 * gate) + 0.5
            gated = value * sigma
            h = gated.astype(BF16)
            hidden[rows, :] = h
            d_h = dot_nt(cot[rows, :], down[c])
            d_v = (d_h * sigma).astype(BF16)
            d_g = (d_h * gated * (1.0 - sigma)).astype(BF16)
            d_value[rows, :] = d_v
            d_gate[rows, :] = d_g
            added = dot(h, down[c])
            d_a = dot_nt(d_v, glu[c, 0]) + dot_nt(d_g, glu[c, 1])
            if offset > 0:
                added = added + summed[rows, :]
                d_a = d_a + d_act[rows, :]
            if offset < T - 1:
                summed[rows, :] = added
                d_act[rows, :] = d_a
            else:
                result[rows, :] = (tokens[rows, :].astype(F32) + added).astype(BF16)
                d_m = (d_gelu[rows, :] * d_a).astype(BF16)
                d_mixed[rows, :] = d_m
                save(adjoint, rows, dot_nt(d_m, w_out[...]))

        @pl.loop(0, D // 128)
        def _(tile):
            rows = pl.ds(pl.multiple_of(tile * 128, 128), 128)
            grad_down[c, rows, :] = dot(cot_t[rows, :], hidden[...]).astype(BF16)
            grad_glu[c, 0, rows, :] = dot(act_t[rows, :], d_value[...]).astype(BF16)
            grad_glu[c, 1, rows, :] = dot(act_t[rows, :], d_gate[...]).astype(BF16)

    def backward_step(index, carry):
        step = L - 1 - index
        return tuple(
            scan_step(
                carry[group],
                spread(keep_next[rows_of(group, step), :]),
                load(adjoint, rows_of(group, step)),
                1.0,
            )
            for group in range(GROUPS)
        )

    finals = segment_rows(lax.fori_loop(0, L, backward_step, none))[::-1]
    seg_masks = [
        clear(first + index * L + 1, first + (index + 1) * L + 1) for index in range(segments)
    ][::-1]
    factor_seg = power(lam, L)
    own, _ = fold(zero1, factor_seg, finals, seg_masks, [None] * segments)
    pending = exchange(own, lam, adj_tp, adj_seq, T + S - 2, False)

    @pl.loop(0, 2 * N // 128)
    def _(tile):
        rows = pl.ds(pl.multiple_of(tile * 128, 128), 128)
        grad_out[rows, :] = dot(state_t[rows, :], d_mixed[...]).astype(BF16)

    carry = arrived(pending, adj_seq, False)
    _, entering = fold(carry, factor_seg, finals, seg_masks, [None] * segments)
    entering = entering[::-1]
    groups = tuple(
        tuple(
            jnp.concatenate([entering[group * 8 + lane][part] for lane in range(8)], 0)
            for part in range(2)
        )
        for group in range(GROUPS)
    )
    sums[...] = jnp.zeros_like(sums)

    def adjoint_step(step, carry, previous):
        new = []
        add_re = zero8
        add_im = zero8
        add_gamma = zero8
        for group in range(GROUPS):
            rows = rows_of(group, step)
            b = scan_step(carry[group], spread(keep_next[rows, :]), load(adjoint, rows), 1.0)
            new.append(b)
            save(adjoint, rows, jnp.concatenate(b, 1))
            u = unpack(load(proj, rows))
            v = previous(group, step)
            mask = spread(keep[rows, :])
            add_re = add_re + mask * (b[0] * v[0] + b[1] * v[1])
            add_im = add_im + mask * (b[0] * v[1] - b[1] * v[0])
            add_gamma = add_gamma + b[0] * u[0] + b[1] * u[1]
        return tuple(new), (add_re, add_im, add_gamma)

    def adjoint_body(index, carry):
        values, totals = carry
        values, added = adjoint_step(
            L - 1 - index, values, lambda group, step: unpack(load(state, rows_of(group, step - 1)))
        )
        return values, tuple(total + add for total, add in zip(totals, added))

    values, totals = lax.fori_loop(0, L - 1, adjoint_body, (groups, (zero8, zero8, zero8)))
    inside = entering_groups()
    _, added = adjoint_step(0, values, lambda group, step: inside[group])
    totals = [
        jnp.sum(total + add, 0, keepdims=True) for total, add in zip(totals, added)
    ]
    small[2:3, :] = jnp.concatenate(totals[:2], 1)
    small[3:4, :] = jnp.concatenate([totals[2] / gamma, jnp.zeros_like(gamma)], 1)
    small[4:8, :] = jnp.zeros((4, D), F32)

    LAST_ROWS = 128

    @pl.loop(0, R // LAST_ROWS)
    def _(tile):
        rows = pl.ds(pl.multiple_of(tile * LAST_ROWS, LAST_ROWS), LAST_ROWS)
        d_p = (load(adjoint, rows) * gamma_signed).astype(BF16)
        d_proj[rows, :] = d_p
        d_m = d_mixed[rows, :].astype(F32)
        d_n = dot_nt(d_p, w_in[...]) + d_m * skip_row
        c = centred[rows, :]
        sums[0:8, :] += jnp.sum((d_n * c).reshape(LAST_ROWS // 8, 8, D), 0)
        sums[8:16, :] += jnp.sum(
            (d_m * normed[rows, :].astype(F32)).reshape(LAST_ROWS // 8, 8, D), 0
        )
        d_c = d_n * gain_row
        mean = jnp.mean(d_c, 1, keepdims=True)
        cross = jnp.mean(d_c * c, 1, keepdims=True)
        inv = inv_std[rows, 0:1]
        grad_tokens[rows, :] = cot[rows, :].astype(F32) + inv * (d_c - mean - c * cross)

    small[0:1, :] = jnp.sum(sums[0:8, :], 0, keepdims=True)
    small[1:2, :] = jnp.sum(sums[8:16, :], 0, keepdims=True)

    @pl.loop(0, D // 128)
    def _(tile):
        rows = pl.ds(pl.multiple_of(tile * 128, 128), 128)
        grad_in[rows, :] = dot(normed_t[rows, :], d_proj[...]).astype(BF16)


def decay_terms(decay_log, angle):
    rate_step = jnp.exp(decay_log)
    radius = jnp.exp(-rate_step)
    return (
        radius * jnp.cos(angle),
        radius * jnp.sin(angle),
        jnp.sqrt(-jnp.expm1(-2.0 * rate_step)),
    )


def local(
    S,
    T,
    tokens,
    ln_gain,
    in_proj,
    decay_log,
    angle,
    out_proj,
    skip,
    glu_proj,
    down_proj,
    lengths,
    cotangent,
):
    R, D = tokens.shape
    n = in_proj.shape[2]
    N = n * T
    hidden = down_proj.shape[0]
    w_in = lax.all_gather(in_proj, "tp", axis=2, tiled=True)
    w_in = jnp.concatenate([w_in[0], w_in[1]], 1)
    w_out = lax.all_gather(out_proj, "tp", axis=1, tiled=True).reshape(2 * N, D)
    glu = lax.all_gather(glu_proj, "tp")
    down = lax.all_gather(down_proj, "tp")
    lam_re, lam_im, gamma = decay_terms(
        lax.all_gather(decay_log, "tp", tiled=True), lax.all_gather(angle, "tp", tiled=True)
    )
    rates = jnp.stack([jnp.concatenate([lam_re, lam_im]), jnp.concatenate([gamma, gamma])])
    rates = jnp.concatenate([rates, jnp.zeros((6, 2 * N), F32)])
    links = 2 * (T - 1 + S - 1)
    vmem = pl.BlockSpec(memory_space=pltpu.VMEM)
    outs = pl.pallas_call(
        functools.partial(layer_kernel, S, T),
        out_shape=(
            jax.ShapeDtypeStruct((R, D), BF16),
            jax.ShapeDtypeStruct((R, D), F32),
            jax.ShapeDtypeStruct((8, D), F32),
            jax.ShapeDtypeStruct((D, 2 * N), BF16),
            jax.ShapeDtypeStruct((2 * N, D), BF16),
            jax.ShapeDtypeStruct((T, 2, D, hidden), BF16),
            jax.ShapeDtypeStruct((T, D, hidden), BF16),
        ),
        in_specs=[pl.BlockSpec(memory_space=pltpu.SMEM)] + [vmem] * 9,
        out_specs=(vmem,) * 7,
        scratch_shapes=[
            pltpu.VMEM((R, D), F32),
            pltpu.VMEM((R, 128), F32),
            pltpu.VMEM((R, D), BF16),
            pltpu.VMEM((D, R), BF16),
            pltpu.VMEM((D, R), BF16),
            pltpu.VMEM((2 * N // 128, R, 128), F32),
            pltpu.VMEM((R, 128), F32),
            pltpu.VMEM((R, 128), F32),
            pltpu.VMEM((2 * N // 128, R, 128), F32),
            pltpu.VMEM((2 * N, R), BF16),
            pltpu.VMEM((R, D), BF16),
            pltpu.VMEM((D, R), BF16),
            pltpu.VMEM((R, D), F32),
            pltpu.VMEM((R, D), F32),
            pltpu.VMEM((R, D), F32),
            pltpu.VMEM((R, D), BF16),
            pltpu.VMEM((2 * N // 128, R, 128), F32),
            pltpu.VMEM((R, 2 * N), BF16),
            pltpu.VMEM((R, hidden), BF16),
            pltpu.VMEM((R, hidden), BF16),
            pltpu.VMEM((R, hidden), BF16),
            pltpu.VMEM((8 * GROUPS, 2 * N), F32),
            pltpu.VMEM((16, D), F32),
            pltpu.VMEM((T, 8, 2 * N), F32),
            pltpu.VMEM((S, 8, 2 * N), F32),
            pltpu.VMEM((T, 8, 2 * N), F32),
            pltpu.VMEM((S, 8, 2 * N), F32),
            pltpu.SemaphoreType.DMA((links,)),
            pltpu.SemaphoreType.DMA((links,)),
        ],
        compiler_params=pltpu.CompilerParams(
            collective_id=0, has_side_effects=True, vmem_limit_bytes=58 * 2**20
        ),
    )(
        lengths,
        tokens,
        cotangent,
        ln_gain.reshape(1, D),
        skip.reshape(1, D),
        rates,
        w_in,
        w_out,
        glu,
        down,
    )
    result, grad_tokens, small, grad_in, grad_out, grad_glu, grad_down = outs
    small = lax.psum(small, ("seq", "tp"))
    t = lax.axis_index("tp")

    def reduced(part):
        part = lax.psum_scatter(part, "tp", scatter_dimension=0, tiled=True)
        return lax.psum(part, "seq").astype(F32)

    grad_in = grad_in.reshape(D, 2, T, n).transpose(2, 1, 0, 3).reshape(T * 2, D, n)
    grad_in = reduced(grad_in)
    grad_out = grad_out.reshape(2, T, n, D).transpose(1, 0, 2, 3).reshape(T * 2, n, D)
    grad_out = reduced(grad_out)
    grad_glu = reduced(grad_glu.reshape(T * 2, D, hidden))
    grad_down = reduced(grad_down)[0].T

    def mine(row):
        return lax.dynamic_slice_in_dim(row, t * n, n)

    g_re, g_im, g_gamma = (mine(small[2, :N]), mine(small[2, N:]), mine(small[3, :N]))
    _, pull = jax.vjp(decay_terms, decay_log, angle)
    grad_decay, grad_angle = pull((g_re, g_im, g_gamma))
    return (
        result,
        grad_tokens,
        small[0],
        grad_in,
        grad_decay,
        grad_angle,
        grad_out,
        small[1],
        grad_glu,
        grad_down,
    )


def solution(mesh):
    in_specs = (
        P(("seq", "tp"), None),
        P(),
        P(None, None, "tp"),
        P("tp"),
        P("tp"),
        P(None, "tp", None),
        P(),
        P(None, None, "tp"),
        P("tp", None),
        P(),
        P(("seq", "tp"), None),
    )
    out_specs = (
        P(("seq", "tp"), None),
        P(("seq", "tp"), None),
        P(),
        P(None, None, "tp"),
        P("tp"),
        P("tp"),
        P(None, "tp", None),
        P(),
        P(None, None, "tp"),
        P("tp", None),
    )
    return jax.shard_map(
        functools.partial(local, mesh.shape["seq"], mesh.shape["tp"]),
        mesh=mesh,
        in_specs=in_specs,
        out_specs=out_specs,
        check_vma=False,
    )
```

time: 3060 us -> 357 us (0.12); the launches traced: 3000 us -> 355 us
  local copies, waits for them, and re-layouts: 2230 us -> 12.4 us
  other arithmetic: 310 us -> 5.75 us
  waiting for transfers between devices: 280 us -> 171 us
  Pallas kernels: 0 us -> 71.5 us
  matrix products: 59.1 us -> 0 us
    slice x306 -> x3, local copies, waits for them, and re-layouts: 1320 us -> 1.32 us  [the longest x1 0.73 us: local(): w_in = jnp.concatenate([w_in[0], w_in[1]], 1)]
    pad x176 -> x0, local copies, waits for them, and re-layouts: 792 us -> none  [the longest x88 464 us: backward_state(): lax.associative_scan(compose, flip_rows((back_re, back_im, d_state_re, d_...]
    add x150 -> x0, other arithmetic: 159 us -> none  [the longest x48 73.2 us: backward_state(): lax.associative_scan(compose, flip_rows((back_re, back_im, d_state_re, d_...]
    psum x3 -> x1, waiting for transfers between devices: 175 us -> 57.7 us  [reduced(): return lax.psum(part, 'seq').astype(F32)]
    concatenate x85 -> x3, other arithmetic: 79.5 us -> 1.52 us  [the longest x1 0.83 us: local(): w_in = jnp.concatenate([w_in[0], w_in[1]], 1)]
    pallas_call x0 -> x1, Pallas kernels: none -> 71.5 us  [local(): pl.pallas_call(functools.partial(layer_kernel, S, T), out_shape=(jax.Shap...]
    rev x8 -> x0, local copies, waits for them, and re-layouts: 64.9 us -> none  [the longest x4 64.9 us: flip_rows(): return tuple((jnp.flip(item, 0) for item in items))]
    dot_general x21 -> x0, matrix products: 59.1 us -> none  [the longest x1 7.21 us: local(): jnp.dot(d_proj_im, in_proj[1].T, preferred_element_type=jnp.float32)]
  transfers between devices with their start and end apart: 7 -> 7, of which waited for: 4 -> 4; matrix products, arithmetic and copies ran while one was open for 42% -> 2% of each run, Pallas kernels for 0% -> 0%
where the time goes in v1:
time: 357 us; the launch traced here: 355 us
  waiting for transfers between devices  171 us (48%)
  blocking collectives  79.2 us (22%)
  Pallas kernels  71.5 us (20%)
  between operations  15 us (4%)
  local copies, waits for them, and re-layouts  12.4 us (3%)
  other arithmetic  5.75 us (2%)
    reduce_scatter x4, waiting for transfers between devices, reduced(): part = lax.psum_scatter(part, 'tp', scatter_dimension=0, tiled=True)  73.9 us
    pallas_call x1, Pallas kernels, local(): pl.pallas_call(functools.partial(layer_kernel, S, T), out_shape=(jax.Shap...  71.5 us
    psum x1, waiting for transfers between devices, reduced(): return lax.psum(part, 'seq').astype(F32)  57.7 us
    psum x1, blocking collectives, local(): small = lax.psum(small, ('seq', 'tp'))  38.7 us
    all_gather x1, waiting for transfers between devices, local(): glu = lax.all_gather(glu_proj, 'tp')  37 us
    all_gather x1, blocking collectives, local(): w_in = lax.all_gather(in_proj, 'tp', axis=2, tiled=True)  16.6 us
    all_gather x1, blocking collectives, local(): w_out = lax.all_gather(out_proj, 'tp', axis=1, tiled=True).reshape(2 * N, D)  13.6 us
    unnamed x1, blocking collectives  10.2 us
  transfers between devices with their start and end apart: 7, of which 4 were waited for; matrix products, arithmetic and copies ran while one was open for 2% of the time, Pallas kernels for 0%

profile of v1, /device:TPU:1, one launch (start us, length us, event | category | flops | bytes accessed | tf_op | source)
XLA Modules:
  0.0 355.1 jit_solution(6187471935744188058)
XLA Ops:
  7.2 0.0 all-gather.7.cloned.1.call-start
  7.2 0.7 all-gather.7.cloned.1.call-update
  7.9 0.0 all-gather.5.cloned.1.call-start
  8.0 0.7 all-gather.5.cloned.1.call-update
  8.7 0.0 reduce-scatter.5.cloned.1.call-start
  8.7 1.0 copy.34
  9.8 0.0 copy-start.10
  9.8 16.6 %all_gather.26 = bf16[2,512,256]{1,0,2:T(2,128)(2,1)S(1)} all-gather(bf16[2,512,64]{1,0,2:T(2,128)(2,1)S(1)} %copy.34), channel_id=1, replica_groups=mesh['seq'=8,'tp'=4] {'tp'}, dimensions={2}, use_global_device_ids=true | all-gather | bytes 655360 | tf_op jit(solution)/shard_map/all_gather | solution.py:492
  26.4 0.7 fusion.6
  27.2 0.5 copy.41
  27.6 0.5 copy.42
  28.1 0.6 reshape.48.skip
  28.7 0.6 dynamic-slice.3
  30.0 0.2 dynamic-update-slice
  30.2 0.2 dynamic-update-slice.1
  30.5 0.1 pad.4.clone
  30.5 10.2 %all-reduce.2 = (f32[256]{0:T(256)S(1)}, f32[256]{0:T(256)S(1)}) all-reduce(f32[256]{0:T(256)S(1)} %dynamic-update-slice, f32[256]{0:T(256)S(1)} %dynamic-update-slice.1), channel_id=1, replica_groups=mesh['seq'=8,'tp'=4] {'tp'}, use_global_device_ids=true, to_apply=%add | all-reduce | flops 512 | bytes 4096
  40.8 0.8 pad_maximum_fusion.w_in
  41.7 13.6 %all_gather.27 = bf16[2,256,512]{2,1,0:T(8,128)(2,1)} all-gather(bf16[2,64,512]{2,1,0:T(8,128)(2,1)S(1)} %copy-done.3), channel_id=1, replica_groups=mesh['seq'=8,'tp'=4] {'tp'}, dimensions={1}, use_global_device_ids=true | all-gather | bytes 655360 | tf_op jit(solution)/shard_map/all_gather | solution.py:494
  55.2 0.7 maximum_maximum_fusion.rates
  55.9 37.0 %all-gather.5.cloned.1.call-done = bf16[8,512,256]{2,1,0:T(8,128)(2,1)} async-done(((bf16[2,512,256]{2,1,0:T(8,128)(2,1)}), bf16[8,512,256]{2,1,0:T(8,128)(2,1)}) %all-gather.5.cloned.1.call-update) | async-done | bytes 2097168 | tf_op jit(solution)/shard_map/all_gather | solution.py:495
  92.9 71.5 %shard_map.186 = (bf16[1024,512]{1,0:T(8,128)(2,1)}, f32[1024,512]{1,0:T(8,128)}, f32[8,512]{1,0:T(8,128)}, bf16[512,512]{1,0:T(8,128)(2,1)}, bf16[512,512]{1,0:...) custom-call(s32[6]{0:T(128)} %lengths.1, bf16[1024,512]{1,0:T(8,128)(2,1)} %tokens.1, ...), custom_call_target="tpu_custom_call" | custom-call | tf_op jit(solution)/shard_map/pallas_call | solution.py:504
  164.4 1.3 copy.37
  165.7 0.8 copy.38
  166.5 0.0 reduce-scatter.5.cloned.1.call-update
  166.6 0.0 reduce-scatter.7.cloned.1.call-start
  166.6 0.8 copy.39
  167.5 0.0 reduce-scatter.7.cloned.1.call-update
  167.5 0.0 reduce-scatter.11.cloned.1.call-start
  167.5 0.5 reduce-scatter.11.cloned.1.call-update
  168.1 0.0 reduce-scatter.9.cloned.1.call-start
  168.1 0.5 reduce-scatter.9.cloned.1.call-update
  168.7 0.0 all-reduce.6.cloned.1.call-start
  168.8 38.7 %psum.35 = f32[8,512]{1,0:T(8,128)S(1)} all-reduce(f32[8,512]{1,0:T(8,128)S(1)} %copy-done.6), channel_id=1, replica_groups=mesh['seq'=8,'tp'=4] {'seq','tp'}, use_global_device_ids=true, to_apply=%region_0.0 | all-reduce | flops 4096 | bytes 32768 | tf_op jit(solution)/shard_map/psum | solution.py:564
  207.5 0.0 reduce-scatter.5.cloned.1.call-done
  207.5 0.0 reduce-scatter.7.cloned.1.call-done
  207.6 29.0 %reduce-scatter.11.cloned.1.call-done = bf16[1,512,256]{2,1,0:T(8,128)(2,1)} async-done(((bf16[4,512,256]{2,1,0:T(8,128)(2,1)}), bf16[1,512,256]{2,1,0:T(8,128)(2,1)}) %reduce-scatter.11.cloned.1.call-update) | async-done | bytes 262160 | tf_op jit(solution)/shard_map/reduce_scatter | solution.py:568
  236.6 44.8 %reduce-scatter.9.cloned.1.call-done = bf16[2,512,256]{2,1,0:T(8,128)(2,1)} async-done(((bf16[8,512,256]{2,1,0:T(8,128)(2,1)}), bf16[2,512,256]{2,1,0:T(8,128)(2,1)}) %reduce-scatter.9.cloned.1.call-update) | async-done | bytes 524304 | tf_op jit(solution)/shard_map/reduce_scatter | solution.py:568
  281.4 0.0 all-reduce.6.cloned.1.call-update
  281.4 0.6 multiply_add_fusion
  282.0 0.6 fusion.7
  282.6 57.7 %all-reduce.6.cloned.1.call-done = (bf16[256,512]{0,1:T(8,128)(2,1)}, bf16[2,512,64]{1,2,0:T(8,128)(2,1)}, bf16[2,64,512]{2,1,0:T(8,128)(2,1)}, bf16[2,512,256]{2,1,0:T(8,128)(2,1)}) async-done(((bf16[256,512]{0,1:T(8,128)(2,1)}, bf16[2,512,64]{1,2,0:T(8,128)(2,1)}, bf16[2,64,512]{2,1,0:T(8,128)(2,1)}, bf16[2,512,256]{2,1,0:T(8,128)(2,1)}), (bf16[256,512]{0,1:T(8,128)(2,1)}, bf16[2,512,64]{1,2,0:T(8,128)(2,1)}, ...) | async-done | bytes 1048592 | tf_op jit(solution)/shard_map/psum | solution.py:569
  340.3 2.1 convert_element_type.12
  342.5 2.0 copy.40
  344.5 0.7 convert_element_type.10
  345.2 0.7 convert_element_type.11
  346.0 1.0 copy.51
  346.9 1.3 copy.52
  (29 shorter events, 0.2 us)
Async XLA Ops:
  7.2 48.7 %all-gather.7.cloned.1.call-start = ((), (), s32[]{:S(2)}) async-start(), calls=%async_computation.9 | async-start | bytes 1310720 | tf_op jit(solution)/shard_map/all_gather | solution.py:496
  7.9 85.0 %all-gather.5.cloned.1.call-start = ((), (), s32[]{:S(2)}) async-start(), calls=%async_computation.8 | async-start | bytes 2621440 | tf_op jit(solution)/shard_map/all_gather | solution.py:495
  8.7 198.9 %reduce-scatter.5.cloned.1.call-start = ((), (), s32[]{:S(2)}) async-start(), calls=%async_computation.4 | async-start | bytes 655360 | tf_op jit(solution)/shard_map/reduce_scatter | solution.py:568
  9.8 18.4 %copy-start.7 = (bf16[512]{0:T(512)(128)(2,1)S(1)}, bf16[512]{0:T(512)(128)(2,1)}, u32[]{:S(2)}) copy-start(bf16[512]{0:T(512)(128)(2,1)} %param.17) | copy-start | bytes 3076
  9.8 19.0 %copy-start.10 = (u32[32]{0:T(128)S(1)}, u32[32]{0:T(128)}, u32[]{:S(2)}) copy-start(u32[32]{0:T(128)} %constant.22) | copy-start | bytes 388
  9.8 20.2 %copy-start.8 = (f32[64]{0:T(128)S(1)}, f32[64]{0:T(128)}, u32[]{:S(2)}) copy-start(f32[64]{0:T(128)} %param.14) | copy-start | bytes 772
  9.8 20.4 %copy-start.9 = (f32[64]{0:T(128)S(1)}, f32[64]{0:T(128)}, u32[]{:S(2)}) copy-start(f32[64]{0:T(128)} %param.15) | copy-start | bytes 772
  26.4 15.2 %copy-start.3 = (bf16[2,64,512]{2,1,0:T(8,128)(2,1)S(1)}, bf16[2,64,512]{2,1,0:T(8,128)(2,1)}, u32[]{:S(2)}) copy-start(bf16[2,64,512]{2,1,0:T(8,128)(2,1)} %param.16) | copy-start | bytes 393220
  164.4 2.2 copy-start.2
  166.6 41.0 %reduce-scatter.7.cloned.1.call-start = ((), (), s32[]{:S(2)}) async-start(), calls=%async_computation.5 | async-start | bytes 655360 | tf_op jit(solution)/shard_map/reduce_scatter | solution.py:568
  167.5 1.3 copy-start.6
  167.5 69.1 %reduce-scatter.11.cloned.1.call-start = ((), (), s32[]{:S(2)}) async-start(), calls=%async_computation.7 | async-start | bytes 1310720 | tf_op jit(solution)/shard_map/reduce_scatter | solution.py:568
  168.1 113.3 %reduce-scatter.9.cloned.1.call-start = ((), (), s32[]{:S(2)}) async-start(), calls=%async_computation.6 | async-start | bytes 2621440 | tf_op jit(solution)/shard_map/reduce_scatter | solution.py:568
  168.7 171.7 %all-reduce.6.cloned.1.call-start = ((), (), s32[]{:S(2)}) async-start(), calls=%async_computation.10 | async-start | bytes 2097152 | tf_op jit(solution)/shard_map/psum | solution.py:569
  281.4 64.6 %copy-start.1 = (bf16[1024,512]{1,0:T(8,128)(2,1)S(1)}, bf16[1024,512]{1,0:T(8,128)(2,1)}, u32[]{:S(2)}) copy-start(bf16[1024,512]{1,0:T(8,128)(2,1)} %get-tuple-element.96) | copy-start | bytes 3145732
  340.3 4.2 %copy-start.5 = (bf16[2,512,64]{1,2,0:T(8,128)(2,1)S(1)}, bf16[2,512,64]{1,2,0:T(8,128)(2,1)}, u32[]{:S(2)}) copy-start(bf16[2,512,64]{1,2,0:T(8,128)(2,1)} %get-tuple-element.67) | copy-start | bytes 393220
  340.3 4.9 %copy-start.4 = (bf16[2,64,512]{2,1,0:T(8,128)(2,1)S(1)}, bf16[2,64,512]{2,1,0:T(8,128)(2,1)}, u32[]{:S(2)}) copy-start(bf16[2,64,512]{2,1,0:T(8,128)(2,1)} %get-tuple-element.68) | copy-start | bytes 393220
  342.5 4.5 %copy-start = (f32[1024,512]{1,0:T(8,128)S(1)}, f32[1024,512]{1,0:T(8,128)}, u32[]{:S(2)}) copy-start(f32[1024,512]{1,0:T(8,128)} %get-tuple-element.97) | copy-start | bytes 6291460
Sparse Core Ops, SparseCore 0:
  9.6 33.5 all-gather.6
  44.8 48.0 all-gather.4
  166.7 18.1 reduce-scatter.4
  187.6 19.9 reduce-scatter.6
  209.7 26.8 reduce-scatter.10
  238.8 42.4 reduce-scatter.8
  284.8 55.4 all-reduce.5

commit v2 on v1

v2 whole, which is shorter than its diff:
```python
import functools
import types
import jax
import jax.numpy as jnp
from jax import lax
from jax.experimental import pallas as pl
from jax.experimental.pallas import tpu as pltpu
from jax.sharding import PartitionSpec as P

epsilon = 1e-05
MESH = pl.DeviceIdType.MESH
F32 = jnp.float32
BF16 = jnp.bfloat16
GROUPS = 2
SEGMENTS = 8 * GROUPS
BLOCK = SEGMENTS * SEGMENTS


def dot(left, right):
    return jnp.dot(left, right, preferred_element_type=F32)


def dot_nt(left, right):
    return lax.dot_general(left, right, (((1,), (1,)), ((), ())), preferred_element_type=F32)


def complex_mul(left_re, left_im, right_re, right_im):
    return (left_re * right_re - left_im * right_im, left_re * right_im + left_im * right_re)


def power(base, exponent):
    result = None
    square = base
    while exponent:
        if exponent & 1:
            result = square if result is None else complex_mul(*result, *square)
        exponent >>= 1
        if exponent:
            square = complex_mul(*square, *square)
    return result


class Links:
    def __init__(self, send_sem, recv_sem):
        self.send_sem = send_sem
        self.recv_sem = recv_sem
        self.started = []

    def send(self, source, target, device):
        index = len(self.started)
        copy = pltpu.make_async_remote_copy(
            src_ref=source,
            dst_ref=target,
            send_sem=self.send_sem.at[index],
            recv_sem=self.recv_sem.at[index],
            device_id=device,
            device_id_type=MESH,
        )
        copy.start()
        self.started.append(copy)
        return copy

    def close(self):
        for copy in self.started:
            copy.wait_send()


def arrive(copies):
    for copy in copies:
        copy.wait_recv()


class Gather:
    def __init__(self, place, buffer):
        self.place = place
        self.buffer = buffer

    def over_tp(self):
        p = self.place
        self.copies = [
            p.links.send(
                self.buffer.at[0, p.chip, p.core],
                self.buffer.at[p.T - k, p.chip, p.core],
                (p.s, lax.rem(p.t + k, p.T)),
            )
            for k in range(1, p.T)
        ]

    def over_plane(self):
        p = self.place
        arrive(self.copies)
        mine = self.buffer.at[pl.ds(1, p.T - 1), p.chip, p.core]
        self.copies = [p.links.send(mine, mine, device) for _, device in p.chips]

    def over_cores(self):
        p = self.place
        arrive(self.copies)
        mine = self.buffer.at[pl.ds(1, p.T - 1), :, p.core]
        self.copies = [p.links.send(mine, mine, p.sibling)]

    def finish(self):
        arrive(self.copies)


class Reduce:
    def __init__(self, place, full, halves, eighths, summed):
        self.place = place
        self.full = full
        self.halves = halves
        self.eighths = eighths
        self.summed = summed

    def over_cores(self):
        p = self.place
        self.copies = [
            p.links.send(self.full.at[:, :, 1 - p.core], self.halves, p.sibling)
        ]

    def over_plane(self):
        p = self.place
        arrive(self.copies)
        parts, chips = self.halves.shape[:2]

        @pl.loop(0, parts * chips)
        def _(index):
            part, chip = (lax.div(index, chips), lax.rem(index, chips))
            self.halves[part, chip] = (
                self.full[part, chip, p.core].astype(F32) + self.halves[part, chip].astype(F32)
            ).astype(BF16)

        self.copies = [
            p.links.send(self.halves.at[:, chip], self.eighths.at[k], device)
            for k, (chip, device) in enumerate(p.chips)
        ]

    def sum_plane(self):
        p = self.place
        arrive(self.copies)

        @pl.loop(0, self.halves.shape[0])
        def _(part):
            total = self.halves[part, p.chip].astype(F32)
            for k in range(len(p.chips)):
                total = total + self.eighths[k, part].astype(F32)
            self.summed[part] = total.astype(BF16)


class Spread:
    def __init__(self, place, buffer):
        self.place = place
        self.buffer = buffer

    def over_plane(self):
        p = self.place
        mine = self.buffer.at[:, p.chip, p.core]
        self.copies = [p.links.send(mine, mine, device) for _, device in p.chips]

    def over_cores(self):
        p = self.place
        arrive(self.copies)
        mine = self.buffer.at[:, :, p.core]
        self.copies = [p.links.send(mine, mine, p.sibling)]

    def finish(self):
        arrive(self.copies)


class Place:
    def __init__(self, S, T, links):
        self.S, self.T, self.links = (S, T, links)
        self.s = lax.axis_index("seq")
        self.t = lax.axis_index("tp")
        C = S // 2
        self.core = lax.rem(self.s, 2)
        self.chip = lax.div(self.s, 2)
        self.sibling = (self.chip * 2 + 1 - self.core, self.t)
        self.chips = []
        for k in range(1, C):
            chip = lax.rem(self.chip + k, C)
            self.chips.append((chip, (chip * 2 + self.core, self.t)))


def layer_kernel(S, T, fused, names, *refs):
    r = types.SimpleNamespace(**dict(zip(names, refs)))
    links = Links(r.send_sem, r.recv_sem)
    place = Place(S, T, links)
    lengths = r.lengths
    tokens = r.tokens
    cot = r.cot
    gain = r.gain
    skip = r.skip
    result, grad_tokens, small = (r.result, r.grad_tokens, r.small)
    turn = r.turn
    tokens_in = r.tokens_in
    cot_in = r.cot_in
    centred = r.centred
    inv_std = r.inv_std
    normed = r.normed
    normed_t = r.normed_t
    cot_t = r.cot_t
    proj = r.proj
    keep = r.keep
    keep_next = r.keep_next
    state = r.state
    state_t = r.state_t
    act = r.act
    act_t = r.act_t
    d_gelu = r.d_gelu
    d_act = r.d_act
    summed = r.summed
    d_mixed = r.d_mixed
    adjoint = r.adjoint
    d_proj = r.d_proj
    hidden = r.hidden
    d_value = r.d_value
    d_gate = r.d_gate
    seg_carry, sums = (r.seg_carry, r.sums)
    w_in, w_out = (r.w_in, r.w_out)
    R, D = tokens.shape
    N = w_in.shape[1] // 2
    n = N // T
    L = R // SEGMENTS
    s = place.s
    t = place.t
    first = (s * T + t) * R

    peers_tp = [lax.rem(t + k, T) for k in range(1, T)]
    peers_seq = [lax.rem(s + k, S) for k in range(1, S)]
    barrier = pltpu.get_barrier_semaphore()
    for peer in peers_tp:
        pl.semaphore_signal(barrier, inc=1, device_id=(s, peer), device_id_type=MESH)
    for peer in peers_seq:
        pl.semaphore_signal(barrier, inc=1, device_id=(peer, t), device_id_type=MESH)

    lane = lax.broadcasted_iota(jnp.int32, (D, 128), 1)
    if fused:
        in_slices, out_slices = (r.in_slices, r.out_slices)
        glu_slices, down_slices = (r.glu_slices, r.down_slices)
        local_copies = [
            pltpu.make_async_copy(r.out_proj, out_slices.at[0], r.local_sem.at[0]),
            pltpu.make_async_copy(r.glu_proj.at[0], glu_slices.at[0, 0], r.local_sem.at[1]),
            pltpu.make_async_copy(r.glu_proj.at[1], glu_slices.at[1, 0], r.local_sem.at[2]),
            pltpu.make_async_copy(r.down_proj, down_slices.at[0], r.local_sem.at[3]),
        ]
        for copy in local_copies:
            copy.start()
        row = lax.broadcasted_iota(jnp.int32, (n, 128), 0)
        column = lax.broadcasted_iota(jnp.int32, (n, 128), 1)
        merged = dot(r.in_proj[0], jnp.where(row == column, 1.0, 0.0).astype(BF16)) + dot(
            r.in_proj[1], jnp.where(row + n == column, 1.0, 0.0).astype(BF16)
        )
        in_slices[0] = merged.astype(BF16).reshape(in_slices.shape[1:])
        r.rates_all[t] = r.rates[...]
        for copy in local_copies:
            copy.wait()
        gather_in = Gather(place, in_slices)
        gather_out = Gather(place, out_slices)
        gather_value = Gather(place, glu_slices.at[0])
        gather_gate = Gather(place, glu_slices.at[1])
        gather_down = Gather(place, down_slices)
        pl.semaphore_wait(barrier, T - 1 + S - 1)
        rate_copies = [
            links.send(r.rates_all.at[t], r.rates_all.at[t], (s, peer)) for peer in peers_tp
        ]
        for gather in (gather_in, gather_out, gather_value, gather_gate, gather_down):
            gather.over_tp()

    starts = []
    total = jnp.int32(0)
    for index in range(lengths.shape[0]):
        starts.append(total)
        total = total + lengths[index]

    def keeps(position):
        hit = position == starts[0]
        for start in starts[1:]:
            hit = hit | (position == start)
        return jnp.where(hit, 0.0, 1.0)

    def clear(low, high):
        hit = (starts[0] >= low) & (starts[0] < high)
        for start in starts[1:]:
            hit = hit | ((start >= low) & (start < high))
        return jnp.where(hit, 0.0, 1.0)

    gain_row = gain[...]
    skip_row = skip[...].astype(F32)

    down_index = lax.broadcasted_iota(jnp.int32, (BLOCK, BLOCK), 0)
    across_index = lax.broadcasted_iota(jnp.int32, (BLOCK, BLOCK), 1)
    turned = lax.rem(down_index, SEGMENTS) * SEGMENTS + lax.div(down_index, SEGMENTS)
    turn[...] = jnp.where(turned == across_index, 1.0, 0.0).astype(BF16)

    def pieces(block):
        return [
            pl.ds(pl.multiple_of(run * L + block * SEGMENTS, SEGMENTS), SEGMENTS)
            for run in range(SEGMENTS)
        ]

    def taken(ref, block):
        return dot(turn[...], jnp.concatenate([ref[piece, :] for piece in pieces(block)], 0))

    def block_rows(tile):
        return pl.ds(pl.multiple_of(tile * BLOCK, BLOCK), BLOCK)

    def norm_tile(tile):
        rows = block_rows(tile)
        x = taken(tokens, tile)
        tokens_in[rows, :] = x.astype(BF16)
        mean = jnp.mean(x, 1, keepdims=True)
        inv = lax.rsqrt(jnp.mean(x * x, 1, keepdims=True) - mean * mean + epsilon)
        c = (x - mean) * inv
        centred[rows, :] = c
        inv_std[rows, :] = jnp.broadcast_to(inv, (BLOCK, 128))
        n_rows = (c * gain_row).astype(BF16)
        normed[rows, :] = n_rows
        normed_t[:, rows] = n_rows.T

    def cot_tile(tile):
        rows = block_rows(tile)
        cot_rows = taken(cot, tile).astype(BF16)
        cot_in[rows, :] = cot_rows
        cot_t[:, rows] = cot_rows.T
        index = tile * BLOCK + lax.broadcasted_iota(jnp.int32, (BLOCK, 128), 0)
        position = first + lax.rem(index, SEGMENTS) * L + lax.div(index, SEGMENTS)
        keep[rows, :] = keeps(position)
        keep_next[rows, :] = keeps(position + 1)

    pl.loop(0, R // BLOCK)(norm_tile)
    if fused:
        gather_in.over_plane()
        gather_out.over_plane()
    pl.loop(0, R // BLOCK)(cot_tile)
    if fused:
        gather_in.over_cores()
        gather_out.over_cores()
        arrive(rate_copies)
        gather_value.over_plane()
        gather_in.finish()
        half = lane < 64
        for k in range(T // 2):
            even, odd = (
                in_slices[lax.rem(2 * k + part + T - t, T)].reshape(D, 128).astype(F32)
                for part in range(2)
            )
            at = k * 128
            w_in[:, at : at + 128] = jnp.where(half, even, pltpu.roll(odd, 64, 1)).astype(BF16)
            w_in[:, N + at : N + at + 128] = jnp.where(half, pltpu.roll(even, 64, 1), odd).astype(
                BF16
            )
        rate_rows = [r.rates_all[z] for z in range(T)]
        half8 = lane[:8] < 64

        def joined(rows, part):
            out = []
            for k in range(T // 2):
                even, odd = (rows[2 * k], rows[2 * k + 1])
                if part == 0:
                    out.append(jnp.where(half8, even, pltpu.roll(odd, 64, 1)))
                else:
                    out.append(jnp.where(half8, pltpu.roll(even, 64, 1), odd))
            return jnp.concatenate(out, 1)

        lam_gamma = joined(rate_rows, 0)
        lam_re = lam_gamma[0:1]
        lam_im = joined(rate_rows, 1)[0:1]
        gamma = lam_gamma[1:2]
    else:
        pl.semaphore_wait(barrier, T - 1 + S - 1)
        lam_re = r.rates[0:1, :N]
        lam_im = r.rates[0:1, N:]
        gamma = r.rates[1:2, :N]
    gamma_signed = jnp.concatenate([gamma, -gamma], 1)

    @pl.loop(0, R // BLOCK)
    def _(tile):
        rows = block_rows(tile)
        proj[rows, :] = dot(normed[rows, :], w_in[...]) * gamma_signed

    low8_re = jnp.broadcast_to(lam_re, (8, N))
    low8_im = jnp.broadcast_to(lam_im, (8, N))

    def rows_of(group, step):
        return pl.ds(pl.multiple_of(step * SEGMENTS + group * 8, 8), 8)

    def spread(row):
        return jnp.concatenate([row] * (N // 128), 1)

    def scan_step(values, mask, add, sign):
        new_re, new_im = complex_mul(low8_re, sign * low8_im, *(value * mask for value in values))
        return (new_re + add[:, :N], new_im + add[:, N:])

    zero8 = jnp.zeros((8, N), F32)
    none = tuple((zero8, zero8) for _ in range(GROUPS))

    def forward_step(step, carry):
        return tuple(
            scan_step(
                carry[group],
                spread(keep[rows_of(group, step), :]),
                proj[rows_of(group, step), :],
                -1.0,
            )
            for group in range(GROUPS)
        )

    def segment_rows(finals):
        return [
            (finals[group][0][sub : sub + 1], finals[group][1][sub : sub + 1])
            for group in range(GROUPS)
            for sub in range(8)
        ]

    def fold(start, factor, items, masks, taken):
        before = []
        carry = start
        for (item_re, item_im), mask, take in zip(items, masks, taken):
            before.append(carry)
            moved = complex_mul(*factor, *carry)
            longer = (moved[0] * mask + item_re, moved[1] * mask + item_im)
            if take is None:
                carry = longer
            else:
                carry = tuple(jnp.where(take, new, old) for new, old in zip(longer, carry))
        return carry, before

    zero1 = (jnp.zeros((1, N), F32), jnp.zeros((1, N), F32))
    lam = (lam_re, lam_im)
    conj = (lam_re, -lam_im)

    def unpack(row):
        return (row[:, :N], row[:, N:])

    def packed(row, height):
        parts = [row[:, at : at + 128] for at in range(0, row.shape[1], 128)]
        return jnp.concatenate(parts + [parts[0]] * (height - len(parts)), 0)

    def unpacked(tile, height):
        return jnp.concatenate([tile[k : k + 1, :] for k in range(height)], 1)

    class Exchange:
        def __init__(self, own, factor, tp_buf, seq_buf, forward):
            self.forward = forward
            self.shift = 0 if forward else 1
            self.factor_tp = power(factor, R)
            self.factor_seq = power(self.factor_tp, T)
            self.tp_buf, self.seq_buf = (tp_buf, seq_buf)
            tp_buf[t] = packed(jnp.concatenate(own, 1), 8)
            self.copies = [
                links.send(tp_buf.at[t], tp_buf.at[t], (s, peer)) for peer in peers_tp
            ]

        def order(self, count):
            return list(range(count)) if self.forward else list(range(count))[::-1]

        def before(self, other, mine):
            return other < mine if self.forward else other > mine

        def value(self, tile):
            return unpack(unpacked(tile, 2 * N // 128))

        def over_seq(self):
            arrive(self.copies)
            row = s * T * R + self.shift
            self.items = [self.value(self.tp_buf[z]) for z in self.order(T)]
            self.masks = [clear(row + z * R, row + (z + 1) * R) for z in self.order(T)]
            block, _ = fold(zero1, self.factor_tp, self.items, self.masks, [None] * T)
            self.seq_buf[s] = packed(jnp.concatenate(block, 1), 8)
            self.copies = [
                links.send(self.seq_buf.at[s], self.seq_buf.at[s], (peer, t)) for peer in peers_seq
            ]

        def carry(self):
            arrive(self.copies)
            blocks = self.order(S)
            span = T * R
            carry, _ = fold(
                zero1,
                self.factor_seq,
                [self.value(self.seq_buf[block]) for block in blocks],
                [clear(block * span + self.shift, (block + 1) * span + self.shift) for block in blocks],
                [self.before(block, s) for block in blocks],
            )
            carry, _ = fold(
                carry,
                self.factor_tp,
                self.items,
                self.masks,
                [self.before(z, t) for z in self.order(T)],
            )
            return carry

    finals = segment_rows(lax.fori_loop(0, L, forward_step, none))
    seg_masks = [clear(first + index * L, first + (index + 1) * L) for index in range(SEGMENTS)]
    factor_seg = power(conj, L)
    own, _ = fold(zero1, factor_seg, finals, seg_masks, [None] * SEGMENTS)
    exchange = Exchange(own, conj, r.state_tp, r.state_seq, True)
    if fused:
        gather_gate.over_plane()
    exchange.over_seq()
    if fused:
        gather_down.over_plane()
        gather_out.finish()
        for i in range(T):
            at = lax.rem(t + i, T) * n
            for part in range(2):
                w_out[pl.ds(pl.multiple_of(part * N + at, n), n), :] = out_slices[
                    i, part * (S // 4) : (part + 1) * (S // 4)
                ].reshape(n, D)
    carry = exchange.carry()
    _, entering = fold(carry, factor_seg, finals, seg_masks, [None] * SEGMENTS)
    for index, (row_re, row_im) in enumerate(entering):
        seg_carry[index : index + 1, :] = jnp.concatenate([row_re, row_im], 1)

    def write_state(step, carry):
        new = forward_step(step, carry)
        for group in range(GROUPS):
            state[rows_of(group, step), :] = jnp.concatenate(new[group], 1)
        return new

    def entering_groups():
        return tuple(
            unpack(seg_carry[group * 8 : group * 8 + 8, :]) for group in range(GROUPS)
        )

    lax.fori_loop(0, L, write_state, entering_groups())

    if fused:
        gather_value.over_cores()

    @pl.loop(0, R // BLOCK)
    def _(tile):
        rows = block_rows(tile)
        low = state[rows, :].astype(BF16)
        state_t[:, rows] = low.T
        x = dot(low, w_out[...]) + skip_row * normed[rows, :].astype(F32)
        scale = 0.7978845608028654
        th = jnp.tanh(scale * (x + 0.044715 * x * x * x))
        half = 0.5 * (1.0 + th)
        a = (x * half).astype(BF16)
        act[rows, :] = a
        act_t[:, rows] = a.T
        d_gelu[rows, :] = half + 0.5 * x * (1.0 - th * th) * scale * (1.0 + 0.134145 * x * x)

    if fused:
        gather_gate.over_cores()
        gather_down.over_cores()
        units = [
            Reduce(
                place,
                r.unit_full.at[i],
                r.unit_halves.at[i],
                r.unit_eighths.at[i],
                r.unit_summed.at[i],
            )
            for i in range(T)
        ]

    for i in range(T):
        c = lax.rem(t + i, T)
        if fused:
            if i == 1:
                for gather in (gather_value, gather_gate, gather_down):
                    gather.finish()

            def weight(part):
                return glu_slices[part, i].reshape(D, -1)

            def weight_down():
                return down_slices[i].reshape(-1, D)

        else:

            def weight(part):
                return r.glu[c, part]

            def weight_down():
                return r.down[c]

        @pl.loop(0, R // BLOCK)
        def _(tile):
            rows = block_rows(tile)
            a = act[rows, :]
            value = dot(a, weight(0))
            gate = dot(a, weight(1))
            sigma = 0.5 * jnp.tanh(0.5 * gate) + 0.5
            gated = value * sigma
            h = gated.astype(BF16)
            hidden[rows, :] = h
            d_h = dot_nt(cot_in[rows, :], weight_down())
            d_v = (d_h * sigma).astype(BF16)
            d_g = (d_h * gated * (1.0 - sigma)).astype(BF16)
            d_value[rows, :] = d_v
            d_gate[rows, :] = d_g
            added = dot(h, weight_down())
            d_a = dot_nt(d_v, weight(0)) + dot_nt(d_g, weight(1))
            if i > 0:
                added = added + summed[rows, :]
                d_a = d_a + d_act[rows, :]
            if i < T - 1:
                summed[rows, :] = added
                d_act[rows, :] = d_a
            else:
                out = (tokens_in[rows, :].astype(F32) + added).astype(BF16)
                out = dot(turn[...], out).astype(BF16)
                for run, piece in enumerate(pieces(tile)):
                    result[piece, :] = out[run * SEGMENTS : run * SEGMENTS + SEGMENTS]
                d_m = (d_gelu[rows, :] * d_a).astype(BF16)
                d_mixed[rows, :] = d_m
                adjoint[rows, :] = dot_nt(d_m, w_out[...])

        if fused and i > 0:
            units[i - 1].over_plane()

        GRAD_ROWS = 128
        for k, (left, right) in enumerate(((cot_t, hidden), (act_t, d_value), (act_t, d_gate))):

            @pl.loop(0, D // GRAD_ROWS)
            def _(tile):
                rows = pl.ds(pl.multiple_of(tile * GRAD_ROWS, GRAD_ROWS), GRAD_ROWS)
                g = dot(left[rows, :], right[...]).astype(BF16)
                if fused:
                    full = r.unit_full
                    r.unit_full[i, k, tile] = g.reshape(full.shape[3:])
                elif k == 0:
                    r.grad_down[c, rows, :] = g
                else:
                    r.grad_glu[c, k - 1, rows, :] = g

        if fused:
            units[i].over_cores()
            if i > 0:
                units[i - 1].sum_plane()
                unit_copies = [] if i == 1 else unit_copies
                if i > 1:
                    unit_copies.append(
                        links.send(
                            r.unit_summed.at[i - 1],
                            r.unit_sums.at[i - 2],
                            (s, lax.rem(t + i - 1, T)),
                        )
                    )

    def backward_step(index, carry):
        step = L - 1 - index
        return tuple(
            scan_step(
                carry[group],
                spread(keep_next[rows_of(group, step), :]),
                adjoint[rows_of(group, step), :],
                1.0,
            )
            for group in range(GROUPS)
        )

    finals = segment_rows(lax.fori_loop(0, L, backward_step, none))[::-1]
    seg_masks = [
        clear(first + index * L + 1, first + (index + 1) * L + 1) for index in range(SEGMENTS)
    ][::-1]
    factor_seg = power(lam, L)
    own, _ = fold(zero1, factor_seg, finals, seg_masks, [None] * SEGMENTS)
    exchange = Exchange(own, lam, r.adj_tp, r.adj_seq, False)
    if fused:
        units[T - 1].over_plane()
    exchange.over_seq()

    grad_out = r.grad_out_full if fused else r.grad_out

    @pl.loop(0, 2 * N // 128)
    def _(tile):
        rows = pl.ds(pl.multiple_of(tile * 128, 128), 128)
        grad_out[rows, :] = dot(state_t[rows, :], d_mixed[...]).astype(BF16)

    if fused:
        out_full = r.out_full
        for i in range(T):
            at = lax.rem(t + i, T) * n
            for part in range(2):
                rows = pl.ds(pl.multiple_of(part * N + at, n), n)
                out_full[i, part * (S // 4) : (part + 1) * (S // 4)] = grad_out[rows, :].reshape(
                    S // 4, 2, -1, D
                )
        out_reduce = Reduce(place, out_full, r.out_halves, r.out_eighths, r.out_summed)
        out_reduce.over_cores()

    carry = exchange.carry()
    _, entering = fold(carry, factor_seg, finals, seg_masks, [None] * SEGMENTS)
    entering = entering[::-1]
    groups = tuple(
        tuple(
            jnp.concatenate([entering[group * 8 + sub][part] for sub in range(8)], 0)
            for part in range(2)
        )
        for group in range(GROUPS)
    )
    sums[...] = jnp.zeros_like(sums)

    def adjoint_step(step, carry, previous):
        new = []
        add_re = zero8
        add_im = zero8
        add_gamma = zero8
        for group in range(GROUPS):
            rows = rows_of(group, step)
            b = scan_step(carry[group], spread(keep_next[rows, :]), adjoint[rows, :], 1.0)
            new.append(b)
            adjoint[rows, :] = jnp.concatenate(b, 1)
            u = unpack(proj[rows, :])
            v = previous(group, step)
            mask = spread(keep[rows, :])
            add_re = add_re + mask * (b[0] * v[0] + b[1] * v[1])
            add_im = add_im + mask * (b[0] * v[1] - b[1] * v[0])
            add_gamma = add_gamma + b[0] * u[0] + b[1] * u[1]
        return tuple(new), (add_re, add_im, add_gamma)

    def adjoint_body(index, carry):
        values, totals = carry
        values, added = adjoint_step(
            L - 1 - index, values, lambda group, step: unpack(state[rows_of(group, step - 1), :])
        )
        return values, tuple(total + add for total, add in zip(totals, added))

    values, totals = lax.fori_loop(0, L - 1, adjoint_body, (groups, (zero8, zero8, zero8)))
    inside = entering_groups()
    _, added = adjoint_step(0, values, lambda group, step: inside[group])
    totals = [jnp.sum(total + add, 0, keepdims=True) for total, add in zip(totals, added)]

    if fused:
        out_reduce.over_plane()
        units[T - 1].sum_plane()
        unit_copies.append(
            links.send(
                r.unit_summed.at[T - 1], r.unit_sums.at[T - 2], (s, lax.rem(t + T - 1, T))
            )
        )

    @pl.loop(0, R // BLOCK)
    def _(tile):
        rows = block_rows(tile)
        d_proj[rows, :] = (adjoint[rows, :] * gamma_signed).astype(BF16)

    grad_in = r.grad_in_full if fused else r.grad_in

    @pl.loop(0, D // 128)
    def _(tile):
        rows = pl.ds(pl.multiple_of(tile * 128, 128), 128)
        grad_in[rows, :] = dot(normed_t[rows, :], d_proj[...]).astype(grad_in.dtype)

    if fused:
        in_full = r.in_full
        for k in range(T // 2):
            re = grad_in[:, k * 128 : k * 128 + 128]
            im = grad_in[:, N + k * 128 : N + k * 128 + 128]
            even = jnp.where(half, re, pltpu.roll(im, 64, 1))
            odd = jnp.where(half, pltpu.roll(re, 64, 1), im)
            for part, value in enumerate((even, odd)):
                in_full[lax.rem(2 * k + part + T - t, T)] = value.astype(BF16).reshape(
                    in_full.shape[1:]
                )
        in_reduce = Reduce(place, in_full, r.in_halves, r.in_eighths, r.in_summed)
        in_reduce.over_cores()
        out_reduce.sum_plane()
        out_copies = [
            links.send(r.out_summed.at[i], r.out_sums.at[i - 1], (s, lax.rem(t + i, T)))
            for i in range(1, T)
        ]
        in_reduce.over_plane()

    @pl.loop(0, R // BLOCK)
    def _(tile):
        rows = block_rows(tile)
        d_m = d_mixed[rows, :].astype(F32)
        d_n = dot_nt(d_proj[rows, :], w_in[...]) + d_m * skip_row
        c = centred[rows, :]
        sums[0:8, :] += jnp.sum((d_n * c).reshape(BLOCK // 8, 8, D), 0)
        sums[8:16, :] += jnp.sum((d_m * normed[rows, :].astype(F32)).reshape(BLOCK // 8, 8, D), 0)
        d_c = d_n * gain_row
        mean = jnp.mean(d_c, 1, keepdims=True)
        cross = jnp.mean(d_c * c, 1, keepdims=True)
        inv = inv_std[rows, 0:1]
        out = cot_in[rows, :].astype(F32) + inv * (d_c - mean - c * cross)
        high = out.astype(BF16)
        out = dot(turn[...], high) + dot(turn[...], (out - high.astype(F32)).astype(BF16))
        for run, piece in enumerate(pieces(tile)):
            grad_tokens[piece, :] = out[run * SEGMENTS : run * SEGMENTS + SEGMENTS]

    small_rows = [
        jnp.sum(sums[0:8, :], 0, keepdims=True),
        jnp.sum(sums[8:16, :], 0, keepdims=True),
        jnp.concatenate(totals[:2], 1),
        jnp.concatenate([totals[2] / gamma, jnp.zeros_like(gamma)], 1),
    ]
    if not fused:
        for k, row in enumerate(small_rows):
            small[k : k + 1, :] = row
        small[4:8, :] = jnp.zeros((4, D), F32)
        links.close()
        return

    small_tp, small_seq = (r.small_tp, r.small_seq)
    small_tp[t] = jnp.concatenate([packed(row, D // 128) for row in small_rows], 0)
    small_copies = [links.send(small_tp.at[t], small_tp.at[t], (s, peer)) for peer in peers_tp]

    def total_of(own, buffer):
        total = own.astype(F32)
        for k in range(buffer.shape[0]):
            total = total + buffer[k].astype(F32)
        return total.astype(BF16)

    unit_sum = r.unit_sum
    arrive(unit_copies)
    unit_sum[:, place.chip, place.core] = total_of(r.unit_summed[0], r.unit_sums)
    unit_spread = Spread(place, unit_sum)
    unit_spread.over_plane()

    in_reduce.sum_plane()
    in_copies = [
        links.send(r.in_summed.at[i], r.in_sums.at[i - 1], (s, lax.rem(t + i, T)))
        for i in range(1, T)
    ]
    out_sum, in_sum = (r.out_sum, r.in_sum)
    arrive(out_copies)
    out_sum[0, place.chip, place.core] = total_of(r.out_summed[0], r.out_sums)
    out_spread = Spread(place, out_sum)
    out_spread.over_plane()

    arrive(small_copies)
    part = small_tp[0]
    for z in range(1, T):
        part = part + small_tp[z]
    small_seq[s] = part
    small_copies = [links.send(small_seq.at[s], small_seq.at[s], (peer, t)) for peer in peers_seq]

    unit_spread.over_cores()
    arrive(in_copies)
    in_sum[0, place.chip, place.core] = total_of(r.in_summed[0], r.in_sums)
    in_spread = Spread(place, in_sum)
    in_spread.over_plane()
    out_spread.over_cores()

    unit_spread.finish()
    for k in range(2):
        r.grad_glu[k] = unit_sum[k + 1].reshape(D, -1).astype(F32)
    width = r.grad_down.shape[0]
    row = lax.broadcasted_iota(jnp.int32, (width, width), 0)
    column = lax.broadcasted_iota(jnp.int32, (width, width), 1)
    unit = jnp.where(row == column, 1.0, 0.0).astype(BF16)
    r.grad_down[...] = dot_nt(unit, unit_sum[0].reshape(D, -1))

    arrive(small_copies)
    part = small_seq[0]
    for block in range(1, S):
        part = part + small_seq[block]
    for k in range(4):
        height = D // 128
        small[k : k + 1, :] = unpacked(part[k * height : (k + 1) * height], height)
    small[4:8, :] = jnp.zeros((4, D), F32)

    out_spread.finish()
    r.grad_out[...] = out_sum[0].reshape(2, n, D).astype(F32)
    in_spread.over_cores()
    in_spread.finish()
    value = in_sum[0].reshape(D, 128).astype(F32)
    r.grad_in[0] = value[:, :n]
    r.grad_in[1] = pltpu.roll(value, 64, 1)[:, :n]
    links.close()


def decay_terms(decay_log, angle):
    rate_step = jnp.exp(decay_log)
    radius = jnp.exp(-rate_step)
    return (
        radius * jnp.cos(angle),
        radius * jnp.sin(angle),
        jnp.sqrt(-jnp.expm1(-2.0 * rate_step)),
    )


def local(
    S,
    T,
    tokens,
    ln_gain,
    in_proj,
    decay_log,
    angle,
    out_proj,
    skip,
    glu_proj,
    down_proj,
    lengths,
    cotangent,
):
    R, D = tokens.shape
    n = in_proj.shape[2]
    N = n * T
    units = down_proj.shape[0]
    C = S // 2
    fused = (
        S % 4 == 0
        and T % 2 == 0
        and 2 * n == 128
        and units % 128 == 0
        and all(size % (16 * S) == 0 for size in (D, 2 * n, units))
        and (2 * C) * 64 == D
    )
    vmem = pl.BlockSpec(memory_space=pltpu.VMEM)
    anywhere = pl.BlockSpec(memory_space=pl.ANY)
    lam_re, lam_im, gamma = decay_terms(decay_log, angle)
    ins = dict(
        lengths=(lengths, pl.BlockSpec(memory_space=pltpu.SMEM)),
        tokens=(tokens, vmem),
        cot=(cotangent, vmem),
        gain=(ln_gain.reshape(1, D), vmem),
        skip=(skip.reshape(1, D), vmem),
    )
    outs = dict(
        result=((R, D), BF16),
        grad_tokens=((R, D), F32),
        small=((8, D), F32),
    )
    scratch = dict(
        turn=((BLOCK, BLOCK), BF16),
        tokens_in=((R, D), BF16),
        cot_in=((R, D), BF16),
        centred=((R, D), F32),
        inv_std=((R, 128), F32),
        normed=((R, D), BF16),
        normed_t=((D, R), BF16),
        cot_t=((D, R), BF16),
        proj=((R, 2 * N), F32),
        keep=((R, 128), F32),
        keep_next=((R, 128), F32),
        state=((R, 2 * N), F32),
        state_t=((2 * N, R), BF16),
        act=((R, D), BF16),
        act_t=((D, R), BF16),
        d_gelu=((R, D), F32),
        d_act=((R, D), F32),
        summed=((R, D), F32),
        d_mixed=((R, D), BF16),
        adjoint=((R, 2 * N), F32),
        d_proj=((R, 2 * N), BF16),
        hidden=((R, units), BF16),
        d_value=((R, units), BF16),
        d_gate=((R, units), BF16),
        seg_carry=((SEGMENTS, 2 * N), F32),
        sums=((16, D), F32),
        state_tp=((T, 8, 128), F32),
        state_seq=((S, 8, 128), F32),
        adj_tp=((T, 8, 128), F32),
        adj_seq=((S, 8, 128), F32),
    )
    if fused:
        rates = jnp.stack(
            [jnp.concatenate([lam_re, lam_im]), jnp.concatenate([gamma, gamma])]
            + [jnp.zeros((2 * n,), F32)] * 6
        )
        ins.update(
            rates=(rates, vmem),
            in_proj=(in_proj, vmem),
            out_proj=(out_proj.reshape(C, 2, 2 * n // S, D), anywhere),
            glu_proj=(glu_proj.reshape(2, C, 2, D // S, units), anywhere),
            down_proj=(down_proj.reshape(C, 2, units // S, D), anywhere),
        )
        outs.update(
            grad_in=((2, D, n), F32),
            grad_out=((2, n, D), F32),
            grad_glu=((2, D, units), F32),
            grad_down=((units, D), F32),
        )

        def whole(parts, rows, lanes, lead=()):
            return (lead + (parts, C, 2, rows, lanes), BF16)

        def halves(parts, rows, lanes, lead=()):
            return (lead + (parts, C, rows, lanes), BF16)

        def eighths(parts, rows, lanes, lead=()):
            return (lead + (C - 1, parts, rows, lanes), BF16)

        def own(parts, rows, lanes, lead=()):
            return (lead + (parts, rows, lanes), BF16)

        unit_sizes = (3, D // S, units, (T,))
        out_sizes = (T, 2 * n // S, D)
        in_sizes = (T, D // S, 2 * n)
        scratch.update(
            w_in=((D, 2 * N), BF16),
            w_out=((2 * N, D), BF16),
            rates_all=((T, 8, 128), F32),
            in_slices=((T, C, 2, D // S, 2 * n), BF16),
            out_slices=((T, C, 2, 2 * n // S, D), BF16),
            glu_slices=((2, T, C, 2, D // S, units), BF16),
            down_slices=((T, C, 2, units // S, D), BF16),
            grad_out_full=((2 * N, D), BF16),
            grad_in_full=((D, 2 * N), F32),
            small_tp=((T, 16, 128), F32),
            small_seq=((S, 16, 128), F32),
            unit_sums=((T - 1, 3, D // S, units), BF16),
            out_sums=((T - 1, 2 * n // S, D), BF16),
            in_sums=((T - 1, D // S, 2 * n), BF16),
            unit_sum=((3, C, 2, D // S, units), BF16),
            out_sum=((1, C, 2, 2 * n // S, D), BF16),
            in_sum=((1, C, 2, D // S, 2 * n), BF16),
        )
        scratch.update(
            unit_full=whole(*unit_sizes),
            unit_halves=halves(*unit_sizes),
            unit_eighths=eighths(*unit_sizes),
            unit_summed=own(*unit_sizes),
            out_full=whole(*out_sizes),
            out_halves=halves(*out_sizes),
            out_eighths=eighths(*out_sizes),
            out_summed=own(*out_sizes),
            in_full=whole(*in_sizes),
            in_halves=halves(*in_sizes),
            in_eighths=eighths(*in_sizes),
            in_summed=own(*in_sizes),
        )
        links = 160
    else:
        w_in = lax.all_gather(in_proj, "tp", axis=2, tiled=True)
        w_out = lax.all_gather(out_proj, "tp", axis=1, tiled=True).reshape(2 * N, D)
        lam_re, lam_im, gamma = (
            lax.all_gather(part, "tp", tiled=True) for part in (lam_re, lam_im, gamma)
        )
        rates = jnp.stack(
            [jnp.concatenate([lam_re, lam_im]), jnp.concatenate([gamma, gamma])]
            + [jnp.zeros((2 * N,), F32)] * 6
        )
        ins.update(
            rates=(rates, vmem),
            w_in=(jnp.concatenate([w_in[0], w_in[1]], 1), vmem),
            w_out=(w_out, vmem),
            glu=(lax.all_gather(glu_proj, "tp"), vmem),
            down=(lax.all_gather(down_proj, "tp"), vmem),
        )
        outs.update(
            grad_in=((D, 2 * N), BF16),
            grad_out=((2 * N, D), BF16),
            grad_glu=((T, 2, D, units), BF16),
            grad_down=((T, D, units), BF16),
        )
        links = 2 * (T - 1 + S - 1)
    names = [*ins, *outs, *scratch, *dict(local_sem=0, send_sem=0, recv_sem=0)]
    result, grad_tokens, small, grad_in, grad_out, grad_glu, grad_down = pl.pallas_call(
        functools.partial(layer_kernel, S, T, fused, names),
        out_shape=tuple(jax.ShapeDtypeStruct(shape, dtype) for shape, dtype in outs.values()),
        in_specs=[spec for _, spec in ins.values()],
        out_specs=(vmem,) * len(outs),
        scratch_shapes=[pltpu.VMEM(shape, dtype) for shape, dtype in scratch.values()]
        + [
            pltpu.SemaphoreType.DMA((4,)),
            pltpu.SemaphoreType.DMA((links,)),
            pltpu.SemaphoreType.DMA((links,)),
        ],
        compiler_params=pltpu.CompilerParams(
            collective_id=0, has_side_effects=True, vmem_limit_bytes=60 * 2**20
        ),
    )(*[value for value, _ in ins.values()])
    t = lax.axis_index("tp")
    if not fused:
        small = lax.psum(small, ("seq", "tp"))

        def reduced(part):
            part = lax.psum_scatter(part, "tp", scatter_dimension=0, tiled=True)
            return lax.psum(part, "seq").astype(F32)

        grad_in = grad_in.reshape(D, 2, T, n).transpose(2, 1, 0, 3).reshape(T * 2, D, n)
        grad_in = reduced(grad_in)
        grad_out = grad_out.reshape(2, T, n, D).transpose(1, 0, 2, 3).reshape(T * 2, n, D)
        grad_out = reduced(grad_out)
        grad_glu = reduced(grad_glu.reshape(T * 2, D, units))
        grad_down = reduced(grad_down)[0].T

    def mine(row):
        return lax.dynamic_slice_in_dim(row, t * n, n)

    g_re, g_im, g_gamma = (mine(small[2, :N]), mine(small[2, N:]), mine(small[3, :N]))
    _, pull = jax.vjp(decay_terms, decay_log, angle)
    grad_decay, grad_angle = pull((g_re, g_im, g_gamma))
    return (
        result,
        grad_tokens,
        small[0],
        grad_in,
        grad_decay,
        grad_angle,
        grad_out,
        small[1],
        grad_glu,
        grad_down,
    )


def solution(mesh):
    in_specs = (
        P(("seq", "tp"), None),
        P(),
        P(None, None, "tp"),
        P("tp"),
        P("tp"),
        P(None, "tp", None),
        P(),
        P(None, None, "tp"),
        P("tp", None),
        P(),
        P(("seq", "tp"), None),
    )
    out_specs = (
        P(("seq", "tp"), None),
        P(("seq", "tp"), None),
        P(),
        P(None, None, "tp"),
        P("tp"),
        P("tp"),
        P(None, "tp", None),
        P(),
        P(None, None, "tp"),
        P("tp", None),
    )
    return jax.shard_map(
        functools.partial(local, mesh.shape["seq"], mesh.shape["tp"]),
        mesh=mesh,
        in_specs=in_specs,
        out_specs=out_specs,
        check_vma=False,
    )
```

time: 357 us -> 120 us (0.34)
  waiting for transfers between devices: 171 us -> 0 us
  blocking collectives: 79.2 us -> 0 us
  Pallas kernels: 71.5 us -> 103 us
  between operations: 15 us -> 0.69 us
  other arithmetic: 5.75 us -> 2.02 us
    reduce_scatter x4 -> x0, waiting for transfers between devices: 73.9 us -> none  [reduced(): part = lax.psum_scatter(part, 'tp', scatter_dimension=0, tiled=True)]
    psum x1 -> x0, waiting for transfers between devices: 57.7 us -> none  [reduced(): return lax.psum(part, 'seq').astype(F32)]
    psum x1 -> x0, blocking collectives: 38.7 us -> none  [local(): small = lax.psum(small, ('seq', 'tp'))]
    all_gather x2 -> x0, waiting for transfers between devices: 37 us -> none  [the longest x1 37 us: local(): glu = lax.all_gather(glu_proj, 'tp')]
    pallas_call x1, Pallas kernels: 71.5 us -> 103 us  [local(): pl.pallas_call(functools.partial(layer_kernel, S, T, fused, names), out_s...]
    all_gather x2 -> x0, blocking collectives: 30.2 us -> none  [the longest x1 16.6 us: local(): w_in = lax.all_gather(in_proj, 'tp', axis=2, tiled=True)]
    unnamed x1 -> x0, blocking collectives: 10.2 us -> none
    convert_element_type x3 -> x0, other arithmetic: 3.59 us -> none  [reduced(): return lax.psum(part, 'seq').astype(F32)]
  transfers between devices with their start and end apart: 7 -> 0, of which waited for: 4 -> 0; matrix products, arithmetic and copies ran while one was open for 2% -> 0% of each run, Pallas kernels for 0% -> 0%
where the time goes in v2:
time: 120 us
  Pallas kernels  103 us (86%)
  local copies, waits for them, and re-layouts  14.1 us (12%)
  other arithmetic  2.02 us (2%)
    pallas_call x1, Pallas kernels, local(): pl.pallas_call(functools.partial(layer_kernel, S, T, fused, names), out_s...  103 us
    unnamed x17, local copies, waits for them, and re-layouts  9.77 us

profile of v2, /device:TPU:1, one launch (start us, length us, event | category | flops | bytes accessed | tf_op | source)
XLA Modules:
  0.0 119.6 jit_solution(13027810779246662342)
XLA Ops:
  0.6 0.0 copy-start.4
  0.7 0.1 pad.3.clone
  0.7 0.1 pad.2.clone
  0.8 0.7 fusion.7
  1.5 0.7 fusion.4
  2.2 0.1 maximum_bitcast_fusion
  2.3 0.7 maximum_maximum_fusion.refs_5_
  2.9 1.3 %reshape.39.refs_4_ = bf16[1,512]{1,0:T(2,128)(2,1)} reshape(bf16[512]{0:T(512)(128)(2,1)} %param.17) | data formatting | bytes 2048 | tf_op jit(solution)/shard_map/reshape | solution.py:915
  4.2 1.7 %copy.21.refs_6_ = bf16[2,512,64]{2,1,0:T(8,128)(2,1)} copy(bf16[2,512,64]{1,2,0:T(8,128)(2,1)} %param.13) | data formatting | bytes 262144 | tf_op args[2]
  6.0 102.7 %shard_map.186 = (bf16[1024,512]{1,0:T(8,128)(2,1)}, f32[1024,512]{1,0:T(8,128)}, f32[8,512]{1,0:T(8,128)}, f32[2,512,64]{2,1,0:T(8,128)}, f32[2,64,512]{2,1,0:T...) custom-call(s32[6]{0:T(128)} %refs_0_.1, bf16[1024,512]{1,0:T(8,128)(2,1)} %refs_1_.1, bf16[1024,512]{1,0:T(8,128)(2,1)} %refs_2_.1, ...), custom_call_target="tpu_custom_call" | custom-call | tf_op jit(solution)/shard_map/pallas_call | solution.py:1047
  108.7 0.0 copy-start
  108.7 0.9 fusion.6
  109.6 1.4 %fusion.5 = (f32[1,512]{1,0:T(1,128)}, f32[1,512]{1,0:T(1,128)}) fusion(f32[8,512]{1,0:T(8,128)} %get-tuple-element.19), kind=kLoop, calls=%fused_computation.16 | loop fusion | bytes 8192 | tf_op jit(solution)/shard_map/slice | solution.py:1091
  110.9 0.0 copy-done.4
  110.9 0.6 multiply_add_fusion
  111.5 1.9 %copy.22 = f32[2,512,64]{1,2,0:T(8,128)} copy(f32[2,512,64]{2,1,0:T(8,128)} %get-tuple-element.27) | data formatting | bytes 524288
  113.5 2.3 %copy.28 = bf16[1024,512]{1,0:T(8,128)(2,1)} copy(bf16[1024,512]{1,0:T(8,128)(2,1)} %get-tuple-element.58) | data formatting | bytes 2097152
  115.7 0.0 copy-done
  115.7 0.0 copy-start.3
  115.7 0.0 copy-start.1
  115.7 1.3 %copy.29 = f32[1024,512]{1,0:T(8,128)} copy(f32[1024,512]{1,0:T(8,128)S(1)} %copy-done) | data formatting | bytes 4194304
  117.0 0.0 copy-done.3
  117.1 0.0 copy-start.2
  117.1 0.7 copy.30
  117.8 0.0 copy-done.1
  117.8 1.0 copy.31
  118.8 0.0 copy-done.2
  118.8 0.8 copy.32
  (2 shorter events, 0.0 us)
Async XLA Ops:
  0.6 110.3 %copy-start.4 = (f32[64]{0:T(128)S(1)}, f32[64]{0:T(128)}, u32[]{:S(2)}) copy-start(f32[64]{0:T(128)} %param.14) | copy-start | bytes 772
  108.7 7.1 %copy-start = (f32[1024,512]{1,0:T(8,128)S(1)}, f32[1024,512]{1,0:T(8,128)}, u32[]{:S(2)}) copy-start(f32[1024,512]{1,0:T(8,128)} %get-tuple-element.59) | copy-start | bytes 6291460
  115.7 1.3 %copy-start.3 = (f32[2,64,512]{2,1,0:T(8,128)S(1)}, f32[2,64,512]{2,1,0:T(8,128)}, u32[]{:S(2)}) copy-start(f32[2,64,512]{2,1,0:T(8,128)} %get-tuple-element.64) | copy-start | bytes 786436
  115.7 2.1 %copy-start.1 = (f32[2,512,256]{2,1,0:T(8,128)S(1)}, f32[2,512,256]{2,1,0:T(8,128)}, u32[]{:S(2)}) copy-start(f32[2,512,256]{2,1,0:T(8,128)} %get-tuple-element.66) | copy-start | bytes 3145732
  117.1 1.7 %copy-start.2 = (f32[256,512]{1,0:T(8,128)S(1)}, f32[256,512]{1,0:T(8,128)}, u32[]{:S(2)}) copy-start(f32[256,512]{1,0:T(8,128)} %get-tuple-element.67) | copy-start | bytes 1572868

commit v3 on v2

--- a/solution.py
+++ b/solution.py
@@ -26,6 +26,10 @@
 
 def complex_mul(left_re, left_im, right_re, right_im):
     return (left_re * right_re - left_im * right_im, left_re * right_im + left_im * right_re)
+
+
+def dot_tn(left, right):
+    return lax.dot_general(left, right, (((0,), (0,)), ((), ())), preferred_element_type=F32)
 
 
 def power(base, exponent):
@@ -71,31 +75,33 @@
 
 
 class Gather:
-    def __init__(self, place, buffer):
+    def __init__(self, place, buffer, first, last):
         self.place = place
         self.buffer = buffer
+        self.slots = range(first, last)
+        self.part = buffer.at[pl.ds(first, last - first)]
 
     def over_tp(self):
         p = self.place
         self.copies = [
             p.links.send(
                 self.buffer.at[0, p.chip, p.core],
-                self.buffer.at[p.T - k, p.chip, p.core],
-                (p.s, lax.rem(p.t + k, p.T)),
+                self.buffer.at[slot, p.chip, p.core],
+                (p.s, lax.rem(p.t + p.T - slot, p.T)),
             )
-            for k in range(1, p.T)
+            for slot in self.slots
         ]
 
     def over_plane(self):
         p = self.place
         arrive(self.copies)
-        mine = self.buffer.at[pl.ds(1, p.T - 1), p.chip, p.core]
+        mine = self.part.at[:, p.chip, p.core]
         self.copies = [p.links.send(mine, mine, device) for _, device in p.chips]
 
     def over_cores(self):
         p = self.place
         arrive(self.copies)
-        mine = self.buffer.at[pl.ds(1, p.T - 1), :, p.core]
+        mine = self.part.at[:, :, p.core]
         self.copies = [p.links.send(mine, mine, p.sibling)]
 
     def finish(self):
@@ -143,6 +149,60 @@
             for k in range(len(p.chips)):
                 total = total + self.eighths[k, part].astype(F32)
             self.summed[part] = total.astype(BF16)
+
+
+class Reduce2(Reduce):
+    def __init__(self, place, full, halves, eighths, summed):
+        super().__init__(place, full, halves, eighths, summed)
+        self.rows = halves.shape[2] // 2
+        self.ours = halves.at[:, :, pl.ds(0, self.rows)]
+        self.theirs = halves.at[:, :, pl.ds(self.rows, self.rows)]
+
+    def sum_cores(self, chip):
+        self.halves[0, chip] = (
+            self.full[0, chip, self.place.core].astype(F32) + self.halves[0, chip].astype(F32)
+        ).astype(BF16)
+
+    def over_plane(self):
+        p = self.place
+        arrive(self.copies)
+        self.sum_cores(p.by_x)
+        self.sum_cores(p.by_y)
+        self.sum_cores(p.by_xy)
+        self.copies = [
+            p.links.send(part.at[0, chip], self.eighths.at[index, 0, rows], device)
+            for index, part, chip, rows, device in (
+                (0, self.ours, p.by_x, pl.ds(0, self.rows), p.x_device),
+                (1, self.ours, p.by_xy, pl.ds(0, self.rows), p.x_device),
+                (0, self.theirs, p.by_y, pl.ds(self.rows, self.rows), p.y_device),
+                (1, self.theirs, p.by_xy, pl.ds(self.rows, self.rows), p.y_device),
+            )
+        ]
+        self.sum_cores(p.chip)
+
+    def turn_plane(self):
+        p = self.place
+        arrive(self.copies)
+        n = self.rows
+        for index, chip in ((0, p.chip), (1, p.by_y)):
+            self.halves[0, chip, 0:n] = (
+                self.halves[0, chip, 0:n].astype(F32) + self.eighths[index, 0, 0:n].astype(F32)
+            ).astype(BF16)
+        for index, chip in ((0, p.chip), (1, p.by_x)):
+            self.halves[0, chip, n:] = (
+                self.halves[0, chip, n:].astype(F32) + self.eighths[index, 0, n:].astype(F32)
+            ).astype(BF16)
+        self.copies = [
+            p.links.send(self.ours.at[0, p.by_y], self.eighths.at[2, 0, pl.ds(0, n)], p.y_device),
+            p.links.send(self.theirs.at[0, p.by_x], self.eighths.at[2, 0, pl.ds(n, n)], p.x_device),
+        ]
+
+    def sum_plane(self):
+        p = self.place
+        arrive(self.copies)
+        self.summed[0] = (
+            self.halves[0, p.chip].astype(F32) + self.eighths[2, 0].astype(F32)
+        ).astype(BF16)
 
 
 class Spread:
@@ -174,6 +234,13 @@
         self.core = lax.rem(self.s, 2)
         self.chip = lax.div(self.s, 2)
         self.sibling = (self.chip * 2 + 1 - self.core, self.t)
+        x = lax.rem(self.chip, 2)
+        y = lax.div(self.chip, 2)
+        self.by_x = y * 2 + 1 - x
+        self.by_y = (1 - y) * 2 + x
+        self.by_xy = (1 - y) * 2 + 1 - x
+        self.x_device = (self.by_x * 2 + self.core, self.t)
+        self.y_device = (self.by_y * 2 + self.core, self.t)
         self.chips = []
         for k in range(1, C):
             chip = lax.rem(self.chip + k, C)
@@ -185,26 +252,22 @@
     links = Links(r.send_sem, r.recv_sem)
     place = Place(S, T, links)
     lengths = r.lengths
-    tokens = r.tokens
-    cot = r.cot
-    gain = r.gain
-    skip = r.skip
-    result, grad_tokens, small = (r.result, r.grad_tokens, r.small)
+    tokens = r.tokens_raw
+    cot = r.cot_raw
+    result = r.result_rows
+    grad_tokens = r.grad_rows
     turn = r.turn
     tokens_in = r.tokens_in
     cot_in = r.cot_in
     centred = r.centred
     inv_std = r.inv_std
     normed = r.normed
-    normed_t = r.normed_t
-    cot_t = r.cot_t
     proj = r.proj
     keep = r.keep
     keep_next = r.keep_next
     state = r.state
-    state_t = r.state_t
+    state_low = r.state_low
     act = r.act
-    act_t = r.act_t
     d_gelu = r.d_gelu
     d_act = r.d_act
     summed = r.summed
@@ -212,12 +275,11 @@
     adjoint = r.adjoint
     d_proj = r.d_proj
     hidden = r.hidden
-    d_value = r.d_value
-    d_gate = r.d_gate
+    d_unit = r.d_unit
     seg_carry, sums = (r.seg_carry, r.sums)
     w_in, w_out = (r.w_in, r.w_out)
     R, D = tokens.shape
-    N = w_in.shape[1] // 2
+    N = w_in.shape[0] // 2
     n = N // T
     L = R // SEGMENTS
     s = place.s
@@ -232,37 +294,48 @@
     for peer in peers_seq:
         pl.semaphore_signal(barrier, inc=1, device_id=(peer, t), device_id_type=MESH)
 
-    lane = lax.broadcasted_iota(jnp.int32, (D, 128), 1)
+    fetched = [
+        pltpu.make_async_copy(source, target, r.local_sem.at[index])
+        for index, (source, target) in enumerate(((r.tokens, tokens), (r.cot, cot)))
+    ]
     if fused:
-        in_slices, out_slices = (r.in_slices, r.out_slices)
-        glu_slices, down_slices = (r.glu_slices, r.down_slices)
-        local_copies = [
-            pltpu.make_async_copy(r.out_proj, out_slices.at[0], r.local_sem.at[0]),
-            pltpu.make_async_copy(r.glu_proj.at[0], glu_slices.at[0, 0], r.local_sem.at[1]),
-            pltpu.make_async_copy(r.glu_proj.at[1], glu_slices.at[1, 0], r.local_sem.at[2]),
-            pltpu.make_async_copy(r.down_proj, down_slices.at[0], r.local_sem.at[3]),
+        in_slices, out_slices, unit_slices = (r.in_slices, r.out_slices, r.unit_slices)
+        units = r.down_proj.shape[2] * S
+        D_rows = r.glu_proj.shape[3]
+        gated_rows = unit_slices.at[0, :, :, pl.ds(0, D_rows)]
+        weights = [
+            pltpu.make_async_copy(source, target, r.local_sem.at[2 + index])
+            for index, (source, target) in enumerate(
+                (
+                    (r.in_proj, in_slices.at[0]),
+                    (r.out_proj, out_slices.at[0]),
+                    (r.glu_proj.at[0], gated_rows.at[:, :, :, pl.ds(0, units)]),
+                    (r.glu_proj.at[1], gated_rows.at[:, :, :, pl.ds(units, units)]),
+                    (r.down_proj, unit_slices.at[0, :, :, pl.ds(D_rows, units // S)]),
+                )
+            )
         ]
-        for copy in local_copies:
+        for copy in weights:
             copy.start()
-        row = lax.broadcasted_iota(jnp.int32, (n, 128), 0)
-        column = lax.broadcasted_iota(jnp.int32, (n, 128), 1)
-        merged = dot(r.in_proj[0], jnp.where(row == column, 1.0, 0.0).astype(BF16)) + dot(
-            r.in_proj[1], jnp.where(row + n == column, 1.0, 0.0).astype(BF16)
-        )
-        in_slices[0] = merged.astype(BF16).reshape(in_slices.shape[1:])
-        r.rates_all[t] = r.rates[...]
-        for copy in local_copies:
+    for copy in fetched:
+        copy.start()
+    if fused:
+        rates_all = r.rates_all
+        rates_all[t] = jnp.zeros(rates_all.shape[1:], F32)
+        for index, row in enumerate(decay_terms(r.decay_log[...], r.angle[...])):
+            rates_all[t, index : index + 1, 0:n] = row
+        gather_in = Gather(place, in_slices, 1, T)
+        gather_out = Gather(place, out_slices, 1, T)
+        gather_units = [Gather(place, unit_slices, slot, slot + 1) for slot in range(1, T)]
+        for copy in weights:
             copy.wait()
-        gather_in = Gather(place, in_slices)
-        gather_out = Gather(place, out_slices)
-        gather_value = Gather(place, glu_slices.at[0])
-        gather_gate = Gather(place, glu_slices.at[1])
-        gather_down = Gather(place, down_slices)
         pl.semaphore_wait(barrier, T - 1 + S - 1)
+        gather_in.over_tp()
         rate_copies = [
-            links.send(r.rates_all.at[t], r.rates_all.at[t], (s, peer)) for peer in peers_tp
+            links.send(rates_all.at[t], rates_all.at[t], (s, peer)) for peer in peers_tp
         ]
-        for gather in (gather_in, gather_out, gather_value, gather_gate, gather_down):
+        gather_out.over_tp()
+        for gather in gather_units:
             gather.over_tp()
 
     starts = []
@@ -283,8 +356,8 @@
             hit = hit | ((start >= low) & (start < high))
         return jnp.where(hit, 0.0, 1.0)
 
-    gain_row = gain[...]
-    skip_row = skip[...].astype(F32)
+    gain_row = r.gain[...]
+    skip_row = r.skip[...].astype(F32)
 
     down_index = lax.broadcasted_iota(jnp.int32, (BLOCK, BLOCK), 0)
     across_index = lax.broadcasted_iota(jnp.int32, (BLOCK, BLOCK), 1)
@@ -314,68 +387,56 @@
         inv_std[rows, :] = jnp.broadcast_to(inv, (BLOCK, 128))
         n_rows = (c * gain_row).astype(BF16)
         normed[rows, :] = n_rows
-        normed_t[:, rows] = n_rows.T
 
     def cot_tile(tile):
         rows = block_rows(tile)
         cot_rows = taken(cot, tile).astype(BF16)
         cot_in[rows, :] = cot_rows
-        cot_t[:, rows] = cot_rows.T
         index = tile * BLOCK + lax.broadcasted_iota(jnp.int32, (BLOCK, 128), 0)
         position = first + lax.rem(index, SEGMENTS) * L + lax.div(index, SEGMENTS)
         keep[rows, :] = keeps(position)
         keep_next[rows, :] = keeps(position + 1)
 
+    fetched[0].wait()
     pl.loop(0, R // BLOCK)(norm_tile)
     if fused:
         gather_in.over_plane()
         gather_out.over_plane()
+    fetched[1].wait()
     pl.loop(0, R // BLOCK)(cot_tile)
+
+    def assemble(slices, weight):
+        for i in range(T):
+            at = lax.rem(t + i, T) * n
+            for part in range(2):
+                weight[pl.ds(pl.multiple_of(part * N + at, n), n), :] = slices[
+                    i, part * (S // 4) : (part + 1) * (S // 4)
+                ].reshape(n, D)
+
     if fused:
         gather_in.over_cores()
-        gather_out.over_cores()
         arrive(rate_copies)
-        gather_value.over_plane()
+        half = lax.broadcasted_iota(jnp.int32, (8, 128), 1) < n
+        rate_rows = [rates_all[z] for z in range(T)]
+        joined = jnp.concatenate(
+            [
+                jnp.where(half, rate_rows[z], pltpu.roll(rate_rows[z + 1], n, 1))
+                for z in range(0, T, 2)
+            ],
+            1,
+        )
+        lam_re, lam_im, gamma = (joined[k : k + 1] for k in range(3))
         gather_in.finish()
-        half = lane < 64
-        for k in range(T // 2):
-            even, odd = (
-                in_slices[lax.rem(2 * k + part + T - t, T)].reshape(D, 128).astype(F32)
-                for part in range(2)
-            )
-            at = k * 128
-            w_in[:, at : at + 128] = jnp.where(half, even, pltpu.roll(odd, 64, 1)).astype(BF16)
-            w_in[:, N + at : N + at + 128] = jnp.where(half, pltpu.roll(even, 64, 1), odd).astype(
-                BF16
-            )
-        rate_rows = [r.rates_all[z] for z in range(T)]
-        half8 = lane[:8] < 64
-
-        def joined(rows, part):
-            out = []
-            for k in range(T // 2):
-                even, odd = (rows[2 * k], rows[2 * k + 1])
-                if part == 0:
-                    out.append(jnp.where(half8, even, pltpu.roll(odd, 64, 1)))
-                else:
-                    out.append(jnp.where(half8, pltpu.roll(even, 64, 1), odd))
-            return jnp.concatenate(out, 1)
-
-        lam_gamma = joined(rate_rows, 0)
-        lam_re = lam_gamma[0:1]
-        lam_im = joined(rate_rows, 1)[0:1]
-        gamma = lam_gamma[1:2]
+        assemble(in_slices, w_in)
     else:
         pl.semaphore_wait(barrier, T - 1 + S - 1)
-        lam_re = r.rates[0:1, :N]
-        lam_im = r.rates[0:1, N:]
-        gamma = r.rates[1:2, :N]
+        lam_re, lam_im, gamma = (r.rates[k : k + 1, :] for k in range(3))
     gamma_signed = jnp.concatenate([gamma, -gamma], 1)
 
     @pl.loop(0, R // BLOCK)
     def _(tile):
         rows = block_rows(tile)
-        proj[rows, :] = dot(normed[rows, :], w_in[...]) * gamma_signed
+        proj[rows, :] = dot_nt(normed[rows, :], w_in[...]) * gamma_signed
 
     low8_re = jnp.broadcast_to(lam_re, (8, N))
     low8_im = jnp.broadcast_to(lam_im, (8, N))
@@ -496,17 +557,14 @@
     own, _ = fold(zero1, factor_seg, finals, seg_masks, [None] * SEGMENTS)
     exchange = Exchange(own, conj, r.state_tp, r.state_seq, True)
     if fused:
-        gather_gate.over_plane()
+        gather_out.over_cores()
+        gather_units[0].over_plane()
     exchange.over_seq()
     if fused:
-        gather_down.over_plane()
+        for gather in gather_units[1:]:
+            gather.over_plane()
         gather_out.finish()
-        for i in range(T):
-            at = lax.rem(t + i, T) * n
-            for part in range(2):
-                w_out[pl.ds(pl.multiple_of(part * N + at, n), n), :] = out_slices[
-                    i, part * (S // 4) : (part + 1) * (S // 4)
-                ].reshape(n, D)
+        assemble(out_slices, w_out)
     carry = exchange.carry()
     _, entering = fold(carry, factor_seg, finals, seg_masks, [None] * SEGMENTS)
     for index, (row_re, row_im) in enumerate(entering):
@@ -525,28 +583,22 @@
 
     lax.fori_loop(0, L, write_state, entering_groups())
 
-    if fused:
-        gather_value.over_cores()
-
     @pl.loop(0, R // BLOCK)
     def _(tile):
         rows = block_rows(tile)
         low = state[rows, :].astype(BF16)
-        state_t[:, rows] = low.T
+        state_low[rows, :] = low
         x = dot(low, w_out[...]) + skip_row * normed[rows, :].astype(F32)
         scale = 0.7978845608028654
         th = jnp.tanh(scale * (x + 0.044715 * x * x * x))
         half = 0.5 * (1.0 + th)
         a = (x * half).astype(BF16)
         act[rows, :] = a
-        act_t[:, rows] = a.T
         d_gelu[rows, :] = half + 0.5 * x * (1.0 - th * th) * scale * (1.0 + 0.134145 * x * x)
 
     if fused:
-        gather_gate.over_cores()
-        gather_down.over_cores()
-        units = [
-            Reduce(
+        reduces = [
+            Reduce2(
                 place,
                 r.unit_full.at[i],
                 r.unit_halves.at[i],
@@ -556,44 +608,58 @@
             for i in range(T)
         ]
 
+    UNIT_ROWS = min(512, R)
+    units = hidden.shape[1]
+    unit_copies = []
+
+    def unit_grads(i):
+        c = lax.rem(t + i, T)
+        gated_grad = dot_tn(act[...], d_unit[...]).astype(BF16)
+        down_grad = dot_tn(hidden[...], cot_in[...]).astype(BF16)
+        if fused:
+            full = r.unit_full
+            full[i, 0, :, :, 0:D_rows] = gated_grad.reshape(S // 2, 2, D_rows, 2 * units)
+            full[i, 0, :, :, D_rows:] = down_grad.reshape(S // 2, 2, units // S, D)
+            reduces[i].over_cores()
+        else:
+            r.grad_glu[c] = gated_grad
+            r.grad_down[c] = down_grad
+
+    def unit_sums(i):
+        reduces[i].sum_plane()
+        if i > 0:
+            unit_copies.append(
+                links.send(r.unit_summed.at[i], r.unit_sums.at[i - 1], (s, lax.rem(t + i, T)))
+            )
+
     for i in range(T):
         c = lax.rem(t + i, T)
         if fused:
-            if i == 1:
-                for gather in (gather_value, gather_gate, gather_down):
-                    gather.finish()
-
-            def weight(part):
-                return glu_slices[part, i].reshape(D, -1)
-
-            def weight_down():
-                return down_slices[i].reshape(-1, D)
-
+            if i > 0:
+                gather_units[i - 1].finish()
+            if i < T - 1:
+                gather_units[i].over_cores()
+            w_gated = unit_slices[i, :, :, 0:D_rows].reshape(D, 2 * units)
+            w_down = unit_slices[i, :, :, D_rows:].reshape(units, D)
         else:
-
-            def weight(part):
-                return r.glu[c, part]
-
-            def weight_down():
-                return r.down[c]
-
-        @pl.loop(0, R // BLOCK)
-        def _(tile):
-            rows = block_rows(tile)
-            a = act[rows, :]
-            value = dot(a, weight(0))
-            gate = dot(a, weight(1))
+            w_gated = r.glu[c]
+            w_down = r.down[c]
+
+        for tile in range(R // UNIT_ROWS):
+            rows = slice(tile * UNIT_ROWS, (tile + 1) * UNIT_ROWS)
+            both = dot(act[rows, :], w_gated)
+            value, gate = (both[:, :units], both[:, units:])
             sigma = 0.5 * jnp.tanh(0.5 * gate) + 0.5
             gated = value * sigma
             h = gated.astype(BF16)
             hidden[rows, :] = h
-            d_h = dot_nt(cot_in[rows, :], weight_down())
-            d_v = (d_h * sigma).astype(BF16)
-            d_g = (d_h * gated * (1.0 - sigma)).astype(BF16)
-            d_value[rows, :] = d_v
-            d_gate[rows, :] = d_g
-            added = dot(h, weight_down())
-            d_a = dot_nt(d_v, weight(0)) + dot_nt(d_g, weight(1))
+            d_h = dot_nt(cot_in[rows, :], w_down)
+            d_both = jnp.concatenate(
+                [(d_h * sigma).astype(BF16), (d_h * gated * (1.0 - sigma)).astype(BF16)], 1
+            )
+            d_unit[rows, :] = d_both
+            added = dot(h, w_down)
+            d_a = dot_nt(d_both, w_gated)
             if i > 0:
                 added = added + summed[rows, :]
                 d_a = d_a + d_act[rows, :]
@@ -601,45 +667,27 @@
                 summed[rows, :] = added
                 d_act[rows, :] = d_a
             else:
-                out = (tokens_in[rows, :].astype(F32) + added).astype(BF16)
-                out = dot(turn[...], out).astype(BF16)
-                for run, piece in enumerate(pieces(tile)):
-                    result[piece, :] = out[run * SEGMENTS : run * SEGMENTS + SEGMENTS]
                 d_m = (d_gelu[rows, :] * d_a).astype(BF16)
                 d_mixed[rows, :] = d_m
                 adjoint[rows, :] = dot_nt(d_m, w_out[...])
+                out = (tokens_in[rows, :].astype(F32) + added).astype(BF16)
+                for block in range(UNIT_ROWS // BLOCK):
+                    turned = dot(turn[...], out[block * BLOCK : block * BLOCK + BLOCK])
+                    turned = turned.astype(BF16)
+                    for run, piece in enumerate(pieces(tile * (UNIT_ROWS // BLOCK) + block)):
+                        result[piece, :] = turned[run * SEGMENTS : run * SEGMENTS + SEGMENTS]
 
         if fused and i > 0:
-            units[i - 1].over_plane()
-
-        GRAD_ROWS = 128
-        for k, (left, right) in enumerate(((cot_t, hidden), (act_t, d_value), (act_t, d_gate))):
-
-            @pl.loop(0, D // GRAD_ROWS)
-            def _(tile):
-                rows = pl.ds(pl.multiple_of(tile * GRAD_ROWS, GRAD_ROWS), GRAD_ROWS)
-                g = dot(left[rows, :], right[...]).astype(BF16)
-                if fused:
-                    full = r.unit_full
-                    r.unit_full[i, k, tile] = g.reshape(full.shape[3:])
-                elif k == 0:
-                    r.grad_down[c, rows, :] = g
-                else:
-                    r.grad_glu[c, k - 1, rows, :] = g
-
-        if fused:
-            units[i].over_cores()
-            if i > 0:
-                units[i - 1].sum_plane()
-                unit_copies = [] if i == 1 else unit_copies
-                if i > 1:
-                    unit_copies.append(
-                        links.send(
-                            r.unit_summed.at[i - 1],
-                            r.unit_sums.at[i - 2],
-                            (s, lax.rem(t + i - 1, T)),
-                        )
-                    )
+            reduces[i - 1].over_plane()
+        if i < T - 1:
+            unit_grads(i)
+        if fused and i > 1:
+            reduces[i - 2].turn_plane()
+        if fused and i > 2:
+            unit_sums(i - 3)
+
+    result_copy = pltpu.make_async_copy(result, r.result, r.local_sem.at[0])
+    result_copy.start()
 
     def backward_step(index, carry):
         step = L - 1 - index
@@ -660,29 +708,30 @@
     factor_seg = power(lam, L)
     own, _ = fold(zero1, factor_seg, finals, seg_masks, [None] * SEGMENTS)
     exchange = Exchange(own, lam, r.adj_tp, r.adj_seq, False)
+    unit_grads(T - 1)
     if fused:
-        units[T - 1].over_plane()
+        reduces[T - 2].turn_plane()
     exchange.over_seq()
-
-    grad_out = r.grad_out_full if fused else r.grad_out
-
-    @pl.loop(0, 2 * N // 128)
-    def _(tile):
-        rows = pl.ds(pl.multiple_of(tile * 128, 128), 128)
-        grad_out[rows, :] = dot(state_t[rows, :], d_mixed[...]).astype(BF16)
-
-    if fused:
-        out_full = r.out_full
+    grad_out = dot_tn(state_low[...], d_mixed[...]).astype(BF16)
+
+    def divide(grad, full):
         for i in range(T):
             at = lax.rem(t + i, T) * n
             for part in range(2):
                 rows = pl.ds(pl.multiple_of(part * N + at, n), n)
-                out_full[i, part * (S // 4) : (part + 1) * (S // 4)] = grad_out[rows, :].reshape(
+                full[i, part * (S // 4) : (part + 1) * (S // 4)] = grad[rows, :].reshape(
                     S // 4, 2, -1, D
                 )
-        out_reduce = Reduce(place, out_full, r.out_halves, r.out_eighths, r.out_summed)
+
+    if fused:
+        r.grad_rates[...] = grad_out
+        divide(r.grad_rates, r.out_full)
+        out_reduce = Reduce(place, r.out_full, r.out_halves, r.out_eighths, r.out_summed)
+        reduces[T - 1].over_plane()
         out_reduce.over_cores()
-
+        unit_sums(T - 3)
+    else:
+        r.grad_out[...] = grad_out
     carry = exchange.carry()
     _, entering = fold(carry, factor_seg, finals, seg_masks, [None] * SEGMENTS)
     entering = entering[::-1]
@@ -727,50 +776,30 @@
 
     if fused:
         out_reduce.over_plane()
-        units[T - 1].sum_plane()
-        unit_copies.append(
-            links.send(
-                r.unit_summed.at[T - 1], r.unit_sums.at[T - 2], (s, lax.rem(t + T - 1, T))
-            )
-        )
-
-    @pl.loop(0, R // BLOCK)
-    def _(tile):
-        rows = block_rows(tile)
-        d_proj[rows, :] = (adjoint[rows, :] * gamma_signed).astype(BF16)
-
-    grad_in = r.grad_in_full if fused else r.grad_in
-
-    @pl.loop(0, D // 128)
-    def _(tile):
-        rows = pl.ds(pl.multiple_of(tile * 128, 128), 128)
-        grad_in[rows, :] = dot(normed_t[rows, :], d_proj[...]).astype(grad_in.dtype)
-
+    d_proj[...] = (adjoint[...] * gamma_signed).astype(BF16)
+    grad_in = dot_tn(d_proj[...], normed[...]).astype(BF16)
     if fused:
-        in_full = r.in_full
-        for k in range(T // 2):
-            re = grad_in[:, k * 128 : k * 128 + 128]
-            im = grad_in[:, N + k * 128 : N + k * 128 + 128]
-            even = jnp.where(half, re, pltpu.roll(im, 64, 1))
-            odd = jnp.where(half, pltpu.roll(re, 64, 1), im)
-            for part, value in enumerate((even, odd)):
-                in_full[lax.rem(2 * k + part + T - t, T)] = value.astype(BF16).reshape(
-                    in_full.shape[1:]
-                )
-        in_reduce = Reduce(place, in_full, r.in_halves, r.in_eighths, r.in_summed)
+        r.grad_rates[...] = grad_in
+        divide(r.grad_rates, r.in_full)
+        in_reduce = Reduce(place, r.in_full, r.in_halves, r.in_eighths, r.in_summed)
         in_reduce.over_cores()
+        reduces[T - 1].turn_plane()
+        unit_sums(T - 2)
         out_reduce.sum_plane()
         out_copies = [
             links.send(r.out_summed.at[i], r.out_sums.at[i - 1], (s, lax.rem(t + i, T)))
             for i in range(1, T)
         ]
         in_reduce.over_plane()
+        unit_sums(T - 1)
+    else:
+        r.grad_in[...] = grad_in
 
     @pl.loop(0, R // BLOCK)
     def _(tile):
         rows = block_rows(tile)
         d_m = d_mixed[rows, :].astype(F32)
-        d_n = dot_nt(d_proj[rows, :], w_in[...]) + d_m * skip_row
+        d_n = dot(d_proj[rows, :], w_in[...]) + d_m * skip_row
         c = centred[rows, :]
         sums[0:8, :] += jnp.sum((d_n * c).reshape(BLOCK // 8, 8, D), 0)
         sums[8:16, :] += jnp.sum((d_m * normed[rows, :].astype(F32)).reshape(BLOCK // 8, 8, D), 0)
@@ -784,6 +813,9 @@
         for run, piece in enumerate(pieces(tile)):
             grad_tokens[piece, :] = out[run * SEGMENTS : run * SEGMENTS + SEGMENTS]
 
+    grad_copy = pltpu.make_async_copy(grad_tokens, r.grad_tokens, r.local_sem.at[1])
+    grad_copy.start()
+    small = r.small
     small_rows = [
         jnp.sum(sums[0:8, :], 0, keepdims=True),
         jnp.sum(sums[8:16, :], 0, keepdims=True),
@@ -795,6 +827,8 @@
             small[k : k + 1, :] = row
         small[4:8, :] = jnp.zeros((4, D), F32)
         links.close()
+        result_copy.wait()
+        grad_copy.wait()
         return
 
     small_tp, small_seq = (r.small_tp, r.small_seq)
@@ -807,9 +841,9 @@
             total = total + buffer[k].astype(F32)
         return total.astype(BF16)
 
-    unit_sum = r.unit_sum
+    unit_sum, out_sum, in_sum = (r.unit_sum, r.out_sum, r.in_sum)
     arrive(unit_copies)
-    unit_sum[:, place.chip, place.core] = total_of(r.unit_summed[0], r.unit_sums)
+    unit_sum[0, place.chip, place.core] = total_of(r.unit_summed[0, 0], r.unit_sums.at[:, 0])
     unit_spread = Spread(place, unit_sum)
     unit_spread.over_plane()
 
@@ -818,7 +852,6 @@
         links.send(r.in_summed.at[i], r.in_sums.at[i - 1], (s, lax.rem(t + i, T)))
         for i in range(1, T)
     ]
-    out_sum, in_sum = (r.out_sum, r.in_sum)
     arrive(out_copies)
     out_sum[0, place.chip, place.core] = total_of(r.out_summed[0], r.out_sums)
     out_spread = Spread(place, out_sum)
@@ -839,13 +872,8 @@
     out_spread.over_cores()
 
     unit_spread.finish()
-    for k in range(2):
-        r.grad_glu[k] = unit_sum[k + 1].reshape(D, -1).astype(F32)
-    width = r.grad_down.shape[0]
-    row = lax.broadcasted_iota(jnp.int32, (width, width), 0)
-    column = lax.broadcasted_iota(jnp.int32, (width, width), 1)
-    unit = jnp.where(row == column, 1.0, 0.0).astype(BF16)
-    r.grad_down[...] = dot_nt(unit, unit_sum[0].reshape(D, -1))
+    unit_copy = pltpu.make_async_copy(unit_sum.at[0], r.grad_units, r.local_sem.at[2])
+    unit_copy.start()
 
     arrive(small_copies)
     part = small_seq[0]
@@ -857,23 +885,79 @@
     small[4:8, :] = jnp.zeros((4, D), F32)
 
     out_spread.finish()
-    r.grad_out[...] = out_sum[0].reshape(2, n, D).astype(F32)
+    out_copy = pltpu.make_async_copy(out_sum.at[0], r.grad_out, r.local_sem.at[3])
+    out_copy.start()
     in_spread.over_cores()
     in_spread.finish()
-    value = in_sum[0].reshape(D, 128).astype(F32)
-    r.grad_in[0] = value[:, :n]
-    r.grad_in[1] = pltpu.roll(value, 64, 1)[:, :n]
+    in_copy = pltpu.make_async_copy(in_sum.at[0], r.grad_in, r.local_sem.at[4])
+    in_copy.start()
+    for copy in (result_copy, grad_copy, unit_copy, out_copy, in_copy):
+        copy.wait()
     links.close()
+
+
+def finish_kernel(T, names, *refs):
+    r = types.SimpleNamespace(**dict(zip(names, refs)))
+    half = r.grad_rows.shape[0] // 2
+    arrays = [(r.result_in, r.result_rows, r.result)] + [
+        tuple(ref.at[pl.ds(at, half)] for ref in (r.grad_tokens_in, r.grad_rows, r.grad_tokens))
+        for at in (0, half)
+    ]
+    fetched = [
+        pltpu.make_async_copy(source, kept, r.local_sem.at[index])
+        for index, (source, kept, _) in enumerate(arrays)
+    ]
+    copies = [
+        pltpu.make_async_copy(kept, target, r.local_sem.at[index])
+        for index, (_, kept, target) in enumerate(arrays)
+    ]
+    for copy in fetched:
+        copy.start()
+    for fetch, copy in zip(fetched, copies):
+        fetch.wait()
+        copy.start()
+    D_rows, lanes = (r.glu.shape[3], r.glu.shape[4])
+    r.glu[0] = r.units_in[:, :, 0:D_rows, :lanes].astype(F32)
+    r.glu[1] = r.units_in[:, :, 0:D_rows, lanes:].astype(F32)
+    r.down[...] = r.units_in[:, :, D_rows:, :].astype(F32)
+    r.out[...] = r.out_in[...].astype(F32)
+    r.in_[...] = r.in_in[...].astype(F32)
+    r.gain[...] = r.small[0:1, :]
+    r.skip[...] = r.small[1:2, :]
+    n = r.decay_log.shape[1]
+    N = T * n
+    t = lax.axis_index("tp")
+
+    def mine(row, first):
+        own = row[:, first : first + n]
+        for z in range(1, T):
+            own = jnp.where(t == z, row[:, first + z * n : first + z * n + n], own)
+        return own
+
+    lam_re, lam_im, gamma = decay_terms(r.decay_log[...], r.angle[...])
+    g_re = mine(r.small[2:3, :], 0)
+    g_im = mine(r.small[2:3, :], N)
+    g_gamma = mine(r.small[3:4, :], 0)
+    rate_step = jnp.exp(r.decay_log[...])
+    r.decay[...] = rate_step * (
+        g_gamma * (1.0 - fall(2.0 * rate_step)) / gamma - g_re * lam_re - g_im * lam_im
+    )
+    r.turn[...] = g_im * lam_re - g_re * lam_im
+    for copy in copies:
+        copy.wait()
+
+
+def fall(value):
+    series = jnp.ones_like(value)
+    for order in range(12, 1, -1):
+        series = 1.0 - value / order * series
+    return jnp.where(value < 0.5, value * series, 1.0 - jnp.exp(-value))
 
 
 def decay_terms(decay_log, angle):
     rate_step = jnp.exp(decay_log)
-    radius = jnp.exp(-rate_step)
-    return (
-        radius * jnp.cos(angle),
-        radius * jnp.sin(angle),
-        jnp.sqrt(-jnp.expm1(-2.0 * rate_step)),
-    )
+    radius = 1.0 - fall(rate_step)
+    return (radius * jnp.cos(angle), radius * jnp.sin(angle), jnp.sqrt(fall(2.0 * rate_step)))
 
 
 def local(
@@ -897,44 +981,44 @@
     units = down_proj.shape[0]
     C = S // 2
     fused = (
-        S % 4 == 0
+        S == 8
         and T % 2 == 0
+        and T > 2
         and 2 * n == 128
-        and units % 128 == 0
+        and 2 * units == D
         and all(size % (16 * S) == 0 for size in (D, 2 * n, units))
-        and (2 * C) * 64 == D
     )
     vmem = pl.BlockSpec(memory_space=pltpu.VMEM)
     anywhere = pl.BlockSpec(memory_space=pl.ANY)
-    lam_re, lam_im, gamma = decay_terms(decay_log, angle)
     ins = dict(
         lengths=(lengths, pl.BlockSpec(memory_space=pltpu.SMEM)),
-        tokens=(tokens, vmem),
-        cot=(cotangent, vmem),
+        tokens=(tokens, anywhere),
+        cot=(cotangent, anywhere),
         gain=(ln_gain.reshape(1, D), vmem),
         skip=(skip.reshape(1, D), vmem),
     )
     outs = dict(
-        result=((R, D), BF16),
-        grad_tokens=((R, D), F32),
-        small=((8, D), F32),
+        result=((R, D), BF16, anywhere),
+        grad_tokens=((R, D), F32, anywhere),
+        small=((8, D), F32, vmem),
     )
     scratch = dict(
+        tokens_raw=((R, D), BF16),
+        cot_raw=((R, D), BF16),
+        result_rows=((R, D), BF16),
+        grad_rows=((R, D), F32),
         turn=((BLOCK, BLOCK), BF16),
         tokens_in=((R, D), BF16),
         cot_in=((R, D), BF16),
         centred=((R, D), F32),
         inv_std=((R, 128), F32),
         normed=((R, D), BF16),
-        normed_t=((D, R), BF16),
-        cot_t=((D, R), BF16),
         proj=((R, 2 * N), F32),
         keep=((R, 128), F32),
         keep_next=((R, 128), F32),
         state=((R, 2 * N), F32),
-        state_t=((2 * N, R), BF16),
+        state_low=((R, 2 * N), BF16),
         act=((R, D), BF16),
-        act_t=((D, R), BF16),
         d_gelu=((R, D), F32),
         d_act=((R, D), F32),
         summed=((R, D), F32),
@@ -942,8 +1026,7 @@
         adjoint=((R, 2 * N), F32),
         d_proj=((R, 2 * N), BF16),
         hidden=((R, units), BF16),
-        d_value=((R, units), BF16),
-        d_gate=((R, units), BF16),
+        d_unit=((R, 2 * units), BF16),
         seg_carry=((SEGMENTS, 2 * N), F32),
         sums=((16, D), F32),
         state_tp=((T, 8, 128), F32),
@@ -951,107 +1034,98 @@
         adj_tp=((T, 8, 128), F32),
         adj_seq=((S, 8, 128), F32),
     )
+    in_rows = in_proj.transpose(0, 2, 1)
     if fused:
-        rates = jnp.stack(
-            [jnp.concatenate([lam_re, lam_im]), jnp.concatenate([gamma, gamma])]
-            + [jnp.zeros((2 * n,), F32)] * 6
-        )
+        unit_rows = D // S + units // S
         ins.update(
-            rates=(rates, vmem),
-            in_proj=(in_proj, vmem),
+            decay_log=(decay_log.reshape(1, n), vmem),
+            angle=(angle.reshape(1, n), vmem),
+            in_proj=(in_rows.reshape(C, 2, 2 * n // S, D), anywhere),
             out_proj=(out_proj.reshape(C, 2, 2 * n // S, D), anywhere),
             glu_proj=(glu_proj.reshape(2, C, 2, D // S, units), anywhere),
             down_proj=(down_proj.reshape(C, 2, units // S, D), anywhere),
         )
         outs.update(
-            grad_in=((2, D, n), F32),
-            grad_out=((2, n, D), F32),
-            grad_glu=((2, D, units), F32),
-            grad_down=((units, D), F32),
-        )
-
-        def whole(parts, rows, lanes, lead=()):
-            return (lead + (parts, C, 2, rows, lanes), BF16)
-
-        def halves(parts, rows, lanes, lead=()):
-            return (lead + (parts, C, rows, lanes), BF16)
-
-        def eighths(parts, rows, lanes, lead=()):
-            return (lead + (C - 1, parts, rows, lanes), BF16)
-
-        def own(parts, rows, lanes, lead=()):
-            return (lead + (parts, rows, lanes), BF16)
-
-        unit_sizes = (3, D // S, units, (T,))
-        out_sizes = (T, 2 * n // S, D)
-        in_sizes = (T, D // S, 2 * n)
+            grad_in=((C, 2, 2 * n // S, D), BF16, anywhere),
+            grad_out=((C, 2, 2 * n // S, D), BF16, anywhere),
+            grad_units=((C, 2, unit_rows, D), BF16, anywhere),
+        )
+
+        def whole(parts, rows, lead=()):
+            return (lead + (parts, C, 2, rows, D), BF16)
+
+        def halves(parts, rows, lead=()):
+            return (lead + (parts, C, rows, D), BF16)
+
+        def eighths(parts, rows, lead=()):
+            return (lead + (C - 1, parts, rows, D), BF16)
+
+        def own(parts, rows, lead=()):
+            return (lead + (parts, rows, D), BF16)
+
+        unit_sizes = (1, unit_rows, (T,))
+        rate_sizes = (T, 2 * n // S)
         scratch.update(
-            w_in=((D, 2 * N), BF16),
+            w_in=((2 * N, D), BF16),
             w_out=((2 * N, D), BF16),
             rates_all=((T, 8, 128), F32),
-            in_slices=((T, C, 2, D // S, 2 * n), BF16),
+            in_slices=((T, C, 2, 2 * n // S, D), BF16),
             out_slices=((T, C, 2, 2 * n // S, D), BF16),
-            glu_slices=((2, T, C, 2, D // S, units), BF16),
-            down_slices=((T, C, 2, units // S, D), BF16),
-            grad_out_full=((2 * N, D), BF16),
-            grad_in_full=((D, 2 * N), F32),
+            unit_slices=((T, C, 2, unit_rows, D), BF16),
+            grad_rates=((2 * N, D), BF16),
             small_tp=((T, 16, 128), F32),
             small_seq=((S, 16, 128), F32),
-            unit_sums=((T - 1, 3, D // S, units), BF16),
+            unit_sums=((T - 1, 1, unit_rows, D), BF16),
             out_sums=((T - 1, 2 * n // S, D), BF16),
-            in_sums=((T - 1, D // S, 2 * n), BF16),
-            unit_sum=((3, C, 2, D // S, units), BF16),
+            in_sums=((T - 1, 2 * n // S, D), BF16),
+            unit_sum=((1, C, 2, unit_rows, D), BF16),
             out_sum=((1, C, 2, 2 * n // S, D), BF16),
-            in_sum=((1, C, 2, D // S, 2 * n), BF16),
-        )
-        scratch.update(
+            in_sum=((1, C, 2, 2 * n // S, D), BF16),
             unit_full=whole(*unit_sizes),
             unit_halves=halves(*unit_sizes),
             unit_eighths=eighths(*unit_sizes),
             unit_summed=own(*unit_sizes),
-            out_full=whole(*out_sizes),
-            out_halves=halves(*out_sizes),
-            out_eighths=eighths(*out_sizes),
-            out_summed=own(*out_sizes),
-            in_full=whole(*in_sizes),
-            in_halves=halves(*in_sizes),
-            in_eighths=eighths(*in_sizes),
-            in_summed=own(*in_sizes),
+            out_full=whole(*rate_sizes),
+            out_halves=halves(*rate_sizes),
+            out_eighths=eighths(*rate_sizes),
+            out_summed=own(*rate_sizes),
+            in_full=whole(*rate_sizes),
+            in_halves=halves(*rate_sizes),
+            in_eighths=eighths(*rate_sizes),
+            in_summed=own(*rate_sizes),
         )
         links = 160
     else:
-        w_in = lax.all_gather(in_proj, "tp", axis=2, tiled=True)
+        w_in = lax.all_gather(in_rows, "tp", axis=1, tiled=True).reshape(2 * N, D)
         w_out = lax.all_gather(out_proj, "tp", axis=1, tiled=True).reshape(2 * N, D)
-        lam_re, lam_im, gamma = (
-            lax.all_gather(part, "tp", tiled=True) for part in (lam_re, lam_im, gamma)
-        )
+        glu = lax.all_gather(glu_proj, "tp")
         rates = jnp.stack(
-            [jnp.concatenate([lam_re, lam_im]), jnp.concatenate([gamma, gamma])]
-            + [jnp.zeros((2 * N,), F32)] * 6
+            [lax.all_gather(part, "tp", tiled=True) for part in decay_terms(decay_log, angle)]
+            + [jnp.zeros((N,), F32)] * 5
         )
         ins.update(
             rates=(rates, vmem),
-            w_in=(jnp.concatenate([w_in[0], w_in[1]], 1), vmem),
+            w_in=(w_in, vmem),
             w_out=(w_out, vmem),
-            glu=(lax.all_gather(glu_proj, "tp"), vmem),
+            glu=(jnp.concatenate([glu[:, 0], glu[:, 1]], 2), vmem),
             down=(lax.all_gather(down_proj, "tp"), vmem),
         )
         outs.update(
-            grad_in=((D, 2 * N), BF16),
-            grad_out=((2 * N, D), BF16),
-            grad_glu=((T, 2, D, units), BF16),
-            grad_down=((T, D, units), BF16),
+            grad_in=((2 * N, D), BF16, vmem),
+            grad_out=((2 * N, D), BF16, vmem),
+            grad_glu=((T, D, 2 * units), BF16, vmem),
+            grad_down=((T, units, D), BF16, vmem),
         )
         links = 2 * (T - 1 + S - 1)
     names = [*ins, *outs, *scratch, *dict(local_sem=0, send_sem=0, recv_sem=0)]
-    result, grad_tokens, small, grad_in, grad_out, grad_glu, grad_down = pl.pallas_call(
+    results = pl.pallas_call(
         functools.partial(layer_kernel, S, T, fused, names),
-        out_shape=tuple(jax.ShapeDtypeStruct(shape, dtype) for shape, dtype in outs.values()),
+        out_shape=tuple(jax.ShapeDtypeStruct(shape, dtype) for shape, dtype, _ in outs.values()),
         in_specs=[spec for _, spec in ins.values()],
-        out_specs=(vmem,) * len(outs),
+        out_specs=tuple(spec for _, _, spec in outs.values()),
         scratch_shapes=[pltpu.VMEM(shape, dtype) for shape, dtype in scratch.values()]
         + [
-            pltpu.SemaphoreType.DMA((4,)),
+            pltpu.SemaphoreType.DMA((7,)),
             pltpu.SemaphoreType.DMA((links,)),
             pltpu.SemaphoreType.DMA((links,)),
         ],
@@ -1059,23 +1133,70 @@
             collective_id=0, has_side_effects=True, vmem_limit_bytes=60 * 2**20
         ),
     )(*[value for value, _ in ins.values()])
-    t = lax.axis_index("tp")
-    if not fused:
-        small = lax.psum(small, ("seq", "tp"))
-
-        def reduced(part):
-            part = lax.psum_scatter(part, "tp", scatter_dimension=0, tiled=True)
-            return lax.psum(part, "seq").astype(F32)
-
-        grad_in = grad_in.reshape(D, 2, T, n).transpose(2, 1, 0, 3).reshape(T * 2, D, n)
-        grad_in = reduced(grad_in)
-        grad_out = grad_out.reshape(2, T, n, D).transpose(1, 0, 2, 3).reshape(T * 2, n, D)
-        grad_out = reduced(grad_out)
-        grad_glu = reduced(grad_glu.reshape(T * 2, D, units))
-        grad_down = reduced(grad_down)[0].T
+    if fused:
+        result, grad_tokens, small, grad_in, grad_out, grad_units = results
+        ins = dict(
+            result_in=(result, anywhere),
+            grad_tokens_in=(grad_tokens, anywhere),
+            small=(small, vmem),
+            in_in=(grad_in, vmem),
+            out_in=(grad_out, vmem),
+            units_in=(grad_units, vmem),
+            decay_log=(decay_log.reshape(1, n), vmem),
+            angle=(angle.reshape(1, n), vmem),
+        )
+        outs = dict(
+            result=((R, D), BF16, anywhere),
+            grad_tokens=((R, D), F32, anywhere),
+            gain=((1, D), F32, vmem),
+            in_=((C, 2, 2 * n // S, D), F32, vmem),
+            decay=((1, n), F32, vmem),
+            turn=((1, n), F32, vmem),
+            out=((C, 2, 2 * n // S, D), F32, vmem),
+            skip=((1, D), F32, vmem),
+            glu=((2, C, 2, D // S, units), F32, vmem),
+            down=((C, 2, units // S, D), F32, vmem),
+        )
+        scratch = dict(result_rows=((R, D), BF16), grad_rows=((R, D), F32))
+        names = [*ins, *outs, *scratch, *dict(local_sem=0)]
+        result, grad_tokens, gain, in_, decay, turn, out, skip_sum, glu, down = pl.pallas_call(
+            functools.partial(finish_kernel, T, names),
+            out_shape=tuple(
+                jax.ShapeDtypeStruct(shape, dtype) for shape, dtype, _ in outs.values()
+            ),
+            in_specs=[spec for _, spec in ins.values()],
+            out_specs=tuple(spec for _, _, spec in outs.values()),
+            scratch_shapes=[pltpu.VMEM(shape, dtype) for shape, dtype in scratch.values()]
+            + [pltpu.SemaphoreType.DMA((3,))],
+            compiler_params=pltpu.CompilerParams(vmem_limit_bytes=60 * 2**20),
+        )(*[value for value, _ in ins.values()])
+        return (
+            result,
+            grad_tokens,
+            gain.reshape(D),
+            in_.reshape(2, n, D).transpose(0, 2, 1),
+            decay.reshape(n),
+            turn.reshape(n),
+            out.reshape(2, n, D),
+            skip_sum.reshape(D),
+            glu.reshape(2, D, units),
+            down.reshape(units, D),
+        )
+    result, grad_tokens, small, grad_in, grad_out, grad_glu, grad_down = results
+    small = lax.psum(small, ("seq", "tp"))
+
+    def reduced(part):
+        part = lax.psum_scatter(part, "tp", scatter_dimension=0, tiled=True)
+        return lax.psum(part, "seq").astype(F32)
+
+    def by_tp(grad):
+        return reduced(grad.reshape(2, T, n, D).transpose(1, 0, 2, 3).reshape(T * 2, n, D))
+
+    grad_glu = reduced(grad_glu)[0].reshape(D, 2, units).transpose(1, 0, 2)
+    grad_down = reduced(grad_down)[0]
 
     def mine(row):
-        return lax.dynamic_slice_in_dim(row, t * n, n)
+        return lax.dynamic_slice_in_dim(row, lax.axis_index("tp") * n, n)
 
     g_re, g_im, g_gamma = (mine(small[2, :N]), mine(small[2, N:]), mine(small[3, :N]))
     _, pull = jax.vjp(decay_terms, decay_log, angle)
@@ -1084,10 +1205,10 @@
         result,
         grad_tokens,
         small[0],
-        grad_in,
+        by_tp(grad_in).transpose(0, 2, 1),
         grad_decay,
         grad_angle,
-        grad_out,
+        by_tp(grad_out),
         small[1],
         grad_glu,
         grad_down,

time: 120 us -> 87.5 us (0.73)
  Pallas kernels: 103 us -> 85.2 us
  local copies, waits for them, and re-layouts: 14.1 us -> 1.26 us
  other arithmetic: 2.02 us -> 0 us
    pallas_call x1, Pallas kernels: 103 us -> 79.8 us  [local(): pl.pallas_call(functools.partial(layer_kernel, S, T, fused, names), out_s...]
    unnamed x17 -> x0, local copies, waits for them, and re-layouts: 9.77 us -> none
    pallas_call x0 -> x1, Pallas kernels: none -> 5.47 us  [local(): pl.pallas_call(functools.partial(finish_kernel, T, names), out_shape=tupl...]
    slice x2 -> x0, local copies, waits for them, and re-layouts: 2.26 us -> none  [the longest x1 1.38 us: local(): small[1]]
where the time goes in v3:
time: 87.5 us; the launch traced here: 87.3 us
  Pallas kernels  85.2 us (97%)
  local copies, waits for them, and re-layouts  1.26 us (1%)
    pallas_call x1, Pallas kernels, local(): pl.pallas_call(functools.partial(layer_kernel, S, T, fused, names), out_s...  79.8 us
    pallas_call x1, Pallas kernels, local(): pl.pallas_call(functools.partial(finish_kernel, T, names), out_shape=tupl...  5.47 us

profile of v3, /device:TPU:1, one launch (start us, length us, event | category | flops | bytes accessed | tf_op | source)
XLA Modules:
  0.0 87.3 jit_solution(6593343058542377201)
XLA Ops:
  0.6 1.3 %reshape.71.refs_4_ = bf16[1,512]{1,0:T(2,128)(2,1)} reshape(bf16[512]{0:T(512)(128)(2,1)} %param.17) | data formatting | bytes 2048 | tf_op jit(solution)/shard_map/reshape | solution.py:998
  1.9 79.8 %shard_map.186 = (bf16[1024,512]{1,0:T(8,128)(2,1)}, f32[1024,512]{1,0:T(8,128)}, f32[8,512]{1,0:T(8,128)}, bf16[4,2,16,512]{3,2,1,0:T(8,128)(2,1)}, bf16[4,2,16...) custom-call(s32[6]{0:T(128)} %refs_0_.1, bf16[1024,512]{1,0:T(8,128)(2,1)} %refs_1_.1, bf16[1024,512]{1,0:T(8,128)(2,1)} %refs_2_.1, ...), custom_call_target="tpu_custom_call" | custom-call | tf_op jit(solution)/shard_map/pallas_call | solution.py:1121
  81.7 5.5 %shard_map.187 = (bf16[1024,512]{1,0:T(8,128)(2,1)}, f32[1024,512]{1,0:T(8,128)}, f32[1,512]{1,0:T(1,128)}, f32[4,2,16,512]{3,2,1,0:T(8,128)}, f32[1,64]{1,0:T(1...) custom-call(bf16[1024,512]{1,0:T(8,128)(2,1)} %get-tuple-element.26., ...), custom_call_target="tpu_custom_call" | custom-call | tf_op jit(solution)/shard_map/pallas_call | solution.py:1162

commit v4 on v3

--- a/solution.py
+++ b/solution.py
@@ -251,11 +251,11 @@
     r = types.SimpleNamespace(**dict(zip(names, refs)))
     links = Links(r.send_sem, r.recv_sem)
     place = Place(S, T, links)
-    lengths = r.lengths
+    lengths = r.counts
     tokens = r.tokens_raw
     cot = r.cot_raw
-    result = r.result_rows
-    grad_tokens = r.grad_rows
+    result = r.tokens_raw
+    grad_tokens = r.d_gelu
     turn = r.turn
     tokens_in = r.tokens_in
     cot_in = r.cot_in
@@ -272,7 +272,7 @@
     d_act = r.d_act
     summed = r.summed
     d_mixed = r.d_mixed
-    adjoint = r.adjoint
+    adjoint = r.summed
     d_proj = r.d_proj
     hidden = r.hidden
     d_unit = r.d_unit
@@ -296,7 +296,9 @@
 
     fetched = [
         pltpu.make_async_copy(source, target, r.local_sem.at[index])
-        for index, (source, target) in enumerate(((r.tokens, tokens), (r.cot, cot)))
+        for index, (source, target) in enumerate(
+            ((r.tokens, tokens), (r.cot, cot), (r.gain, r.gain_row), (r.skip, r.skip_row), (r.lengths, r.counts))
+        )
     ]
     if fused:
         in_slices, out_slices, unit_slices = (r.in_slices, r.out_slices, r.unit_slices)
@@ -304,9 +306,11 @@
         D_rows = r.glu_proj.shape[3]
         gated_rows = unit_slices.at[0, :, :, pl.ds(0, D_rows)]
         weights = [
-            pltpu.make_async_copy(source, target, r.local_sem.at[2 + index])
+            pltpu.make_async_copy(source, target, r.local_sem.at[5 + index])
             for index, (source, target) in enumerate(
                 (
+                    (r.decay_log, r.decay_row),
+                    (r.angle, r.angle_row),
                     (r.in_proj, in_slices.at[0]),
                     (r.out_proj, out_slices.at[0]),
                     (r.glu_proj.at[0], gated_rows.at[:, :, :, pl.ds(0, units)]),
@@ -322,22 +326,21 @@
     if fused:
         rates_all = r.rates_all
         rates_all[t] = jnp.zeros(rates_all.shape[1:], F32)
-        for index, row in enumerate(decay_terms(r.decay_log[...], r.angle[...])):
-            rates_all[t, index : index + 1, 0:n] = row
         gather_in = Gather(place, in_slices, 1, T)
         gather_out = Gather(place, out_slices, 1, T)
         gather_units = [Gather(place, unit_slices, slot, slot + 1) for slot in range(1, T)]
         for copy in weights:
             copy.wait()
+        for index, row in enumerate(decay_terms(r.decay_row[...], r.angle_row[...])):
+            rates_all[t, index : index + 1, 0:n] = row
         pl.semaphore_wait(barrier, T - 1 + S - 1)
         gather_in.over_tp()
         rate_copies = [
             links.send(rates_all.at[t], rates_all.at[t], (s, peer)) for peer in peers_tp
         ]
-        gather_out.over_tp()
-        for gather in gather_units:
-            gather.over_tp()
-
+
+    for copy in fetched[2:]:
+        copy.wait()
     starts = []
     total = jnp.int32(0)
     for index in range(lengths.shape[0]):
@@ -356,8 +359,8 @@
             hit = hit | ((start >= low) & (start < high))
         return jnp.where(hit, 0.0, 1.0)
 
-    gain_row = r.gain[...]
-    skip_row = r.skip[...].astype(F32)
+    gain_row = r.gain_row[...]
+    skip_row = r.skip_row[...].astype(F32).reshape(1, D)
 
     down_index = lax.broadcasted_iota(jnp.int32, (BLOCK, BLOCK), 0)
     across_index = lax.broadcasted_iota(jnp.int32, (BLOCK, BLOCK), 1)
@@ -401,7 +404,8 @@
     pl.loop(0, R // BLOCK)(norm_tile)
     if fused:
         gather_in.over_plane()
-        gather_out.over_plane()
+        gather_out.over_tp()
+        gather_units[0].over_tp()
     fetched[1].wait()
     pl.loop(0, R // BLOCK)(cot_tile)
 
@@ -415,6 +419,7 @@
 
     if fused:
         gather_in.over_cores()
+        gather_units[1].over_tp()
         arrive(rate_copies)
         half = lax.broadcasted_iota(jnp.int32, (8, 128), 1) < n
         rate_rows = [rates_all[z] for z in range(T)]
@@ -427,6 +432,9 @@
         )
         lam_re, lam_im, gamma = (joined[k : k + 1] for k in range(3))
         gather_in.finish()
+        for gather in gather_units[2:]:
+            gather.over_tp()
+        gather_out.over_plane()
         assemble(in_slices, w_in)
     else:
         pl.semaphore_wait(barrier, T - 1 + S - 1)
@@ -557,12 +565,11 @@
     own, _ = fold(zero1, factor_seg, finals, seg_masks, [None] * SEGMENTS)
     exchange = Exchange(own, conj, r.state_tp, r.state_seq, True)
     if fused:
+        gather_units[0].over_plane()
         gather_out.over_cores()
-        gather_units[0].over_plane()
     exchange.over_seq()
     if fused:
-        for gather in gather_units[1:]:
-            gather.over_plane()
+        gather_units[1].over_plane()
         gather_out.finish()
         assemble(out_slices, w_out)
     carry = exchange.carry()
@@ -582,6 +589,9 @@
         )
 
     lax.fori_loop(0, L, write_state, entering_groups())
+    if fused:
+        for gather in gather_units[2:]:
+            gather.over_plane()
 
     @pl.loop(0, R // BLOCK)
     def _(tile):
@@ -990,12 +1000,13 @@
     )
     vmem = pl.BlockSpec(memory_space=pltpu.VMEM)
     anywhere = pl.BlockSpec(memory_space=pl.ANY)
+    hbm = pl.BlockSpec(memory_space=pltpu.HBM)
     ins = dict(
-        lengths=(lengths, pl.BlockSpec(memory_space=pltpu.SMEM)),
-        tokens=(tokens, anywhere),
-        cot=(cotangent, anywhere),
-        gain=(ln_gain.reshape(1, D), vmem),
-        skip=(skip.reshape(1, D), vmem),
+        lengths=(lengths, hbm),
+        tokens=(tokens, hbm),
+        cot=(cotangent, hbm),
+        gain=(ln_gain.reshape(1, D), hbm),
+        skip=(skip, hbm),
     )
     outs = dict(
         result=((R, D), BF16, anywhere),
@@ -1003,10 +1014,10 @@
         small=((8, D), F32, vmem),
     )
     scratch = dict(
+        gain_row=((1, D), F32),
+        skip_row=((D,), BF16),
         tokens_raw=((R, D), BF16),
         cot_raw=((R, D), BF16),
-        result_rows=((R, D), BF16),
-        grad_rows=((R, D), F32),
         turn=((BLOCK, BLOCK), BF16),
         tokens_in=((R, D), BF16),
         cot_in=((R, D), BF16),
@@ -1023,7 +1034,6 @@
         d_act=((R, D), F32),
         summed=((R, D), F32),
         d_mixed=((R, D), BF16),
-        adjoint=((R, 2 * N), F32),
         d_proj=((R, 2 * N), BF16),
         hidden=((R, units), BF16),
         d_unit=((R, 2 * units), BF16),
@@ -1038,12 +1048,12 @@
     if fused:
         unit_rows = D // S + units // S
         ins.update(
-            decay_log=(decay_log.reshape(1, n), vmem),
-            angle=(angle.reshape(1, n), vmem),
-            in_proj=(in_rows.reshape(C, 2, 2 * n // S, D), anywhere),
-            out_proj=(out_proj.reshape(C, 2, 2 * n // S, D), anywhere),
-            glu_proj=(glu_proj.reshape(2, C, 2, D // S, units), anywhere),
-            down_proj=(down_proj.reshape(C, 2, units // S, D), anywhere),
+            decay_log=(decay_log.reshape(1, n), hbm),
+            angle=(angle.reshape(1, n), hbm),
+            in_proj=(in_rows.reshape(C, 2, 2 * n // S, D), hbm),
+            out_proj=(out_proj.reshape(C, 2, 2 * n // S, D), hbm),
+            glu_proj=(glu_proj.reshape(2, C, 2, D // S, units), hbm),
+            down_proj=(down_proj.reshape(C, 2, units // S, D), hbm),
         )
         outs.update(
             grad_in=((C, 2, 2 * n // S, D), BF16, anywhere),
@@ -1069,6 +1079,8 @@
             w_in=((2 * N, D), BF16),
             w_out=((2 * N, D), BF16),
             rates_all=((T, 8, 128), F32),
+            decay_row=((1, n), F32),
+            angle_row=((1, n), F32),
             in_slices=((T, C, 2, 2 * n // S, D), BF16),
             out_slices=((T, C, 2, 2 * n // S, D), BF16),
             unit_slices=((T, C, 2, unit_rows, D), BF16),
@@ -1117,7 +1129,7 @@
             grad_down=((T, units, D), BF16, vmem),
         )
         links = 2 * (T - 1 + S - 1)
-    names = [*ins, *outs, *scratch, *dict(local_sem=0, send_sem=0, recv_sem=0)]
+    names = [*ins, *outs, *scratch, *dict(counts=0, local_sem=0, send_sem=0, recv_sem=0)]
     results = pl.pallas_call(
         functools.partial(layer_kernel, S, T, fused, names),
         out_shape=tuple(jax.ShapeDtypeStruct(shape, dtype) for shape, dtype, _ in outs.values()),
@@ -1125,14 +1137,20 @@
         out_specs=tuple(spec for _, _, spec in outs.values()),
         scratch_shapes=[pltpu.VMEM(shape, dtype) for shape, dtype in scratch.values()]
         + [
-            pltpu.SemaphoreType.DMA((7,)),
+            pltpu.SMEM(lengths.shape, jnp.int32),
+            pltpu.SemaphoreType.DMA((12,)),
             pltpu.SemaphoreType.DMA((links,)),
             pltpu.SemaphoreType.DMA((links,)),
         ],
         compiler_params=pltpu.CompilerParams(
-            collective_id=0, has_side_effects=True, vmem_limit_bytes=60 * 2**20
+            collective_id=0, has_side_effects=True, vmem_limit_bytes=46 * 2**20
         ),
-    )(*[value for value, _ in ins.values()])
+    )(
+        *[
+            pltpu.with_memory_space_constraint(value, pltpu.HBM) if spec is hbm else value
+            for value, spec in ins.values()
+        ]
+    )
     if fused:
         result, grad_tokens, small, grad_in, grad_out, grad_units = results
         ins = dict(
@@ -1168,7 +1186,7 @@
             out_specs=tuple(spec for _, _, spec in outs.values()),
             scratch_shapes=[pltpu.VMEM(shape, dtype) for shape, dtype in scratch.values()]
             + [pltpu.SemaphoreType.DMA((3,))],
-            compiler_params=pltpu.CompilerParams(vmem_limit_bytes=60 * 2**20),
+            compiler_params=pltpu.CompilerParams(vmem_limit_bytes=16 * 2**20),
         )(*[value for value, _ in ins.values()])
         return (
             result,

time: 87.5 us -> 80.5 us (0.920)
  Pallas kernels: 85.2 us -> 79.5 us
  local copies, waits for them, and re-layouts: 1.26 us -> 0.01 us
    pallas_call x1, Pallas kernels: 79.8 us -> 76.3 us  [local(): pl.pallas_call(functools.partial(layer_kernel, S, T, fused, names), out_s...]
    pallas_call x1, Pallas kernels: 5.47 us -> 3.23 us  [local(): pl.pallas_call(functools.partial(finish_kernel, T, names), out_shape=tupl...]
    reshape x1 -> x0, local copies, waits for them, and re-layouts: 1.26 us -> none  [local(): skip.reshape(1, D)]
where the time goes in v4:
time: 80.5 us; the launch traced here: 80.4 us
  Pallas kernels  79.5 us (99%)
  between operations  0.85 us (1%)
    pallas_call x1, Pallas kernels, local(): pl.pallas_call(functools.partial(layer_kernel, S, T, fused, names), out_s...  76.3 us
    pallas_call x1, Pallas kernels, local(): pl.pallas_call(functools.partial(finish_kernel, T, names), out_shape=tupl...  3.23 us

profile of v4, /device:TPU:1, one launch (start us, length us, event | category | flops | bytes accessed | tf_op | source)
XLA Modules:
  0.0 80.4 jit_solution(10339153039259592882)
XLA Ops:
  0.6 0.0 copy-start.1
  0.7 0.0 copy-start
  0.7 76.3 %shard_map.186 = (bf16[1024,512]{1,0:T(8,128)(2,1)S(1)}, f32[1024,512]{1,0:T(8,128)S(1)}, f32[8,512]{1,0:T(8,128)S(1)}, bf16[4,2,16,512]{3,2,1,0:T(8,128)(2,1)S(...) custom-call(s32[6]{0:T(128)} %refs_0_.1, bf16[1024,512]{1,0:T(8,128)(2,1)} %refs_1_.1, ...), custom_call_target="tpu_custom_call" | custom-call | tf_op jit(solution)/shard_map/pallas_call | solution.py:1133
  77.0 0.0 copy-done.1
  77.0 0.0 copy-done
  77.0 3.2 %shard_map.187 = (bf16[1024,512]{1,0:T(8,128)(2,1)}, f32[1024,512]{1,0:T(8,128)}, f32[1,512]{1,0:T(1,128)}, f32[4,2,16,512]{3,2,1,0:T(8,128)}, f32[1,64]{1,0:T(1...) custom-call(bf16[1024,512]{1,0:T(8,128)(2,1)S(1)} %get-tuple-element, ...), custom_call_target="tpu_custom_call" | custom-call | tf_op jit(solution)/shard_map/pallas_call | solution.py:1180
Async XLA Ops:
  0.6 76.3 %copy-start.1 = (f32[64]{0:T(128)S(1)}, f32[64]{0:T(128)}, u32[]{:S(2)}) copy-start(f32[64]{0:T(128)} %param.15) | copy-start | bytes 772
  0.7 76.3 %copy-start = (f32[64]{0:T(128)S(1)}, f32[64]{0:T(128)}, u32[]{:S(2)}) copy-start(f32[64]{0:T(128)} %param.14) | copy-start | bytes 772

commit v5 on v4

--- a/solution.py
+++ b/solution.py
@@ -508,66 +508,81 @@
         return jnp.concatenate([tile[k : k + 1, :] for k in range(height)], 1)
 
     class Exchange:
-        def __init__(self, own, factor, tp_buf, seq_buf, forward):
+        def __init__(self, own, factor, buffer, forward):
             self.forward = forward
             self.shift = 0 if forward else 1
-            self.factor_tp = power(factor, R)
-            self.factor_seq = power(self.factor_tp, T)
-            self.tp_buf, self.seq_buf = (tp_buf, seq_buf)
-            tp_buf[t] = packed(jnp.concatenate(own, 1), 8)
-            self.copies = [
-                links.send(tp_buf.at[t], tp_buf.at[t], (s, peer)) for peer in peers_tp
-            ]
-
-        def order(self, count):
-            return list(range(count)) if self.forward else list(range(count))[::-1]
-
-        def before(self, other, mine):
-            return other < mine if self.forward else other > mine
-
-        def value(self, tile):
-            return unpack(unpacked(tile, 2 * N // 128))
-
-        def over_seq(self):
-            arrive(self.copies)
-            row = s * T * R + self.shift
-            self.items = [self.value(self.tp_buf[z]) for z in self.order(T)]
-            self.masks = [clear(row + z * R, row + (z + 1) * R) for z in self.order(T)]
-            block, _ = fold(zero1, self.factor_tp, self.items, self.masks, [None] * T)
-            self.seq_buf[s] = packed(jnp.concatenate(block, 1), 8)
-            self.copies = [
-                links.send(self.seq_buf.at[s], self.seq_buf.at[s], (peer, t)) for peer in peers_seq
+            self.factor = power(factor, R)
+            self.buffer = buffer
+            buffer[t, s] = packed(jnp.concatenate(own, 1), 2 * N // 128)
+            mine = buffer.at[t, s]
+            self.copies = [links.send(mine, mine, (s, peer)) for peer in peers_tp]
+            self.copies += [links.send(mine, mine, (peer, t)) for peer in peers_seq]
+            self.copies += [
+                links.send(mine, mine, (peer, peer_tp))
+                for peer_tp in peers_tp
+                for peer in peers_seq
             ]
 
         def carry(self):
             arrive(self.copies)
-            blocks = self.order(S)
-            span = T * R
-            carry, _ = fold(
-                zero1,
-                self.factor_seq,
-                [self.value(self.seq_buf[block]) for block in blocks],
-                [clear(block * span + self.shift, (block + 1) * span + self.shift) for block in blocks],
-                [self.before(block, s) for block in blocks],
+
+            def order(count):
+                return list(range(count)) if self.forward else list(range(count))[::-1]
+
+            def ahead(block, z):
+                mine, other = (s * T + t, block * T + z)
+                return other < mine if self.forward else other > mine
+
+            rows = [
+                jnp.concatenate(
+                    [unpacked(self.buffer[z, block], 2 * N // 128) for block in range(S)], 0
+                )
+                for z in range(T)
+            ]
+            block = lax.broadcasted_iota(jnp.int32, (S, N), 0)
+            carry = (jnp.zeros((S, N), F32), jnp.zeros((S, N), F32))
+            for z in order(T):
+                low = (block * T + z) * R + self.shift
+                mask = clear(low, low + R)
+                item = (rows[z][:, :N], rows[z][:, N:])
+                moved = complex_mul(*self.factor, *carry)
+                longer = (moved[0] * mask + item[0], moved[1] * mask + item[1])
+                mine = block == s
+                taken = jnp.logical_or(jnp.logical_not(mine), ahead(s, z))
+                carry = tuple(jnp.where(taken, new, old) for new, old in zip(longer, carry))
+            result = zero1
+            whole = power(self.factor, T)
+            for b in order(S):
+                low = b * T * R + self.shift
+                mask = clear(low, low + T * R)
+                moved = complex_mul(*whole, *result)
+                longer = (
+                    moved[0] * mask + carry[0][b : b + 1],
+                    moved[1] * mask + carry[1][b : b + 1],
+                )
+                earlier = b < s if self.forward else b > s
+                result = tuple(jnp.where(earlier, new, old) for new, old in zip(longer, result))
+            inside = tuple(
+                jnp.sum(jnp.where(block == s, part, 0.0), 0, keepdims=True) for part in carry
             )
-            carry, _ = fold(
-                carry,
-                self.factor_tp,
-                self.items,
-                self.masks,
-                [self.before(z, t) for z in self.order(T)],
-            )
-            return carry
+            for z in order(T):
+                low = (s * T + z) * R + self.shift
+                mask = clear(low, low + R)
+                moved = complex_mul(*self.factor, *result)
+                longer = (moved[0] * mask, moved[1] * mask)
+                result = tuple(
+                    jnp.where(ahead(s, z), new, old) for new, old in zip(longer, result)
+                )
+            return (result[0] + inside[0], result[1] + inside[1])
 
     finals = segment_rows(lax.fori_loop(0, L, forward_step, none))
     seg_masks = [clear(first + index * L, first + (index + 1) * L) for index in range(SEGMENTS)]
     factor_seg = power(conj, L)
     own, _ = fold(zero1, factor_seg, finals, seg_masks, [None] * SEGMENTS)
-    exchange = Exchange(own, conj, r.state_tp, r.state_seq, True)
+    exchange = Exchange(own, conj, r.state_all, True)
     if fused:
         gather_units[0].over_plane()
         gather_out.over_cores()
-    exchange.over_seq()
     if fused:
         gather_units[1].over_plane()
         gather_out.finish()
@@ -689,8 +704,7 @@
 
         if fused and i > 0:
             reduces[i - 1].over_plane()
-        if i < T - 1:
-            unit_grads(i)
+        unit_grads(i)
         if fused and i > 1:
             reduces[i - 2].turn_plane()
         if fused and i > 2:
@@ -717,11 +731,10 @@
     ][::-1]
     factor_seg = power(lam, L)
     own, _ = fold(zero1, factor_seg, finals, seg_masks, [None] * SEGMENTS)
-    exchange = Exchange(own, lam, r.adj_tp, r.adj_seq, False)
-    unit_grads(T - 1)
+    exchange = Exchange(own, lam, r.adj_all, False)
     if fused:
         reduces[T - 2].turn_plane()
-    exchange.over_seq()
+        reduces[T - 1].over_plane()
     grad_out = dot_tn(state_low[...], d_mixed[...]).astype(BF16)
 
     def divide(grad, full):
@@ -737,7 +750,6 @@
         r.grad_rates[...] = grad_out
         divide(r.grad_rates, r.out_full)
         out_reduce = Reduce(place, r.out_full, r.out_halves, r.out_eighths, r.out_summed)
-        reduces[T - 1].over_plane()
         out_reduce.over_cores()
         unit_sums(T - 3)
     else:
@@ -1039,10 +1051,8 @@
         d_unit=((R, 2 * units), BF16),
         seg_carry=((SEGMENTS, 2 * N), F32),
         sums=((16, D), F32),
-        state_tp=((T, 8, 128), F32),
-        state_seq=((S, 8, 128), F32),
-        adj_tp=((T, 8, 128), F32),
-        adj_seq=((S, 8, 128), F32),
+        state_all=((T, S, 2 * N // 128, 128), F32),
+        adj_all=((T, S, 2 * N // 128, 128), F32),
     )
     in_rows = in_proj.transpose(0, 2, 1)
     if fused:
@@ -1106,7 +1116,7 @@
             in_eighths=eighths(*rate_sizes),
             in_summed=own(*rate_sizes),
         )
-        links = 160
+        links = 200
     else:
         w_in = lax.all_gather(in_rows, "tp", axis=1, tiled=True).reshape(2 * N, D)
         w_out = lax.all_gather(out_proj, "tp", axis=1, tiled=True).reshape(2 * N, D)
@@ -1128,7 +1138,7 @@
             grad_glu=((T, D, 2 * units), BF16, vmem),
             grad_down=((T, units, D), BF16, vmem),
         )
-        links = 2 * (T - 1 + S - 1)
+        links = 2 * (T * S - 1)
     names = [*ins, *outs, *scratch, *dict(counts=0, local_sem=0, send_sem=0, recv_sem=0)]
     results = pl.pallas_call(
         functools.partial(layer_kernel, S, T, fused, names),

time: 80.5 us -> 77.5 us (0.963)
  Pallas kernels: 79.5 us -> 76.5 us
    pallas_call x1, Pallas kernels: 76.3 us -> 73.2 us  [local(): pl.pallas_call(functools.partial(layer_kernel, S, T, fused, names), out_s...]
where the time goes in v5:
time: 77.5 us; the launch traced here: 77.3 us
  Pallas kernels  76.5 us (99%)
  between operations  0.85 us (1%)
    pallas_call x1, Pallas kernels, local(): pl.pallas_call(functools.partial(layer_kernel, S, T, fused, names), out_s...  73.2 us
    pallas_call x1, Pallas kernels, local(): pl.pallas_call(functools.partial(finish_kernel, T, names), out_shape=tupl...  3.23 us

profile of v5, /device:TPU:1, one launch (start us, length us, event | category | flops | bytes accessed | tf_op | source)
XLA Modules:
  0.0 77.3 jit_solution(17068439987173909865)
XLA Ops:
  0.6 0.0 copy-start.1
  0.7 0.0 copy-start
  0.7 73.2 %shard_map.186 = (bf16[1024,512]{1,0:T(8,128)(2,1)S(1)}, f32[1024,512]{1,0:T(8,128)S(1)}, f32[8,512]{1,0:T(8,128)S(1)}, bf16[4,2,16,512]{3,2,1,0:T(8,128)(2,1)S(...) custom-call(s32[6]{0:T(128)} %refs_0_.1, bf16[1024,512]{1,0:T(8,128)(2,1)} %refs_1_.1, ...), custom_call_target="tpu_custom_call" | custom-call | tf_op jit(solution)/shard_map/pallas_call | solution.py:1143
  73.9 0.0 copy-done.1
  73.9 0.0 copy-done
  73.9 3.2 %shard_map.187 = (bf16[1024,512]{1,0:T(8,128)(2,1)}, f32[1024,512]{1,0:T(8,128)}, f32[1,512]{1,0:T(1,128)}, f32[4,2,16,512]{3,2,1,0:T(8,128)}, f32[1,64]{1,0:T(1...) custom-call(bf16[1024,512]{1,0:T(8,128)(2,1)S(1)} %get-tuple-element, ...), custom_call_target="tpu_custom_call" | custom-call | tf_op jit(solution)/shard_map/pallas_call | solution.py:1190
Async XLA Ops:
  0.6 73.3 %copy-start.1 = (f32[64]{0:T(128)S(1)}, f32[64]{0:T(128)}, u32[]{:S(2)}) copy-start(f32[64]{0:T(128)} %param.15) | copy-start | bytes 772
  0.7 73.3 %copy-start = (f32[64]{0:T(128)S(1)}, f32[64]{0:T(128)}, u32[]{:S(2)}) copy-start(f32[64]{0:T(128)} %param.14) | copy-start | bytes 772

commit v6 on v5

--- a/solution.py
+++ b/solution.py
@@ -48,30 +48,46 @@
     def __init__(self, send_sem, recv_sem):
         self.send_sem = send_sem
         self.recv_sem = recv_sem
-        self.started = []
-
-    def send(self, source, target, device):
-        index = len(self.started)
-        copy = pltpu.make_async_remote_copy(
+        self.groups = []
+
+    def group(self, whole):
+        group = Group(self, len(self.groups), whole)
+        self.groups.append(group)
+        return group
+
+    def send(self, whole, copies):
+        group = self.group(whole)
+        for source, target, device in copies:
+            group.add(source, target, device)
+        return group
+
+    def close(self):
+        for group in self.groups:
+            group.last.wait_send()
+
+
+class Group:
+    def __init__(self, links, index, whole):
+        self.links = links
+        self.index = index
+        self.whole = whole
+
+    def copy(self, source, target, device):
+        return pltpu.make_async_remote_copy(
             src_ref=source,
             dst_ref=target,
-            send_sem=self.send_sem.at[index],
-            recv_sem=self.recv_sem.at[index],
+            send_sem=self.links.send_sem.at[self.index],
+            recv_sem=self.links.recv_sem.at[self.index],
             device_id=device,
             device_id_type=MESH,
         )
-        copy.start()
-        self.started.append(copy)
-        return copy
-
-    def close(self):
-        for copy in self.started:
-            copy.wait_send()
-
-
-def arrive(copies):
-    for copy in copies:
-        copy.wait_recv()
+
+    def add(self, source, target, device):
+        self.copy(source, target, device).start()
+        self.last = self.copy(self.whole, self.whole, device)
+
+    def arrive(self):
+        self.last.wait_recv()
 
 
 class Gather:
@@ -83,29 +99,35 @@
 
     def over_tp(self):
         p = self.place
-        self.copies = [
-            p.links.send(
-                self.buffer.at[0, p.chip, p.core],
-                self.buffer.at[slot, p.chip, p.core],
-                (p.s, lax.rem(p.t + p.T - slot, p.T)),
-            )
-            for slot in self.slots
-        ]
+        self.copies = p.links.send(
+            self.part.at[:, p.chip, p.core],
+            [
+                (
+                    self.buffer.at[0, p.chip, p.core],
+                    self.buffer.at[slot, p.chip, p.core],
+                    (p.s, lax.rem(p.t + p.T - slot, p.T)),
+                )
+                for slot in self.slots
+            ],
+        )
 
     def over_plane(self):
         p = self.place
-        arrive(self.copies)
+        self.copies.arrive()
         mine = self.part.at[:, p.chip, p.core]
-        self.copies = [p.links.send(mine, mine, device) for _, device in p.chips]
+        self.copies = p.links.send(
+            self.part.at[:, pl.ds(0, len(p.chips)), p.core],
+            [(mine, mine, device) for _, device in p.chips],
+        )
 
     def over_cores(self):
         p = self.place
-        arrive(self.copies)
+        self.copies.arrive()
         mine = self.part.at[:, :, p.core]
-        self.copies = [p.links.send(mine, mine, p.sibling)]
+        self.copies = p.links.send(mine, [(mine, mine, p.sibling)])
 
     def finish(self):
-        arrive(self.copies)
+        self.copies.arrive()
 
 
 class Reduce:
@@ -118,13 +140,13 @@
 
     def over_cores(self):
         p = self.place
-        self.copies = [
-            p.links.send(self.full.at[:, :, 1 - p.core], self.halves, p.sibling)
-        ]
+        self.copies = p.links.send(
+            self.halves, [(self.full.at[:, :, 1 - p.core], self.halves, p.sibling)]
+        )
 
     def over_plane(self):
         p = self.place
-        arrive(self.copies)
+        self.copies.arrive()
         parts, chips = self.halves.shape[:2]
 
         @pl.loop(0, parts * chips)
@@ -134,14 +156,17 @@
                 self.full[part, chip, p.core].astype(F32) + self.halves[part, chip].astype(F32)
             ).astype(BF16)
 
-        self.copies = [
-            p.links.send(self.halves.at[:, chip], self.eighths.at[k], device)
-            for k, (chip, device) in enumerate(p.chips)
-        ]
+        self.copies = p.links.send(
+            self.eighths,
+            [
+                (self.halves.at[:, chip], self.eighths.at[k], device)
+                for k, (chip, device) in enumerate(p.chips)
+            ],
+        )
 
     def sum_plane(self):
         p = self.place
-        arrive(self.copies)
+        self.copies.arrive()
 
         @pl.loop(0, self.halves.shape[0])
         def _(part):
@@ -165,24 +190,27 @@
 
     def over_plane(self):
         p = self.place
-        arrive(self.copies)
+        self.copies.arrive()
         self.sum_cores(p.by_x)
         self.sum_cores(p.by_y)
         self.sum_cores(p.by_xy)
-        self.copies = [
-            p.links.send(part.at[0, chip], self.eighths.at[index, 0, rows], device)
-            for index, part, chip, rows, device in (
-                (0, self.ours, p.by_x, pl.ds(0, self.rows), p.x_device),
-                (1, self.ours, p.by_xy, pl.ds(0, self.rows), p.x_device),
-                (0, self.theirs, p.by_y, pl.ds(self.rows, self.rows), p.y_device),
-                (1, self.theirs, p.by_xy, pl.ds(self.rows, self.rows), p.y_device),
-            )
-        ]
+        self.copies = p.links.send(
+            self.eighths.at[pl.ds(0, 2)],
+            [
+                (part.at[0, chip], self.eighths.at[index, 0, rows], device)
+                for index, part, chip, rows, device in (
+                    (0, self.ours, p.by_x, pl.ds(0, self.rows), p.x_device),
+                    (1, self.ours, p.by_xy, pl.ds(0, self.rows), p.x_device),
+                    (0, self.theirs, p.by_y, pl.ds(self.rows, self.rows), p.y_device),
+                    (1, self.theirs, p.by_xy, pl.ds(self.rows, self.rows), p.y_device),
+                )
+            ],
+        )
         self.sum_cores(p.chip)
 
     def turn_plane(self):
         p = self.place
-        arrive(self.copies)
+        self.copies.arrive()
         n = self.rows
         for index, chip in ((0, p.chip), (1, p.by_y)):
             self.halves[0, chip, 0:n] = (
@@ -192,14 +220,17 @@
             self.halves[0, chip, n:] = (
                 self.halves[0, chip, n:].astype(F32) + self.eighths[index, 0, n:].astype(F32)
             ).astype(BF16)
-        self.copies = [
-            p.links.send(self.ours.at[0, p.by_y], self.eighths.at[2, 0, pl.ds(0, n)], p.y_device),
-            p.links.send(self.theirs.at[0, p.by_x], self.eighths.at[2, 0, pl.ds(n, n)], p.x_device),
-        ]
+        self.copies = p.links.send(
+            self.eighths.at[2],
+            [
+                (self.ours.at[0, p.by_y], self.eighths.at[2, 0, pl.ds(0, n)], p.y_device),
+                (self.theirs.at[0, p.by_x], self.eighths.at[2, 0, pl.ds(n, n)], p.x_device),
+            ],
+        )
 
     def sum_plane(self):
         p = self.place
-        arrive(self.copies)
+        self.copies.arrive()
         self.summed[0] = (
             self.halves[0, p.chip].astype(F32) + self.eighths[2, 0].astype(F32)
         ).astype(BF16)
@@ -213,16 +244,19 @@
     def over_plane(self):
         p = self.place
         mine = self.buffer.at[:, p.chip, p.core]
-        self.copies = [p.links.send(mine, mine, device) for _, device in p.chips]
+        self.copies = p.links.send(
+            self.buffer.at[:, pl.ds(0, len(p.chips)), p.core],
+            [(mine, mine, device) for _, device in p.chips],
+        )
 
     def over_cores(self):
         p = self.place
-        arrive(self.copies)
+        self.copies.arrive()
         mine = self.buffer.at[:, :, p.core]
-        self.copies = [p.links.send(mine, mine, p.sibling)]
+        self.copies = p.links.send(mine, [(mine, mine, p.sibling)])
 
     def finish(self):
-        arrive(self.copies)
+        self.copies.arrive()
 
 
 class Place:
@@ -335,9 +369,10 @@
             rates_all[t, index : index + 1, 0:n] = row
         pl.semaphore_wait(barrier, T - 1 + S - 1)
         gather_in.over_tp()
-        rate_copies = [
-            links.send(rates_all.at[t], rates_all.at[t], (s, peer)) for peer in peers_tp
-        ]
+        rate_copies = links.send(
+            rates_all.at[pl.ds(0, T - 1)],
+            [(rates_all.at[t], rates_all.at[t], (s, peer)) for peer in peers_tp],
+        )
 
     for copy in fetched[2:]:
         copy.wait()
@@ -420,7 +455,7 @@
     if fused:
         gather_in.over_cores()
         gather_units[1].over_tp()
-        arrive(rate_copies)
+        rate_copies.arrive()
         half = lax.broadcasted_iota(jnp.int32, (8, 128), 1) < n
         rate_rows = [rates_all[z] for z in range(T)]
         joined = jnp.concatenate(
@@ -515,16 +550,21 @@
             self.buffer = buffer
             buffer[t, s] = packed(jnp.concatenate(own, 1), 2 * N // 128)
             mine = buffer.at[t, s]
-            self.copies = [links.send(mine, mine, (s, peer)) for peer in peers_tp]
-            self.copies += [links.send(mine, mine, (peer, t)) for peer in peers_seq]
-            self.copies += [
-                links.send(mine, mine, (peer, peer_tp))
+            self.copies = [
+                links.send(
+                    buffer.at[0], [(mine, mine, (peer, peer_tp)) for peer in [s, *peers_seq]]
+                )
                 for peer_tp in peers_tp
-                for peer in peers_seq
             ]
+            self.copies.append(
+                links.send(
+                    buffer.at[0, pl.ds(0, S - 1)], [(mine, mine, (peer, t)) for peer in peers_seq]
+                )
+            )
 
         def carry(self):
-            arrive(self.copies)
+            for copies in self.copies:
+                copies.arrive()
 
             def order(count):
                 return list(range(count)) if self.forward else list(range(count))[::-1]
@@ -635,7 +675,7 @@
 
     UNIT_ROWS = min(512, R)
     units = hidden.shape[1]
-    unit_copies = []
+    unit_copies = links.group(r.unit_sums) if fused else None
 
     def unit_grads(i):
         c = lax.rem(t + i, T)
@@ -653,9 +693,7 @@
     def unit_sums(i):
         reduces[i].sum_plane()
         if i > 0:
-            unit_copies.append(
-                links.send(r.unit_summed.at[i], r.unit_sums.at[i - 1], (s, lax.rem(t + i, T)))
-            )
+            unit_copies.add(r.unit_summed.at[i], r.unit_sums.at[i - 1], (s, lax.rem(t + i, T)))
 
     for i in range(T):
         c = lax.rem(t + i, T)
@@ -808,10 +846,13 @@
         reduces[T - 1].turn_plane()
         unit_sums(T - 2)
         out_reduce.sum_plane()
-        out_copies = [
-            links.send(r.out_summed.at[i], r.out_sums.at[i - 1], (s, lax.rem(t + i, T)))
-            for i in range(1, T)
-        ]
+        out_copies = links.send(
+            r.out_sums,
+            [
+                (r.out_summed.at[i], r.out_sums.at[i - 1], (s, lax.rem(t + i, T)))
+                for i in range(1, T)
+            ],
+        )
         in_reduce.over_plane()
         unit_sums(T - 1)
     else:
@@ -855,7 +896,10 @@
 
     small_tp, small_seq = (r.small_tp, r.small_seq)
     small_tp[t] = jnp.concatenate([packed(row, D // 128) for row in small_rows], 0)
-    small_copies = [links.send(small_tp.at[t], small_tp.at[t], (s, peer)) for peer in peers_tp]
+    small_copies = links.send(
+        small_tp.at[pl.ds(0, T - 1)],
+        [(small_tp.at[t], small_tp.at[t], (s, peer)) for peer in peers_tp],
+    )
 
     def total_of(own, buffer):
         total = own.astype(F32)
@@ -864,30 +908,33 @@
         return total.astype(BF16)
 
     unit_sum, out_sum, in_sum = (r.unit_sum, r.out_sum, r.in_sum)
-    arrive(unit_copies)
+    unit_copies.arrive()
     unit_sum[0, place.chip, place.core] = total_of(r.unit_summed[0, 0], r.unit_sums.at[:, 0])
     unit_spread = Spread(place, unit_sum)
     unit_spread.over_plane()
 
     in_reduce.sum_plane()
-    in_copies = [
-        links.send(r.in_summed.at[i], r.in_sums.at[i - 1], (s, lax.rem(t + i, T)))
-        for i in range(1, T)
-    ]
-    arrive(out_copies)
+    in_copies = links.send(
+        r.in_sums,
+        [(r.in_summed.at[i], r.in_sums.at[i - 1], (s, lax.rem(t + i, T))) for i in range(1, T)],
+    )
+    out_copies.arrive()
     out_sum[0, place.chip, place.core] = total_of(r.out_summed[0], r.out_sums)
     out_spread = Spread(place, out_sum)
     out_spread.over_plane()
 
-    arrive(small_copies)
+    small_copies.arrive()
     part = small_tp[0]
     for z in range(1, T):
         part = part + small_tp[z]
     small_seq[s] = part
-    small_copies = [links.send(small_seq.at[s], small_seq.at[s], (peer, t)) for peer in peers_seq]
+    small_copies = links.send(
+        small_seq.at[pl.ds(0, S - 1)],
+        [(small_seq.at[s], small_seq.at[s], (peer, t)) for peer in peers_seq],
+    )
 
     unit_spread.over_cores()
-    arrive(in_copies)
+    in_copies.arrive()
     in_sum[0, place.chip, place.core] = total_of(r.in_summed[0], r.in_sums)
     in_spread = Spread(place, in_sum)
     in_spread.over_plane()
@@ -897,7 +944,7 @@
     unit_copy = pltpu.make_async_copy(unit_sum.at[0], r.grad_units, r.local_sem.at[2])
     unit_copy.start()
 
-    arrive(small_copies)
+    small_copies.arrive()
     part = small_seq[0]
     for block in range(1, S):
         part = part + small_seq[block]
@@ -1116,7 +1163,7 @@
             in_eighths=eighths(*rate_sizes),
             in_summed=own(*rate_sizes),
         )
-        links = 200
+        links = 19 + 8 * T
     else:
         w_in = lax.all_gather(in_rows, "tp", axis=1, tiled=True).reshape(2 * N, D)
         w_out = lax.all_gather(out_proj, "tp", axis=1, tiled=True).reshape(2 * N, D)
@@ -1138,7 +1185,7 @@
             grad_glu=((T, D, 2 * units), BF16, vmem),
             grad_down=((T, units, D), BF16, vmem),
         )
-        links = 2 * (T * S - 1)
+        links = 2 * T
     names = [*ins, *outs, *scratch, *dict(counts=0, local_sem=0, send_sem=0, recv_sem=0)]
     results = pl.pallas_call(
         functools.partial(layer_kernel, S, T, fused, names),

time: 77.5 us -> 74.8 us (0.965)
  Pallas kernels: 76.5 us -> 73.8 us
    pallas_call x1, Pallas kernels: 73.2 us -> 70.6 us  [local(): pl.pallas_call(functools.partial(layer_kernel, S, T, fused, names), out_s...]
where the time goes in v6:
time: 74.8 us; the launch traced here: 74.7 us
  Pallas kernels  73.8 us (99%)
  between operations  0.85 us (1%)
    pallas_call x1, Pallas kernels, local(): pl.pallas_call(functools.partial(layer_kernel, S, T, fused, names), out_s...  70.6 us
    pallas_call x1, Pallas kernels, local(): pl.pallas_call(functools.partial(finish_kernel, T, names), out_shape=tupl...  3.23 us

profile of v6, /device:TPU:1, one launch (start us, length us, event | category | flops | bytes accessed | tf_op | source)
XLA Modules:
  0.0 74.7 jit_solution(12169666960887001633)
XLA Ops:
  0.6 0.0 copy-start.1
  0.7 0.0 copy-start
  0.7 70.6 %shard_map.186 = (bf16[1024,512]{1,0:T(8,128)(2,1)S(1)}, f32[1024,512]{1,0:T(8,128)S(1)}, f32[8,512]{1,0:T(8,128)S(1)}, bf16[4,2,16,512]{3,2,1,0:T(8,128)(2,1)S(...) custom-call(s32[6]{0:T(128)} %refs_0_.1, bf16[1024,512]{1,0:T(8,128)(2,1)} %refs_1_.1, ...), custom_call_target="tpu_custom_call" | custom-call | tf_op jit(solution)/shard_map/pallas_call | solution.py:1190
  71.3 0.0 copy-done.1
  71.3 0.0 copy-done
  71.3 3.2 %shard_map.187 = (bf16[1024,512]{1,0:T(8,128)(2,1)}, f32[1024,512]{1,0:T(8,128)}, f32[1,512]{1,0:T(1,128)}, f32[4,2,16,512]{3,2,1,0:T(8,128)}, f32[1,64]{1,0:T(1...) custom-call(bf16[1024,512]{1,0:T(8,128)(2,1)S(1)} %get-tuple-element, ...), custom_call_target="tpu_custom_call" | custom-call | tf_op jit(solution)/shard_map/pallas_call | solution.py:1237
Async XLA Ops:
  0.6 70.6 %copy-start.1 = (f32[64]{0:T(128)S(1)}, f32[64]{0:T(128)}, u32[]{:S(2)}) copy-start(f32[64]{0:T(128)} %param.15) | copy-start | bytes 772
  0.7 70.6 %copy-start = (f32[64]{0:T(128)S(1)}, f32[64]{0:T(128)}, u32[]{:S(2)}) copy-start(f32[64]{0:T(128)} %param.14) | copy-start | bytes 772

commit v7 on v6

--- a/solution.py
+++ b/solution.py
@@ -659,7 +659,8 @@
         half = 0.5 * (1.0 + th)
         a = (x * half).astype(BF16)
         act[rows, :] = a
-        d_gelu[rows, :] = half + 0.5 * x * (1.0 - th * th) * scale * (1.0 + 0.134145 * x * x)
+        d_act[rows, :] = x
+        summed[rows, :] = half
 
     if fused:
         reduces = [
@@ -711,6 +712,11 @@
         for tile in range(R // UNIT_ROWS):
             rows = slice(tile * UNIT_ROWS, (tile + 1) * UNIT_ROWS)
             both = dot(act[rows, :], w_gated)
+            if i == 0:
+                x = d_act[rows, :]
+                half = summed[rows, :]
+                slope = 1.5957691216057308 * (1.0 + 0.134145 * x * x)
+                d_gelu[rows, :] = half + x * half * (1.0 - half) * slope
             value, gate = (both[:, :units], both[:, units:])
             sigma = 0.5 * jnp.tanh(0.5 * gate) + 0.5
             gated = value * sigma
@@ -793,6 +799,9 @@
     else:
         r.grad_out[...] = grad_out
     carry = exchange.carry()
+    if fused:
+        reduces[T - 1].turn_plane()
+        out_reduce.over_plane()
     _, entering = fold(carry, factor_seg, finals, seg_masks, [None] * SEGMENTS)
     entering = entering[::-1]
     groups = tuple(
@@ -834,8 +843,6 @@
     _, added = adjoint_step(0, values, lambda group, step: inside[group])
     totals = [jnp.sum(total + add, 0, keepdims=True) for total, add in zip(totals, added)]
 
-    if fused:
-        out_reduce.over_plane()
     d_proj[...] = (adjoint[...] * gamma_signed).astype(BF16)
     grad_in = dot_tn(d_proj[...], normed[...]).astype(BF16)
     if fused:
@@ -843,7 +850,6 @@
         divide(r.grad_rates, r.in_full)
         in_reduce = Reduce(place, r.in_full, r.in_halves, r.in_eighths, r.in_summed)
         in_reduce.over_cores()
-        reduces[T - 1].turn_plane()
         unit_sums(T - 2)
         out_reduce.sum_plane()
         out_copies = links.send(
@@ -967,23 +973,13 @@
 
 def finish_kernel(T, names, *refs):
     r = types.SimpleNamespace(**dict(zip(names, refs)))
-    half = r.grad_rows.shape[0] // 2
-    arrays = [(r.result_in, r.result_rows, r.result)] + [
-        tuple(ref.at[pl.ds(at, half)] for ref in (r.grad_tokens_in, r.grad_rows, r.grad_tokens))
-        for at in (0, half)
+    copies = [
+        pltpu.make_async_copy(source, target, r.local_sem.at[index])
+        for index, (source, target) in enumerate(
+            ((r.result_in, r.result), (r.grad_tokens_in, r.grad_tokens))
+        )
     ]
-    fetched = [
-        pltpu.make_async_copy(source, kept, r.local_sem.at[index])
-        for index, (source, kept, _) in enumerate(arrays)
-    ]
-    copies = [
-        pltpu.make_async_copy(kept, target, r.local_sem.at[index])
-        for index, (_, kept, target) in enumerate(arrays)
-    ]
-    for copy in fetched:
-        copy.start()
-    for fetch, copy in zip(fetched, copies):
-        fetch.wait()
+    for copy in copies:
         copy.start()
     D_rows, lanes = (r.glu.shape[3], r.glu.shape[4])
     r.glu[0] = r.units_in[:, :, 0:D_rows, :lanes].astype(F32)
@@ -1211,8 +1207,8 @@
     if fused:
         result, grad_tokens, small, grad_in, grad_out, grad_units = results
         ins = dict(
-            result_in=(result, anywhere),
-            grad_tokens_in=(grad_tokens, anywhere),
+            result_in=(pltpu.with_memory_space_constraint(result, pltpu.VMEM), vmem),
+            grad_tokens_in=(pltpu.with_memory_space_constraint(grad_tokens, pltpu.VMEM), vmem),
             small=(small, vmem),
             in_in=(grad_in, vmem),
             out_in=(grad_out, vmem),
@@ -1232,8 +1228,7 @@
             glu=((2, C, 2, D // S, units), F32, vmem),
             down=((C, 2, units // S, D), F32, vmem),
         )
-        scratch = dict(result_rows=((R, D), BF16), grad_rows=((R, D), F32))
-        names = [*ins, *outs, *scratch, *dict(local_sem=0)]
+        names = [*ins, *outs, *dict(local_sem=0)]
         result, grad_tokens, gain, in_, decay, turn, out, skip_sum, glu, down = pl.pallas_call(
             functools.partial(finish_kernel, T, names),
             out_shape=tuple(
@@ -1241,8 +1236,7 @@
             ),
             in_specs=[spec for _, spec in ins.values()],
             out_specs=tuple(spec for _, _, spec in outs.values()),
-            scratch_shapes=[pltpu.VMEM(shape, dtype) for shape, dtype in scratch.values()]
-            + [pltpu.SemaphoreType.DMA((3,))],
+            scratch_shapes=[pltpu.SemaphoreType.DMA((2,))],
             compiler_params=pltpu.CompilerParams(vmem_limit_bytes=16 * 2**20),
         )(*[value for value, _ in ins.values()])
         return (

time: 74.8 us -> 72.8 us (0.973)
  Pallas kernels: 73.8 us -> 71.3 us
    pallas_call x1, Pallas kernels: 70.6 us -> 68.3 us  [local(): pl.pallas_call(functools.partial(layer_kernel, S, T, fused, names), out_s...]
where the time goes in v7:
time: 72.8 us; the launch traced here: 72.2 us
  Pallas kernels  71.3 us (98%)
  between operations  0.85 us (1%)
    pallas_call x1, Pallas kernels, local(): pl.pallas_call(functools.partial(layer_kernel, S, T, fused, names), out_s...  68.3 us
    pallas_call x1, Pallas kernels, local(): pl.pallas_call(functools.partial(finish_kernel, T, names), out_shape=tupl...  3.02 us

profile of v7, /device:TPU:1, one launch (start us, length us, event | category | flops | bytes accessed | tf_op | source)
XLA Modules:
  0.0 72.2 jit_solution(12185513591814094284)
XLA Ops:
  0.6 0.0 copy-start.1
  0.7 0.0 copy-start
  0.7 68.3 %shard_map.186 = (bf16[1024,512]{1,0:T(8,128)(2,1)S(1)}, f32[1024,512]{1,0:T(8,128)S(1)}, f32[8,512]{1,0:T(8,128)S(1)}, bf16[4,2,16,512]{3,2,1,0:T(8,128)(2,1)S(...) custom-call(s32[6]{0:T(128)} %refs_0_.1, bf16[1024,512]{1,0:T(8,128)(2,1)} %refs_1_.1, ...), custom_call_target="tpu_custom_call" | custom-call | tf_op jit(solution)/shard_map/pallas_call | solution.py:1186
  69.0 0.0 copy-done.1
  69.0 0.0 copy-done
  69.0 3.0 %shard_map.187 = (bf16[1024,512]{1,0:T(8,128)(2,1)}, f32[1024,512]{1,0:T(8,128)}, f32[1,512]{1,0:T(1,128)}, f32[4,2,16,512]{3,2,1,0:T(8,128)}, f32[1,64]{1,0:T(1...) custom-call(bf16[1024,512]{1,0:T(8,128)(2,1)S(1)} %get-tuple-element, ...), custom_call_target="tpu_custom_call" | custom-call | tf_op jit(solution)/shard_map/pallas_call | solution.py:1232
Async XLA Ops:
  0.6 68.3 %copy-start.1 = (f32[64]{0:T(128)S(1)}, f32[64]{0:T(128)}, u32[]{:S(2)}) copy-start(f32[64]{0:T(128)} %param.15) | copy-start | bytes 772
  0.7 68.3 %copy-start = (f32[64]{0:T(128)S(1)}, f32[64]{0:T(128)}, u32[]{:S(2)}) copy-start(f32[64]{0:T(128)} %param.14) | copy-start | bytes 772

commit v8 on v7

--- a/solution.py
+++ b/solution.py
@@ -802,6 +802,7 @@
     if fused:
         reduces[T - 1].turn_plane()
         out_reduce.over_plane()
+        unit_sums(T - 2)
     _, entering = fold(carry, factor_seg, finals, seg_masks, [None] * SEGMENTS)
     entering = entering[::-1]
     groups = tuple(
@@ -850,7 +851,6 @@
         divide(r.grad_rates, r.in_full)
         in_reduce = Reduce(place, r.in_full, r.in_halves, r.in_eighths, r.in_summed)
         in_reduce.over_cores()
-        unit_sums(T - 2)
         out_reduce.sum_plane()
         out_copies = links.send(
             r.out_sums,

time: 72.8 us -> 71.8 us (0.986)
  no operation moved by 1% of the time
where the time goes in v8:
time: 71.8 us; the launch traced here: 71.6 us
  Pallas kernels  70.8 us (99%)
  between operations  0.85 us (1%)
    pallas_call x1, Pallas kernels, local(): pl.pallas_call(functools.partial(layer_kernel, S, T, fused, names), out_s...  67.7 us
    pallas_call x1, Pallas kernels, local(): pl.pallas_call(functools.partial(finish_kernel, T, names), out_shape=tupl...  3.02 us

profile of v8, /device:TPU:1, one launch (start us, length us, event | category | flops | bytes accessed | tf_op | source)
XLA Modules:
  0.0 71.6 jit_solution(7337860375520253967)
XLA Ops:
  0.6 0.0 copy-start.1
  0.7 0.0 copy-start
  0.7 67.7 %shard_map.186 = (bf16[1024,512]{1,0:T(8,128)(2,1)S(1)}, f32[1024,512]{1,0:T(8,128)S(1)}, f32[8,512]{1,0:T(8,128)S(1)}, bf16[4,2,16,512]{3,2,1,0:T(8,128)(2,1)S(...) custom-call(s32[6]{0:T(128)} %refs_0_.1, bf16[1024,512]{1,0:T(8,128)(2,1)} %refs_1_.1, ...), custom_call_target="tpu_custom_call" | custom-call | tf_op jit(solution)/shard_map/pallas_call | solution.py:1186
  68.4 0.0 copy-done.1
  68.4 0.0 copy-done
  68.4 3.0 %shard_map.187 = (bf16[1024,512]{1,0:T(8,128)(2,1)}, f32[1024,512]{1,0:T(8,128)}, f32[1,512]{1,0:T(1,128)}, f32[4,2,16,512]{3,2,1,0:T(8,128)}, f32[1,64]{1,0:T(1...) custom-call(bf16[1024,512]{1,0:T(8,128)(2,1)S(1)} %get-tuple-element, ...), custom_call_target="tpu_custom_call" | custom-call | tf_op jit(solution)/shard_map/pallas_call | solution.py:1232
Async XLA Ops:
  0.6 67.8 %copy-start.1 = (f32[64]{0:T(128)S(1)}, f32[64]{0:T(128)}, u32[]{:S(2)}) copy-start(f32[64]{0:T(128)} %param.15) | copy-start | bytes 772
  0.7 67.8 %copy-start = (f32[64]{0:T(128)S(1)}, f32[64]{0:T(128)}, u32[]{:S(2)}) copy-start(f32[64]{0:T(128)} %param.14) | copy-start | bytes 772
